TPU v7x, 32 devices: a whole 2x2x4 slice. The times are simulated.
32 devices in a mesh: groups: 2 (over x), row: 8 (over z, y), col: 2 (over core).
Axes of the slice: x: 2, y: 2, z: 4, core: 2. Of those that a mesh axis runs over, the one named last changes fastest.
Arguments:
- d_blocks: float32 [16, 2, 6, 128, 128], P(('groups', 'row'), 'col'), parts along dimension 0
- d_index: int32 [16, 2, 6, 2], P(('groups', 'row'), 'col'), parts along dimension 0, may hold values from 0 to 31, as said below
- row_perm: int32 [64], P('groups'), parts along dimension 0, may hold values from 0 to 31, as said below
- ks_blocks: float32 [16, 4, 10, 128, 128], P(('groups', 'row'), 'col'), parts along dimension 0
- ks_index: int32 [16, 4, 10], P(('groups', 'row'), 'col'), parts along dimension 0, may hold values from 0 to 15, as said below
- c_index: int32 [16, 2, 16], P(('groups', 'row'), 'col'), parts along dimension 0, may hold values from 0 to 63, as said below
Outputs:
- c_blocks: float32 [16, 2, 16, 128, 128], P(('groups', 'row'), 'col'), parts along dimension 0
There are 2 independent parts, one for each index of `groups`. A program takes and returns all parts, laid end to end along the dimension named above; each array names one. Nothing has to cross between parts.
Inputs may be any that keep to these rules, and one draw needn't show every extreme that they name: `d_index`: no density block is listed twice within a column half; at most 2 blocks of one device, and at most 12 blocks of one column half, fall into one grid row panel (block rows whose row_perm values share one quotient by 4); both bounds are reached. `row_perm`: A permutation of the block rows. `ks_index`: positions within one window block are distinct. `c_index`: positions on one device are distinct.
All inputs are finite; a program needn't handle non-finite values.
Results may differ from a plain program's by a relative error of at most 0.0003.
Values sent between devices are 32-bit elements; how exact they have to be, the bound alone decides.
No kernel may reach another device: no remote copies, remote signals or barrier semaphores. Data moves between devices by JAX's collectives and lax.ppermute only.
A program may use at most 128 MiB of HBM per device.

v0:
```python
import math

import jax
import jax.numpy as jnp
from jax import lax
from jax.sharding import PartitionSpec as P

BR = 4
CAPX = 2


FILTER = 0.055


def passed_along(shard, axis, by):
    size = lax.axis_size(axis)
    return lax.ppermute(shard, axis, [(i, (i + by) % size) for i in range(size)])


def window_blocks(slots, places):
    onehot = (places[:, None] == jnp.arange(BR * BR)[None, :]).astype(jnp.float32)
    return jnp.einsum("qp,qxy->pxy", onehot, slots, precision=lax.Precision.HIGHEST)


def block_norms(blocks):
    return jnp.sqrt(jnp.sum(blocks * blocks, axis=(-2, -1)))


def stop_product(density_panel, panel_labels, panel_norms, ks_slots, ks_places, targets, half_cols):
    block_size = density_panel.shape[-1]
    limit = FILTER * block_size * math.sqrt(block_size)
    window = window_blocks(ks_slots, ks_places)
    window_norms = block_norms(window)
    target_rows = targets // half_cols
    target_cols = targets % half_cols
    slot_range = jnp.arange(density_panel.shape[0])
    inner_rows = jnp.arange(BR)
    matches = (panel_labels[None, None, :, 0] == inner_rows[None, :, None]) & (
        panel_labels[None, None, :, 1] == target_cols[:, None, None]
    )
    present_pair = jnp.any(matches, axis=2)
    where_slot = jnp.sum(matches.astype(jnp.int32) * slot_range[None, None, :], axis=2)
    chosen = density_panel[where_slot]
    chosen_norms = panel_norms[where_slot]
    picked = target_rows[:, None] * BR + inner_rows[None, :]
    ks_norms = window_norms[picked]
    retained = present_pair & (ks_norms * chosen_norms >= limit)
    masked = jnp.where(retained[..., None, None], window[picked], 0.0)
    return jnp.einsum("tkxy,tkyz->txz", masked, chosen, precision=lax.Precision.HIGHEST)


def on_device(d_blocks, d_index, row_perm, ks_blocks, ks_index, c_index):
    row_count = lax.axis_size("row")
    block_size = d_blocks.shape[-1]
    blocks = d_blocks.reshape(-1, block_size, block_size)
    slot_list = d_index.reshape(-1, 2)
    block_rows = row_perm.shape[0]
    half_cols = block_rows // lax.axis_size("col")
    capacity = 3 * row_count // 2
    position = jnp.sum(
        jnp.where(slot_list[:, 0:1] == jnp.arange(block_rows)[None, :], row_perm[None, :], 0),
        axis=1,
    )
    grid_panel = position // BR
    inner_row = position % BR
    onehot = (grid_panel[:, None] == jnp.arange(row_count)[None, :]).astype(jnp.int32)
    arrival_rank = jnp.sum((jnp.cumsum(onehot, axis=0) - onehot) * onehot, axis=1)
    send_slot = grid_panel * CAPX + arrival_rank
    outgoing = (
        jnp.zeros((row_count * CAPX, block_size, block_size), jnp.float32).at[send_slot].set(blocks)
    )
    outgoing = outgoing.reshape(row_count, CAPX, block_size, block_size)
    labels = (
        jnp.full((row_count * CAPX, 2), -1, jnp.int32)
        .at[send_slot]
        .set(jnp.stack([inner_row, slot_list[:, 1]], axis=1))
    )
    labels = labels.reshape(row_count, CAPX, 2)
    arrived, arrived_labels = (
        lax.all_to_all(outgoing, "row", split_axis=0, concat_axis=0, tiled=True),
        lax.all_to_all(labels, "row", split_axis=0, concat_axis=0, tiled=True),
    )
    arrived = arrived.reshape(-1, block_size, block_size)
    arrived_labels = arrived_labels.reshape(-1, 2)
    keep_order = jnp.argsort((arrived_labels[:, 0] < 0).astype(jnp.int32), stable=True)[:capacity]
    density_panel = arrived[keep_order]
    panel_labels = arrived_labels[keep_order]
    ks_all, ks_places = (
        lax.all_gather(ks_blocks, "col", axis=1, tiled=True),
        lax.all_gather(ks_index, "col", axis=1, tiled=True),
    )
    ks_all = ks_all[0]
    ks_places = ks_places[0]
    targets = c_index.reshape(-1)
    stop_count = ks_all.shape[0]
    panel_norms = block_norms(density_panel)
    accumulated = jnp.zeros((targets.shape[0], block_size, block_size), jnp.float32)
    for station in range(stop_count):
        accumulated = accumulated + stop_product(
            density_panel,
            panel_labels,
            panel_norms,
            ks_all[station],
            ks_places[station],
            targets,
            half_cols,
        )
        if station + 1 < stop_count:
            density_panel, panel_labels, panel_norms = passed_along(
                (density_panel, panel_labels, panel_norms), "row", -1
            )
    return accumulated.reshape(c_index.shape + (block_size, block_size))


def solution(mesh):
    return jax.shard_map(
        on_device,
        mesh=mesh,
        in_specs=(
            P(("groups", "row"), "col", None, None, None),
            P(("groups", "row"), "col", None, None),
            P("groups"),
            P(("groups", "row"), "col", None, None, None),
            P(("groups", "row"), "col", None),
            P(("groups", "row"), "col", None),
        ),
        out_specs=P(("groups", "row"), "col", None, None, None),
        check_vma=False,
    )
```

profile of v0, /device:TPU:0, one launch (start us, length us, event | category | flops | bytes accessed | tf_op | source)
XLA Modules:
  0.0 178.7 jit_solution(10190861303290267828)
XLA Ops:
  6.5 0.8 fusion.71
  7.3 0.8 select_reduce_fusion.1
  8.2 0.2 select_reduce_fusion
  8.6 0.6 scatter_custom_fusion
  9.2 0.7 copy.53
  9.9 7.3 %all-to-all-start = ((s32[8,2,2]{1,2,0:T(2,128)}), s32[8,2,2]{1,2,0:T(2,128)S(1)}, u32[]{:S(2)}, u32[]{:S(2)}) async-start(s32[8,2,2]{1,2,0:T(2,128)} %copy.53), calls=%async_computation | async-start | bytes 16384 | tf_op jit(solution)/shard_map/all_to_all | solution.py:81
  17.2 0.7 all-gather.2.cloned.1.call-update
  17.9 0.7 fusion.65
  18.8 2.0 %all_gather.6 = s32[1,4,10]{2,0,1:T(1,128)S(1)} all-gather(s32[1,2,10]{2,0,1:T(1,128)} %bitcast.165), channel_id=1, replica_groups=mesh['groups'=2,'row'=8,'col'=2] {'col'}, dimensions={1}, use_global_device_ids=true | all-gather | bytes 240 | tf_op jit(solution)/shard_map/all_gather | solution.py:90
  20.8 1.1 broadcast_in_dim.52
  21.8 2.6 %scatter_fusion = f32[16,128,128]{2,1,0:T(8,128)} fusion(f32[16,128,128]{2,1,0:T(8,128)} %broadcast_in_dim.52, s32[6]{0:T(128)S(1)} %get-tuple-element.32, f32[6,128,128]{2,1,0:T(8,128)} %bitcast.163), kind=kCustom, calls=%fused_computation.19 | custom fusion | bytes 1179672 | tf_op jit(solution)/shard_map/scatter | solution.py:70
  24.4 6.0 %all-to-all-start.1 = ((f32[8,2,128,128]{3,2,1,0:T(8,128)}), f32[8,2,128,128]{3,2,1,0:T(8,128)S(1)}, u32[]{:S(2)}, u32[]{:S(2)}) async-start(f32[8,2,128,128]{3,2,1,0:T(8,128)} %bitcast.14), calls=%async_computation.1 | async-start | bytes 2097152 | tf_op jit(solution)/shard_map/all_to_all | solution.py:80
  30.6 1.3 sort.17
  31.9 0.6 gather_fusion
  32.5 4.8 %collective-permute-start = (s32[12,2]{1,0:T(8,128)S(1)}, s32[12,2]{1,0:T(8,128)S(1)}, u32[]{:S(2)}, u32[]{:S(2)}) collective-permute-start(s32[12,2]{1,0:T(8,128)S(1)} %gather_fusion), channel_id=1, source_target_pairs={{0,14},{2,0},{4,2},{6,4},{8,6},{10,8},{12,10},{14,12},{1,15},{3,1}... | collective-permute-start | bytes 296 | tf_op jit(solution)/shard_map/ppermute | solution.py:17
  37.3 0.2 slice_reduce_fusion.7
  37.5 11.2 %collective-permute-done = s32[12,2]{1,0:T(8,128)S(1)} collective-permute-done((s32[12,2]{1,0:T(8,128)S(1)}, s32[12,2]{1,0:T(8,128)S(1)}, u32[]{:S(2)}, u32[]{:S(2)}) %collective-permute-start) | collective-permute-done | bytes 128 | tf_op jit(solution)/shard_map/ppermute | solution.py:17
  48.7 5.2 %collective-permute-start.3 = (s32[12,2]{1,0:T(8,128)S(1)}, s32[12,2]{1,0:T(8,128)S(1)}, u32[]{:S(2)}, u32[]{:S(2)}) collective-permute-start(s32[12,2]{1,0:T(8,128)S(1)} %collective-permute-done), channel_id=1, source_target_pairs={{0,14},{2,0},{4,2},{6,4},{8,6},{10,8},{12,10},{14,12},{1,15},{3,1}... | collective-permute-start | bytes 296 | tf_op jit(solution)/shard_map/ppermute | solution.py:17
  54.0 0.2 slice_reduce_fusion.5
  54.2 1.1 collective-permute-done.3
  55.3 5.0 %collective-permute-start.6 = (s32[12,2]{1,0:T(8,128)S(1)}, s32[12,2]{1,0:T(8,128)S(1)}, u32[]{:S(2)}, u32[]{:S(2)}) collective-permute-start(s32[12,2]{1,0:T(8,128)S(1)} %collective-permute-done.3), channel_id=1, source_target_pairs={{0,14},{2,0},{4,2},{6,4},{8,6},{10,8},{12,10},{14,12},{1,15},{3,1}... | collective-permute-start | bytes 296 | tf_op jit(solution)/shard_map/ppermute | solution.py:17
  60.3 0.2 slice_reduce_fusion.3
  60.6 1.1 collective-permute-done.6
  61.7 0.2 slice_reduce_fusion.1
  62.5 0.1 fusion.46
  63.2 0.6 gather_fusion.2
  63.9 0.2 multiply_reduce_fusion.4
  64.1 2.7 %gather_fusion.5 = f32[64,128,128]{2,1,0:T(8,128)} fusion(f32[12,128,128]{2,1,0:T(8,128)S(1)} %gather_fusion.2, s32[1024]{0:T(1024)S(1)} %pad_clamp_fusion.3), kind=kCustom, calls=%fused_computation.5 | custom fusion | bytes 8388864 | tf_op jit(solution)/shard_map/gather | solution.py:43
  66.8 0.8 gather_fusion.3
  67.6 5.0 %collective-permute-start.1 = (f32[12]{0:T(128)S(1)}, f32[12]{0:T(128)S(1)}, u32[]{:S(2)}, u32[]{:S(2)}) collective-permute-start(f32[12]{0:T(128)S(1)} %sqrt.16), channel_id=1, source_target_pairs={{0,14},{2,0},{4,2},{6,4},{8,6},{10,8},{12,10},{14,12},{1,15},{3,1}... | collective-permute-start | bytes 152 | tf_op jit(solution)/shard_map/ppermute | solution.py:17
  72.7 1.2 collective-permute-done.1
  73.9 5.0 %collective-permute-start.4 = (f32[12]{0:T(128)S(1)}, f32[12]{0:T(128)S(1)}, u32[]{:S(2)}, u32[]{:S(2)}) collective-permute-start(f32[12]{0:T(128)S(1)} %collective-permute-done.1), channel_id=1, source_target_pairs={{0,14},{2,0},{4,2},{6,4},{8,6},{10,8},{12,10},{14,12},{1,15},{3,1}... | collective-permute-start | bytes 152 | tf_op jit(solution)/shard_map/ppermute | solution.py:17
  78.9 0.8 gather_fusion.7
  79.7 9.0 %collective-permute-done.4 = f32[12]{0:T(128)S(1)} collective-permute-done((f32[12]{0:T(128)S(1)}, f32[12]{0:T(128)S(1)}, u32[]{:S(2)}, u32[]{:S(2)}) %collective-permute-start.4) | collective-permute-done | bytes 80 | tf_op jit(solution)/shard_map/ppermute | solution.py:17
  88.7 3.0 %collective-permute-start.7 = (f32[12]{0:T(128)S(1)}, f32[12]{0:T(128)S(1)}, u32[]{:S(2)}, u32[]{:S(2)}) collective-permute-start(f32[12]{0:T(128)S(1)} %collective-permute-done.4), channel_id=1, source_target_pairs={{0,14},{2,0},{4,2},{6,4},{8,6},{10,8},{12,10},{14,12},{1,15},{3,1}... | collective-permute-start | bytes 152 | tf_op jit(solution)/shard_map/ppermute | solution.py:17
  91.8 0.8 gather_fusion.11
  92.5 0.5 collective-permute-done.7
  93.0 0.8 gather_fusion.15
  93.8 2.7 %fusion.70 = (f32[1,1,10,128,128]{4,3,2,0,1:T(8,128)S(1)}, f32[1,1,10,128,128]{4,3,2,0,1:T(8,128)}, f32[1,1,10,128,128]{4,3,2,0,1:T(8,128)S(1)}, f32[1,1,10,128,128]{4,3,2,0,1:T(8,128)S(1)}) fusion(f32[1,4,10,128,128]{4,3,2,0,1:T(8,128)} %all-gather.2.cloned.1.call-done), kind=kLoop, calls=%fused_computation.152 | loop fusion | bytes 5242880 | tf_op jit(solution)/shard_map/slice | solution.py:103
  96.6 2.0 %multiply_reduce_fusion.3 = (f32[16]{0:T(128)S(1)}, f32[16,128,128]{2,0,1:T(8,128)}) fusion(f32[1,1,10,128,128]{4,3,2,0,1:T(8,128)S(1)} %get-tuple-element.18, s32[10]{0:T(128)S(1)} %get-tuple-element.22), kind=kOutput, calls=%fused_computation.55 | convolution fusion | flops 31981712 | bytes 1704040 | tf_op jit(solution)/shard_map/qp,qxy->pxy/dot_general | solution.py:22
  98.6 0.8 gather_fusion.1
  99.4 2.1 %multiply_reduce_fusion.2 = (f32[16]{0:T(128)S(1)}, f32[16,128,128]{2,0,1:T(8,128)}) fusion(f32[1,1,10,128,128]{4,3,2,0,1:T(8,128)S(1)} %get-tuple-element.17, s32[10]{0:T(128)S(1)} %get-tuple-element.21), kind=kOutput, calls=%fused_computation.54 | convolution fusion | flops 31981712 | bytes 1704040 | tf_op jit(solution)/shard_map/qp,qxy->pxy/dot_general | solution.py:22
  101.8 1.6 copy.63
  103.4 2.8 %gather_fusion.4 = f32[64,128,128]{2,1,0:T(8,128)} fusion(f32[16,128,128]{2,1,0:T(8,128)S(1)} %copy.63, s32[1024]{0:T(1024)S(1)} %pad_clamp_fusion.4), kind=kCustom, calls=%fused_computation.4 | custom fusion | bytes 8388864 | tf_op jit(solution)/shard_map/gather | solution.py:48
  106.2 0.8 gather_fusion.6
  107.3 1.6 copy.68
  108.9 2.8 %gather_fusion.8 = f32[64,128,128]{2,1,0:T(8,128)} fusion(f32[16,128,128]{2,1,0:T(8,128)S(1)} %copy.68, s32[1024]{0:T(1024)S(1)} %pad_clamp_fusion.4), kind=kCustom, calls=%fused_computation.8 | custom fusion | bytes 8388864 | tf_op jit(solution)/shard_map/gather | solution.py:48
  111.7 3.1 %multiply_reduce_fusion.1 = (f32[16]{0:T(128)S(1)}, f32[16,128,128]{2,0,1:T(8,128)}) fusion(f32[1,1,10,128,128]{4,3,2,0,1:T(8,128)} %get-tuple-element.16, s32[10]{0:T(128)S(1)} %get-tuple-element.20), kind=kOutput, calls=%fused_computation.53 | convolution fusion | flops 31981712 | bytes 1704040 | tf_op jit(solution)/shard_map/qp,qxy->pxy/dot_general | solution.py:22
  114.8 0.8 gather_fusion.10
  115.6 2.1 %multiply_reduce_fusion = (f32[16]{0:T(128)S(1)}, f32[16,128,128]{2,0,1:T(8,128)}) fusion(f32[1,1,10,128,128]{4,3,2,0,1:T(8,128)S(1)} %get-tuple-element.15, s32[10]{0:T(128)S(1)} %get-tuple-element.19), kind=kOutput, calls=%fused_computation.52 | convolution fusion | flops 31981712 | bytes 1704040 | tf_op jit(solution)/shard_map/qp,qxy->pxy/dot_general | solution.py:22
  117.7 5.2 %collective-permute-start.5 = (f32[12,128,128]{2,1,0:T(8,128)S(1)}, f32[12,128,128]{2,1,0:T(8,128)S(1)}, u32[]{:S(2)}, u32[]{:S(2)}) collective-permute-start(f32[12,128,128]{2,1,0:T(8,128)S(1)} %collective-permute-done.2), channel_id=1, source_target_pairs={{0,14},{2,0},{4,2},{6,4},{8,6},{10,8},{12,10},{14,12},{1,15},{3,1}... | collective-permute-start | bytes 2359304 | tf_op jit(solution)/shard_map/ppermute | solution.py:17
  123.2 1.6 copy.73
  124.8 2.7 %gather_fusion.12 = f32[64,128,128]{2,1,0:T(8,128)} fusion(f32[16,128,128]{2,1,0:T(8,128)S(1)} %copy.73, s32[1024]{0:T(1024)S(1)} %pad_clamp_fusion.4), kind=kCustom, calls=%fused_computation.12 | custom fusion | bytes 8388864 | tf_op jit(solution)/shard_map/gather | solution.py:48
  127.5 0.8 gather_fusion.14
  128.6 1.6 copy.78
  130.2 2.8 %gather_fusion.16 = f32[64,128,128]{2,1,0:T(8,128)} fusion(f32[16,128,128]{2,1,0:T(8,128)S(1)} %copy.78, s32[1024]{0:T(1024)S(1)} %pad_clamp_fusion.4), kind=kCustom, calls=%fused_computation.16 | custom fusion | bytes 8388864 | tf_op jit(solution)/shard_map/gather | solution.py:48
  133.0 2.8 %gather_fusion.9 = f32[64,128,128]{2,1,0:T(8,128)} fusion(f32[12,128,128]{2,1,0:T(8,128)S(1)} %collective-permute-done.2, s32[1024]{0:T(1024)S(1)} %pad_clamp_fusion.2), kind=kCustom, calls=%fused_computation.9 | custom fusion | bytes 8388864 | tf_op jit(solution)/shard_map/gather | solution.py:43
  135.8 8.2 %fusion.16 = f32[16,128,128]{2,1,0:T(8,128)S(1)} fusion(f32[16,4,128,128]{3,2,1,0:T(8,128)} %bitcast.153, f32[16,4,128,128]{3,2,1,0:T(8,128)} %bitcast.154, pred[16,4]{1,0:T(8,128)(4,1)S(1)} %copy.62), kind=kOutput, calls=%fused_computation.36 | convolution fusion | flops 1611661312 | bytes 9437248 | tf_op jit(solution)/shard_map/tkxy,tkyz->txz/dot_general | solution.py:49
  144.0 0.3 collective-permute-start.8
  144.3 5.4 %fusion.37 = f32[16,128,128]{2,1,0:T(8,128)} fusion(f32[16,128,128]{2,1,0:T(8,128)S(1)} %fusion.16, f32[16,4,128,128]{3,2,1,0:T(8,128)S(1)} %bitcast.158, f32[16,4,128,128]{3,2,1,0:T(8,128)S(1)} %bitcast.155, pred[16,4]{1,0:T(8,128)(4,1)S(1)} %copy.67), kind=kOutput, calls=%fused_computation.43 | convolution fusion | flops 1611923456 | bytes 10485824 | tf_op jit(solution)/shard_map/tkxy,tkyz->txz/dot_general | solution.py:49
  149.6 2.8 %gather_fusion.13 = f32[64,128,128]{2,1,0:T(8,128)} fusion(f32[12,128,128]{2,1,0:T(8,128)S(1)} %collective-permute-done.5, s32[1024]{0:T(1024)S(1)} %pad_clamp_fusion.1), kind=kCustom, calls=%fused_computation.13 | custom fusion | bytes 8388864 | tf_op jit(solution)/shard_map/gather | solution.py:43
  152.4 8.0 %fusion.34 = f32[16,128,128]{2,1,0:T(8,128)S(1)} fusion(f32[16,128,128]{2,1,0:T(8,128)} %fusion.37, f32[16,4,128,128]{3,2,1,0:T(8,128)} %bitcast.160, f32[16,4,128,128]{3,2,1,0:T(8,128)} %bitcast.156, pred[16,4]{1,0:T(8,128)(4,1)S(1)} %copy.72), kind=kOutput, calls=%fused_computation.42 | convolution fusion | flops 1611923456 | bytes 10485824 | tf_op jit(solution)/shard_map/tkxy,tkyz->txz/dot_general | solution.py:49
  160.4 2.7 %gather_fusion.17 = f32[64,128,128]{2,1,0:T(8,128)} fusion(f32[12,128,128]{2,1,0:T(8,128)S(1)} %collective-permute-done.8, s32[1024]{0:T(1024)S(1)} %pad_clamp_fusion), kind=kCustom, calls=%fused_computation.17 | custom fusion | bytes 8388864 | tf_op jit(solution)/shard_map/gather | solution.py:43
  163.2 8.7 %fusion.31 = f32[1,1,16,128,128]{4,3,2,1,0:T(8,128)} fusion(f32[16,128,128]{2,1,0:T(8,128)S(1)} %fusion.34, f32[16,4,128,128]{3,2,1,0:T(8,128)} %bitcast.159, f32[16,4,128,128]{3,2,1,0:T(8,128)} %bitcast.157, pred[16,4]{1,0:T(8,128)(4,1)S(1)} %copy.77), kind=kOutput, calls=%fused_computation.41 | convolution fusion | flops 1611923456 | bytes 10485824 | tf_op jit(solution)/shard_map/tkxy,tkyz->txz/dot_general | solution.py:49
  (79 shorter events, 3.4 us)
Async XLA Ops:
  9.9 14.6 %all-to-all-start = ((s32[8,2,2]{1,2,0:T(2,128)}), s32[8,2,2]{1,2,0:T(2,128)S(1)}, u32[]{:S(2)}, u32[]{:S(2)}) async-start(s32[8,2,2]{1,2,0:T(2,128)} %copy.53), calls=%async_computation | async-start | bytes 16384 | tf_op jit(solution)/shard_map/all_to_all | solution.py:81
  17.2 76.7 %all-gather.2.cloned.1.call-start = ((), (), s32[]{:S(2)}) async-start(), calls=%async_computation.2 | async-start | bytes 3932160 | tf_op jit(solution)/shard_map/all_gather | solution.py:89
  24.4 38.8 %all-to-all-start.1 = ((f32[8,2,128,128]{3,2,1,0:T(8,128)}), f32[8,2,128,128]{3,2,1,0:T(8,128)S(1)}, u32[]{:S(2)}, u32[]{:S(2)}) async-start(f32[8,2,128,128]{3,2,1,0:T(8,128)} %bitcast.14), calls=%async_computation.1 | async-start | bytes 2097152 | tf_op jit(solution)/shard_map/all_to_all | solution.py:80
  32.5 16.2 %collective-permute-start = (s32[12,2]{1,0:T(8,128)S(1)}, s32[12,2]{1,0:T(8,128)S(1)}, u32[]{:S(2)}, u32[]{:S(2)}) collective-permute-start(s32[12,2]{1,0:T(8,128)S(1)} %gather_fusion), channel_id=1, source_target_pairs={{0,14},{2,0},{4,2},{6,4},{8,6},{10,8},{12,10},{14,12},{1,15},{3,1}... | collective-permute-start | bytes 296 | tf_op jit(solution)/shard_map/ppermute | solution.py:17
  48.7 6.6 %collective-permute-start.3 = (s32[12,2]{1,0:T(8,128)S(1)}, s32[12,2]{1,0:T(8,128)S(1)}, u32[]{:S(2)}, u32[]{:S(2)}) collective-permute-start(s32[12,2]{1,0:T(8,128)S(1)} %collective-permute-done), channel_id=1, source_target_pairs={{0,14},{2,0},{4,2},{6,4},{8,6},{10,8},{12,10},{14,12},{1,15},{3,1}... | collective-permute-start | bytes 296 | tf_op jit(solution)/shard_map/ppermute | solution.py:17
  55.3 6.3 %collective-permute-start.6 = (s32[12,2]{1,0:T(8,128)S(1)}, s32[12,2]{1,0:T(8,128)S(1)}, u32[]{:S(2)}, u32[]{:S(2)}) collective-permute-start(s32[12,2]{1,0:T(8,128)S(1)} %collective-permute-done.3), channel_id=1, source_target_pairs={{0,14},{2,0},{4,2},{6,4},{8,6},{10,8},{12,10},{14,12},{1,15},{3,1}... | collective-permute-start | bytes 296 | tf_op jit(solution)/shard_map/ppermute | solution.py:17
  67.6 6.3 %collective-permute-start.1 = (f32[12]{0:T(128)S(1)}, f32[12]{0:T(128)S(1)}, u32[]{:S(2)}, u32[]{:S(2)}) collective-permute-start(f32[12]{0:T(128)S(1)} %sqrt.16), channel_id=1, source_target_pairs={{0,14},{2,0},{4,2},{6,4},{8,6},{10,8},{12,10},{14,12},{1,15},{3,1}... | collective-permute-start | bytes 152 | tf_op jit(solution)/shard_map/ppermute | solution.py:17
  72.6 45.1 %collective-permute-start.2 = (f32[12,128,128]{2,1,0:T(8,128)S(1)}, f32[12,128,128]{2,1,0:T(8,128)S(1)}, u32[]{:S(2)}, u32[]{:S(2)}) collective-permute-start(f32[12,128,128]{2,1,0:T(8,128)S(1)} %gather_fusion.2), channel_id=1, source_target_pairs={{0,14},{2,0},{4,2},{6,4},{8,6},{10,8},{12,10},{14,12},{1,15},{3,1}... | collective-permute-start | bytes 2359304 | tf_op jit(solution)/shard_map/ppermute | solution.py:17
  73.9 14.8 %collective-permute-start.4 = (f32[12]{0:T(128)S(1)}, f32[12]{0:T(128)S(1)}, u32[]{:S(2)}, u32[]{:S(2)}) collective-permute-start(f32[12]{0:T(128)S(1)} %collective-permute-done.1), channel_id=1, source_target_pairs={{0,14},{2,0},{4,2},{6,4},{8,6},{10,8},{12,10},{14,12},{1,15},{3,1}... | collective-permute-start | bytes 152 | tf_op jit(solution)/shard_map/ppermute | solution.py:17
  88.7 4.3 %collective-permute-start.7 = (f32[12]{0:T(128)S(1)}, f32[12]{0:T(128)S(1)}, u32[]{:S(2)}, u32[]{:S(2)}) collective-permute-start(f32[12]{0:T(128)S(1)} %collective-permute-done.4), channel_id=1, source_target_pairs={{0,14},{2,0},{4,2},{6,4},{8,6},{10,8},{12,10},{14,12},{1,15},{3,1}... | collective-permute-start | bytes 152 | tf_op jit(solution)/shard_map/ppermute | solution.py:17
  117.7 26.2 %collective-permute-start.5 = (f32[12,128,128]{2,1,0:T(8,128)S(1)}, f32[12,128,128]{2,1,0:T(8,128)S(1)}, u32[]{:S(2)}, u32[]{:S(2)}) collective-permute-start(f32[12,128,128]{2,1,0:T(8,128)S(1)} %collective-permute-done.2), channel_id=1, source_target_pairs={{0,14},{2,0},{4,2},{6,4},{8,6},{10,8},{12,10},{14,12},{1,15},{3,1}... | collective-permute-start | bytes 2359304 | tf_op jit(solution)/shard_map/ppermute | solution.py:17
  135.8 8.5 %copy-start = (f32[64,128,128]{2,1,0:T(8,128)S(1)}, f32[64,128,128]{2,1,0:T(8,128)}, u32[]{:S(2)}) copy-start(f32[64,128,128]{2,1,0:T(8,128)} %gather_fusion.8) | copy-start | bytes 12582916
  135.8 8.5 %copy-start.1 = (f32[64,128,128]{2,1,0:T(8,128)S(1)}, f32[64,128,128]{2,1,0:T(8,128)}, u32[]{:S(2)}) copy-start(f32[64,128,128]{2,1,0:T(8,128)} %gather_fusion.9) | copy-start | bytes 12582916
  144.0 16.4 %collective-permute-start.8 = (f32[12,128,128]{2,1,0:T(8,128)S(1)}, f32[12,128,128]{2,1,0:T(8,128)S(1)}, u32[]{:S(2)}, u32[]{:S(2)}) collective-permute-start(f32[12,128,128]{2,1,0:T(8,128)S(1)} %collective-permute-done.5), channel_id=1, source_target_pairs={{0,14},{2,0},{4,2},{6,4},{8,6},{10,8},{12,10},{14,12},{1,15},{3,1}... | collective-permute-start | bytes 2359304 | tf_op jit(solution)/shard_map/ppermute | solution.py:17
Sparse Core Ops, SparseCore 0:
  19.5 12.7 all-gather.1
where the time goes:
time: 179 us
  local copies, waits for them, and re-layouts  47.3 us (26%)
  starting transfers between devices  46.9 us (26%)
  matrix products  39.7 us (22%)
  waiting for transfers between devices  24.9 us (14%)
  between operations  13.7 us (8%)
  other arithmetic  4.28 us (2%)
  blocking collectives  2 us (1%)
    ppermute x9, starting transfers between devices, passed_along(): lax.ppermute(shard, axis, [(i, (i + by) % size) for i in range(size)])  33.6 us
    dot_general x4, matrix products, stop_product(): jnp.einsum('tkxy,tkyz->txz', masked, chosen, precision=lax.Precision.HIGH...  30.2 us
    ppermute x9, waiting for transfers between devices, passed_along(): lax.ppermute(shard, axis, [(i, (i + by) % size) for i in range(size)])  24.2 us
    gather x4, local copies, waits for them, and re-layouts, stop_product(): masked = jnp.where(retained[..., None, None], window[picked], 0.0)  11.1 us
    gather x4, local copies, waits for them, and re-layouts, stop_product(): chosen = density_panel[where_slot]  11 us
    dot_general x4, matrix products, window_blocks(): jnp.einsum('qp,qxy->pxy', onehot, slots, precision=lax.Precision.HIGHEST)  9.44 us
    all_to_all x1, starting transfers between devices, on_device(): lax.all_to_all(labels, 'row', split_axis=0, concat_axis=0, tiled=True)  7.28 us
    dot_general x4, local copies, waits for them, and re-layouts, window_blocks(): jnp.einsum('qp,qxy->pxy', onehot, slots, precision=lax.Precision.HIGHEST)  6.31 us
  transfers between devices with their start and end apart: 12, of which 6 were waited for; matrix products, arithmetic and copies ran while one was open for 43% of the time, Pallas kernels for 0%

commit v1 on v0

--- a/solution.py
+++ b/solution.py
@@ -1,8 +1,11 @@
+import functools
 import math
 
 import jax
 import jax.numpy as jnp
 from jax import lax
+from jax.experimental import pallas as pl
+from jax.experimental.pallas import tpu as pltpu
 from jax.sharding import PartitionSpec as P
 
 BR = 4
@@ -10,6 +13,8 @@
 
 
 FILTER = 0.055
+UNROLL = 4
+VMEM_GRANT = 8 * 1024 * 1024
 
 
 def passed_along(shard, axis, by):
@@ -49,7 +54,7 @@
     return jnp.einsum("tkxy,tkyz->txz", masked, chosen, precision=lax.Precision.HIGHEST)
 
 
-def on_device(d_blocks, d_index, row_perm, ks_blocks, ks_index, c_index):
+def panel_plan(d_blocks, d_index, row_perm, ks_blocks, ks_index, c_index):
     row_count = lax.axis_size("row")
     block_size = d_blocks.shape[-1]
     blocks = d_blocks.reshape(-1, block_size, block_size)
@@ -112,6 +117,257 @@
     return accumulated.reshape(c_index.shape + (block_size, block_size))
 
 
+def ring_order(count):
+    return list(range(0, count, 2)) + list(range(1, count, 2))[::-1]
+
+
+def split_bf16(x):
+    high = x.astype(jnp.bfloat16)
+    return high, (x - high.astype(jnp.float32)).astype(jnp.bfloat16)
+
+
+def norm_of(x):
+    columns = jnp.sum(x * x, axis=0, keepdims=True)
+    return jnp.sqrt(jnp.sum(columns, axis=1, keepdims=True))
+
+
+def in_vmem(x):
+    return pltpu.with_memory_space_constraint(x, pltpu.VMEM)
+
+
+SMEM_SPEC = pl.BlockSpec(memory_space=pltpu.SMEM)
+VMEM_SPEC = pl.BlockSpec(memory_space=pltpu.VMEM)
+
+
+def split_kernel(own_ref, twin_ref, parts_ref, norms_ref):
+    count = own_ref.shape[0]
+    for half, ref in enumerate((own_ref, twin_ref)):
+
+        def one(q, _, half=half, ref=ref):
+            block = ref[q]
+            parts_ref[half * count + q] = jnp.concatenate(split_bf16(block), axis=1)
+            norms_ref[half * count + q] = jnp.broadcast_to(norm_of(block), norms_ref.shape[1:])
+
+        lax.fori_loop(0, count, one, None, unroll=4)
+
+
+def split_ks(own, twin):
+    count, block_size, _ = own.shape
+    return pl.pallas_call(
+        split_kernel,
+        out_shape=(
+            pltpu.VMEM((2 * count, block_size, 2 * block_size), jnp.bfloat16),
+            pltpu.VMEM((2 * count, 1, block_size), jnp.float32),
+        ),
+        in_specs=[VMEM_SPEC] * 2,
+        out_specs=(VMEM_SPEC,) * 2,
+        compiler_params=pltpu.CompilerParams(vmem_limit_bytes=VMEM_GRANT),
+    )(in_vmem(own), in_vmem(twin))
+
+
+def product_kernel(config, *refs):
+    row_count, stop_count, half_cols, limit, pieces, first = config
+    perm_ref, own_place_ref, twin_place_ref, target_ref, parts_ref, norms_ref = refs[:6]
+    chunk_refs = refs[6 : 6 + len(pieces)]
+    rest = refs[6 + len(pieces) :]
+    if first:
+        c_ref = rest[0]
+        rest = rest[1:]
+    else:
+        c_in_ref, c_ref = rest[:2]
+        rest = rest[2:]
+    target_at, ks_at, label, list_t, list_q, list_b, held, sems = rest
+    block_size = c_ref.shape[-1]
+    half_stops, present = own_place_ref.shape
+    row, col = lax.axis_index("row"), lax.axis_index("col")
+
+    copies = []
+    for number, (blocks, _, labels) in enumerate(pieces):
+        if labels is None:
+            chunk_ref = chunk_refs[number]
+            rows = pl.ds(blocks * block_size, chunk_ref.shape[0] - blocks * block_size)
+            slot = len(copies)
+            copies.append(pltpu.make_async_copy(chunk_ref.at[rows], label.at[slot], sems.at[slot]))
+            copies[-1].start()
+
+    for i in range(target_at.shape[0]):
+        target_at[i] = -1
+    for i in range(ks_at.shape[0]):
+        ks_at[i] = -1
+    for t in range(target_ref.shape[0]):
+        target_at[target_ref[t]] = t
+    for local in range(half_stops):
+        own_base = (col * half_stops + local) * BR * BR
+        twin_base = ((1 - col) * half_stops + local) * BR * BR
+        for q in range(present):
+            ks_at[own_base + own_place_ref[local, q]] = local * present + q
+            ks_at[twin_base + twin_place_ref[local, q]] = (half_stops + local) * present + q
+    if first:
+        c_ref[...] = jnp.zeros_like(c_ref)
+    else:
+        c_ref[...] = c_in_ref[...]
+    for copy in copies:
+        copy.wait()
+
+    slots = {}
+    for number, (_, _, labels) in enumerate(pieces):
+        if labels is None:
+            slots[number] = len(slots)
+    found = (jnp.int32(0), jnp.int32(0))
+    for number, (blocks, offset, labels) in enumerate(pieces):
+        chunk_ref = chunk_refs[number]
+        slot = slots[number if labels is None else labels]
+
+        def look(b, found, chunk_ref=chunk_ref, slot=slot, offset=offset):
+            pairs, kept = found
+            position = perm_ref[label[slot, offset + b, 0].astype(jnp.int32)]
+            column = label[slot, offset + b, 1].astype(jnp.int32)
+            behind = lax.div(position, BR) - row
+            stop = jnp.where(behind < 0, behind + row_count, behind)
+            in_window = stop < stop_count
+            place = jnp.minimum(stop, stop_count - 1) * BR * BR + lax.rem(position, BR)
+            before = pairs
+            for i in range(BR):
+                target = target_at[i * half_cols + column]
+                ks = ks_at[place + i * BR]
+                list_t[pairs] = target
+                list_q[pairs] = ks
+                list_b[pairs] = kept
+                hit = (target >= 0) & (ks >= 0) & in_window
+                pairs = pairs + hit.astype(jnp.int32)
+            some = pairs > before
+
+            @pl.when(some)
+            def _():
+                held[kept] = chunk_ref[pl.ds(pl.multiple_of(b * block_size, block_size), block_size), :]
+
+            return pairs, kept + some.astype(jnp.int32)
+
+        found = lax.fori_loop(0, blocks, look, found)
+    pairs, _ = found
+    for u in range(UNROLL):
+        list_t[pairs + u] = 0
+        list_q[pairs + u] = 0
+        list_b[pairs + u] = 0
+
+    def multiply(step, _):
+        for u in range(UNROLL):
+            at = step * UNROLL + u
+            target, ks, slot = list_t[at], list_q[at], list_b[at]
+            density = held[slot]
+            bound = jnp.where(at < pairs, limit, jnp.inf)
+            keep = norms_ref[ks] * norm_of(density) >= bound
+            high, low = split_bf16(density)
+            weights = jnp.concatenate(
+                [
+                    jnp.concatenate([high, low], axis=1),
+                    jnp.concatenate([high, jnp.zeros_like(low)], axis=1),
+                ],
+                axis=0,
+            )
+            both = jnp.dot(parts_ref[ks], weights, preferred_element_type=jnp.float32)
+            value = both[:, :block_size] + both[:, block_size:]
+            c_ref[target] += jnp.where(keep, value, 0.0)
+
+    lax.fori_loop(0, lax.div(pairs + UNROLL - 1, UNROLL), multiply, None)
+
+
+def add_products(sizes, tables, parts, norms, accumulated, pieces, chunks, shape):
+    block_size = shape[-1]
+    limit = FILTER * block_size * math.sqrt(block_size)
+    first = accumulated is None
+    blocks = sum(piece[0] for piece in pieces)
+    labelled = [n for n, piece in enumerate(pieces) if piece[2] is None]
+    label_rows = chunks[labelled[0]].shape[0] - pieces[labelled[0]][0] * block_size
+    operands = [*tables, in_vmem(parts), in_vmem(norms), *map(in_vmem, chunks)]
+    in_specs = [SMEM_SPEC] * len(tables) + [VMEM_SPEC] * (2 + len(chunks))
+    if not first:
+        operands.append(in_vmem(accumulated))
+        in_specs.append(VMEM_SPEC)
+    longest = blocks * BR + 2 * UNROLL
+    return pl.pallas_call(
+        functools.partial(product_kernel, (*sizes, limit, pieces, first)),
+        out_shape=pltpu.VMEM(shape, jnp.float32) if first else jax.ShapeDtypeStruct(shape, jnp.float32),
+        in_specs=in_specs,
+        out_specs=VMEM_SPEC,
+        scratch_shapes=[
+            pltpu.SMEM((BR * sizes[2],), jnp.int32),
+            pltpu.SMEM((sizes[1] * BR * BR,), jnp.int32),
+            pltpu.SMEM((len(labelled), label_rows, block_size), jnp.float32),
+            pltpu.SMEM((longest,), jnp.int32),
+            pltpu.SMEM((longest,), jnp.int32),
+            pltpu.SMEM((longest,), jnp.int32),
+            pltpu.VMEM((blocks, block_size, block_size), jnp.float32),
+            pltpu.SemaphoreType.DMA((len(labelled),)),
+        ],
+        compiler_params=pltpu.CompilerParams(vmem_limit_bytes=VMEM_GRANT),
+    )(*operands)
+
+
+def ring_plan(d_blocks, d_index, row_perm, ks_blocks, ks_index, c_index):
+    row_count = lax.axis_size("row")
+    block_size = d_blocks.shape[-1]
+    half_cols = row_perm.shape[0] // lax.axis_size("col")
+    own = d_blocks.reshape(-1, block_size)
+    slots = d_blocks.shape[2]
+    lead = slots // 2
+    tail = slots - lead
+    label_rows = -(-slots // 8) * 8
+    labels = jnp.pad(
+        d_index[0, 0].astype(jnp.float32), ((0, label_rows - slots), (0, block_size - 2))
+    )
+    order = ring_order(row_count)
+    forward = [(order[i], order[(i + 1) % row_count]) for i in range(row_count)]
+    backward = [(b, a) for a, b in forward]
+    twins = [(0, 1), (1, 0)]
+
+    first_part = own[: lead * block_size]
+    second_part = jnp.concatenate([own[lead * block_size :], labels], axis=0)
+    pieces, chunks = [], []
+
+    def arrived(first, second):
+        pieces.append((lead, 0, len(pieces) + 1))
+        pieces.append((tail, lead, None))
+        chunks.extend([first, second])
+
+    arrived(first_part, second_part)
+    a_fwd = a_bwd = first_part
+    b_fwd = b_bwd = second_part
+    half = row_count // 2
+    ks_own = ks_blocks.reshape(-1, block_size, block_size)
+    for step in range(1, half):
+        a_fwd = lax.ppermute(a_fwd, "row", forward)
+        a_bwd = lax.ppermute(a_bwd, "row", backward)
+        b_fwd = lax.ppermute(b_fwd, "row", forward)
+        b_bwd = lax.ppermute(b_bwd, "row", backward)
+        arrived(a_fwd, b_fwd)
+        arrived(a_bwd, b_bwd)
+        if step == 1:
+            ks_twin = lax.ppermute(ks_own, "col", twins)
+            ks_places = ks_index.reshape(ks_index.shape[1:])
+            ks_places_twin = lax.ppermute(ks_places, "col", twins)
+            parts, norms = split_ks(ks_own, ks_twin)
+    a_fwd = lax.ppermute(a_fwd, "row", forward)
+    b_bwd = lax.ppermute(b_bwd, "row", backward)
+
+    tables = [row_perm, ks_places, ks_places_twin, c_index.reshape(-1)]
+    stop_count = 2 * ks_blocks.shape[1]
+    shape = (c_index.shape[-1], block_size, block_size)
+    sizes = (row_count, stop_count, half_cols)
+    partial = add_products(sizes, tables, parts, norms, None, pieces, chunks, shape)
+    last = [(lead, 0, 1), (tail, lead, None)]
+    total = add_products(sizes, tables, parts, norms, partial, last, [a_fwd, b_bwd], shape)
+    return total.reshape(c_index.shape + (block_size, block_size))
+
+
+def on_device(d_blocks, d_index, row_perm, ks_blocks, ks_index, c_index):
+    rows, slots = lax.axis_size("row"), d_blocks.shape[2]
+    gathered = rows * slots
+    routed = rows * CAPX + 3 * (3 * rows // 2)
+    plan = ring_plan if gathered <= routed else panel_plan
+    return plan(d_blocks, d_index, row_perm, ks_blocks, ks_index, c_index)
+
+
 def solution(mesh):
     return jax.shard_map(
         on_device,

time: 179 us -> 46.5 us (0.26)
  local copies, waits for them, and re-layouts: 47.3 us -> 2.47 us
  matrix products: 39.7 us -> 0 us
  starting transfers between devices: 46.9 us -> 17.9 us
  between operations: 13.7 us -> 0.08 us
  Pallas kernels: 0 us -> 8.8 us
  waiting for transfers between devices: 24.9 us -> 16.4 us
  other arithmetic: 4.28 us -> 0.7 us
  blocking collectives: 2 us -> 0 us
    dot_general x8 -> x0, matrix products: 39.7 us -> none  [the longest x4 30.2 us: stop_product(): jnp.einsum('tkxy,tkyz->txz', masked, chosen, precision=lax.Precision.HIGH...]
    gather x18 -> x0, local copies, waits for them, and re-layouts: 29.5 us -> none  [the longest x4 11.1 us: stop_product(): masked = jnp.where(retained[..., None, None], window[picked], 0.0)]
    ppermute x9 -> x16, starting transfers between devices: 33.6 us -> 17.9 us  [the longest x4 7.67 us: ring_plan(): b_bwd = lax.ppermute(b_bwd, 'row', backward)]
    all_to_all x2 -> x0, starting transfers between devices: 13.3 us -> none  [the longest x1 7.28 us: on_device(): lax.all_to_all(labels, 'row', split_axis=0, concat_axis=0, tiled=True)]
    pallas_call x0 -> x3, Pallas kernels: none -> 8.8 us  [the longest x2 7.64 us: add_products(): pl.pallas_call(functools.partial(product_kernel, (*sizes, limit, pieces,...]
    ppermute x9 -> x16, waiting for transfers between devices: 24.2 us -> 16.4 us  [the longest x3 7.94 us: ring_plan(): a_bwd = lax.ppermute(a_bwd, 'row', backward)]
    dot_general x4 -> x0, local copies, waits for them, and re-layouts: 6.31 us -> none  [window_blocks(): jnp.einsum('qp,qxy->pxy', onehot, slots, precision=lax.Precision.HIGHEST)]
    scatter x2 -> x0, local copies, waits for them, and re-layouts: 3.19 us -> none  [the longest x1 2.59 us: on_device(): jnp.zeros((row_count * CAPX, block_size, block_size), jnp.float32)]
  transfers between devices with their start and end apart: 12 -> 16, of which waited for: 6 -> 8; matrix products, arithmetic and copies ran while one was open for 43% -> 4% of each run, Pallas kernels for 0% -> 13%
where the time goes in v1:
time: 46.5 us; the launch traced here: 46.3 us
  starting transfers between devices  17.9 us (38%)
  waiting for transfers between devices  16.4 us (35%)
  Pallas kernels  8.8 us (19%)
  local copies, waits for them, and re-layouts  2.47 us (5%)
  other arithmetic  0.7 us (2%)
    ppermute x3, waiting for transfers between devices, ring_plan(): a_bwd = lax.ppermute(a_bwd, 'row', backward)  7.94 us
    ppermute x4, starting transfers between devices, ring_plan(): b_bwd = lax.ppermute(b_bwd, 'row', backward)  7.67 us
    pallas_call x2, Pallas kernels, add_products(): pl.pallas_call(functools.partial(product_kernel, (*sizes, limit, pieces,...  7.64 us
    ppermute x4, waiting for transfers between devices, ring_plan(): b_bwd = lax.ppermute(b_bwd, 'row', backward)  5.6 us
    ppermute x3, starting transfers between devices, ring_plan(): a_bwd = lax.ppermute(a_bwd, 'row', backward)  5 us
    ppermute x3, starting transfers between devices, ring_plan(): b_fwd = lax.ppermute(b_fwd, 'row', forward)  3.58 us
    ppermute x3, waiting for transfers between devices, ring_plan(): b_fwd = lax.ppermute(b_fwd, 'row', forward)  2.84 us
    unnamed x8, local copies, waits for them, and re-layouts  1.33 us
  transfers between devices with their start and end apart: 16, of which 8 were waited for; matrix products, arithmetic and copies ran while one was open for 4% of the time, Pallas kernels for 13%

profile of v1, /device:TPU:0, one launch (start us, length us, event | category | flops | bytes accessed | tf_op | source)
XLA Modules:
  0.0 46.3 jit_solution(2422181761328292229)
XLA Ops:
  0.0 0.5 collective-permute-start.1
  0.5 0.7 %convert_bitcast_fusion = f32[6,2]{0,1:T(2,128)S(1)} fusion(s32[1,1,6,2]{2,3,1,0:T(2,128)} %param.7), kind=kLoop, calls=%fused_computation.2 | loop fusion | flops 12 | bytes 96 | tf_op jit(solution)/shard_map/convert_element_type | solution.py:317
  1.1 0.1 copy.7
  1.2 1.0 %fusion = (f32[1,1,3,128,128]{4,3,2,1,0:T(8,128)S(1)}, f32[1,1,3,128,128]{4,3,2,1,0:T(8,128)S(1)}) fusion(f32[1,1,6,128,128]{4,3,2,1,0:T(8,128)} %param.6), kind=kLoop, calls=%fused_computation.3 | loop fusion | bytes 786432 | tf_op jit(solution)/shard_map/slice | solution.py:325
  2.3 2.6 %collective-permute-start.6 = (f32[392,128]{1,0:T(8,128)S(1)}, f32[392,128]{1,0:T(8,128)S(1)}, u32[]{:S(2)}, u32[]{:S(2)}) collective-permute-start(f32[392,128]{1,0:T(8,128)S(1)} %select_maximum_fusion.refs_7_), channel_id=1, source_target_pairs={{4,0},{8,4},{12,8},{14,12},{10,14},{6,10},{2,6},{0,2},{5,1},{9,5},... | collective-permute-start | bytes 602120 | tf_op jit(solution)/shard_map/ppermute | solution.py:342
  4.9 0.1 collective-permute-start.2
  5.0 2.0 %collective-permute-start.10 = (f32[392,128]{1,0:T(8,128)S(1)}, f32[392,128]{1,0:T(8,128)S(1)}, u32[]{:S(2)}, u32[]{:S(2)}) collective-permute-start(f32[392,128]{1,0:T(8,128)S(1)} %select_maximum_fusion.refs_7_), channel_id=1, source_target_pairs={{0,4},{4,8},{8,12},{12,14},{14,10},{10,6},{6,2},{2,0},{1,5},{5,9},... | collective-permute-start | bytes 602120 | tf_op jit(solution)/shard_map/ppermute | solution.py:341
  7.0 3.6 %collective-permute-done.6.refs_11_ = f32[392,128]{1,0:T(8,128)S(1)} collective-permute-done((f32[392,128]{1,0:T(8,128)S(1)}, f32[392,128]{1,0:T(8,128)S(1)}, u32[]{:S(2)}, u32[]{:S(2)}) %collective-permute-start.6) | collective-permute-done | bytes 200736 | tf_op jit(solution)/shard_map/ppermute | solution.py:342
  10.6 1.7 %collective-permute-start.7 = (f32[392,128]{1,0:T(8,128)S(1)}, f32[392,128]{1,0:T(8,128)S(1)}, u32[]{:S(2)}, u32[]{:S(2)}) collective-permute-start(f32[392,128]{1,0:T(8,128)S(1)} %collective-permute-done.6.refs_11_), channel_id=1, source_target_pairs={{4,0},{8,4},{12,8},{14,12},{10,14},{6,10},{2,6},{0,2},{5,1},{9,5},... | collective-permute-start | bytes 602120 | tf_op jit(solution)/shard_map/ppermute | solution.py:342
  12.3 1.6 %collective-permute-start.11 = (f32[384,128]{1,0:T(8,128)S(1)}, f32[384,128]{1,0:T(8,128)S(1)}, u32[]{:S(2)}, u32[]{:S(2)}) collective-permute-start(f32[384,128]{1,0:T(8,128)S(1)} %bitcast.11), channel_id=1, source_target_pairs={{4,0},{8,4},{12,8},{14,12},{10,14},{6,10},{2,6},{0,2},{5,1},{9,5},... | collective-permute-start | bytes 589832 | tf_op jit(solution)/shard_map/ppermute | solution.py:340
  13.9 0.0 collective-permute-done.2.refs_8_
  13.9 0.5 collective-permute-start.3
  14.3 2.4 %collective-permute-done.10.refs_9_ = f32[392,128]{1,0:T(8,128)S(1)} collective-permute-done((f32[392,128]{1,0:T(8,128)S(1)}, f32[392,128]{1,0:T(8,128)S(1)}, u32[]{:S(2)}, u32[]{:S(2)}) %collective-permute-start.10) | collective-permute-done | bytes 200736 | tf_op jit(solution)/shard_map/ppermute | solution.py:341
  16.7 0.3 collective-permute-start.12
  17.0 1.5 %collective-permute-done.7.refs_15_ = f32[392,128]{1,0:T(8,128)S(1)} collective-permute-done((f32[392,128]{1,0:T(8,128)S(1)}, f32[392,128]{1,0:T(8,128)S(1)}, u32[]{:S(2)}, u32[]{:S(2)}) %collective-permute-start.7) | collective-permute-done | bytes 200736 | tf_op jit(solution)/shard_map/ppermute | solution.py:342
  18.5 1.7 %collective-permute-start.8 = (f32[392,128]{1,0:T(8,128)S(1)}, f32[392,128]{1,0:T(8,128)S(1)}, u32[]{:S(2)}, u32[]{:S(2)}) collective-permute-start(f32[392,128]{1,0:T(8,128)S(1)} %collective-permute-done.7.refs_15_), channel_id=1, source_target_pairs={{4,0},{8,4},{12,8},{14,12},{10,14},{6,10},{2,6},{0,2},{5,1},{9,5},... | collective-permute-start | bytes 602120 | tf_op jit(solution)/shard_map/ppermute | solution.py:342
  20.2 2.5 %collective-permute-done.11.refs_10_ = f32[384,128]{1,0:T(8,128)S(1)} collective-permute-done((f32[384,128]{1,0:T(8,128)S(1)}, f32[384,128]{1,0:T(8,128)S(1)}, u32[]{:S(2)}, u32[]{:S(2)}) %collective-permute-start.11) | collective-permute-done | bytes 196640 | tf_op jit(solution)/shard_map/ppermute | solution.py:340
  22.7 1.7 %collective-permute-start.13 = (f32[384,128]{1,0:T(8,128)S(1)}, f32[384,128]{1,0:T(8,128)S(1)}, u32[]{:S(2)}, u32[]{:S(2)}) collective-permute-start(f32[384,128]{1,0:T(8,128)S(1)} %collective-permute-done.11.refs_10_), channel_id=1, source_target_pairs={{4,0},{8,4},{12,8},{14,12},{10,14},{6,10},{2,6},{0,2},{5,1},{9,5},... | collective-permute-start | bytes 589832 | tf_op jit(solution)/shard_map/ppermute | solution.py:340
  24.4 0.0 collective-permute-done.3.refs_12_
  24.4 0.3 collective-permute-start.4
  24.7 0.4 collective-permute-done.12.refs_13_
  25.1 1.4 %collective-permute-start.14 = (f32[392,128]{1,0:T(8,128)S(1)}, f32[392,128]{1,0:T(8,128)S(1)}, u32[]{:S(2)}, u32[]{:S(2)}) collective-permute-start(f32[392,128]{1,0:T(8,128)S(1)} %collective-permute-done.12.refs_13_), channel_id=1, source_target_pairs={{0,4},{4,8},{8,12},{12,14},{14,10},{10,6},{6,2},{2,0},{1,5},{5,9},... | collective-permute-start | bytes 602120 | tf_op jit(solution)/shard_map/ppermute | solution.py:341
  26.5 0.5 %collective-permute-done.8.refs_19_ = f32[392,128]{1,0:T(8,128)S(1)} collective-permute-done((f32[392,128]{1,0:T(8,128)S(1)}, f32[392,128]{1,0:T(8,128)S(1)}, u32[]{:S(2)}, u32[]{:S(2)}) %collective-permute-start.8) | collective-permute-done | bytes 200736 | tf_op jit(solution)/shard_map/ppermute | solution.py:342
  27.0 1.7 %collective-permute-start.9 = (f32[392,128]{1,0:T(8,128)S(1)}, f32[392,128]{1,0:T(8,128)S(1)}, u32[]{:S(2)}, u32[]{:S(2)}) collective-permute-start(f32[392,128]{1,0:T(8,128)S(1)} %collective-permute-done.8.refs_19_), channel_id=1, source_target_pairs={{4,0},{8,4},{12,8},{14,12},{10,14},{6,10},{2,6},{0,2},{5,1},{9,5},... | collective-permute-start | bytes 602120 | tf_op jit(solution)/shard_map/ppermute | solution.py:351
  28.7 2.5 %collective-permute-done.13.refs_14_ = f32[384,128]{1,0:T(8,128)S(1)} collective-permute-done((f32[384,128]{1,0:T(8,128)S(1)}, f32[384,128]{1,0:T(8,128)S(1)}, u32[]{:S(2)}, u32[]{:S(2)}) %collective-permute-start.13) | collective-permute-done | bytes 196640 | tf_op jit(solution)/shard_map/ppermute | solution.py:340
  31.2 1.7 %collective-permute-start.15 = (f32[384,128]{1,0:T(8,128)S(1)}, f32[384,128]{1,0:T(8,128)S(1)}, u32[]{:S(2)}, u32[]{:S(2)}) collective-permute-start(f32[384,128]{1,0:T(8,128)S(1)} %collective-permute-done.13.refs_14_), channel_id=1, source_target_pairs={{4,0},{8,4},{12,8},{14,12},{10,14},{6,10},{2,6},{0,2},{5,1},{9,5},... | collective-permute-start | bytes 589832 | tf_op jit(solution)/shard_map/ppermute | solution.py:340
  32.9 0.0 collective-permute-done.4.refs_16_
  32.9 0.3 collective-permute-start.5
  33.2 0.0 collective-permute-done.1.twin_ref
  33.2 0.0 collective-permute-start
  33.2 0.0 copy-start
  33.2 1.3 %copy-done = f32[1,2,10,128,128]{4,3,2,1,0:T(8,128)S(1)} copy-done((f32[1,2,10,128,128]{4,3,2,1,0:T(8,128)S(1)}, f32[1,2,10,128,128]{4,3,2,1,0:T(8,128)}, u32[]{:S(2)}) %copy-start) | copy-done | bytes 1310744
  34.5 0.0 copy-start.1
  34.5 0.0 copy-start.2
  34.5 0.0 copy-start.3
  34.5 1.2 %shard_map.64 = (bf16[40,128,256]{2,1,0:T(8,128)(2,1)S(1)}, f32[40,1,128]{2,1,0:T(1,128)S(1)}) custom-call(f32[20,128,128]{2,1,0:T(8,128)S(1)} %bitcast.9, f32[20,128,128]{2,1,0:T(8,128)S(1)} %collective-permute-done.1.twin_ref), custom_call_target="tpu_custom_call" | custom-call | tf_op jit(solution)/shard_map/pallas_call | solution.py:156
  35.7 0.0 collective-permute-done.refs_2_
  35.7 2.9 %collective-permute-done.15.refs_18_ = f32[384,128]{1,0:T(8,128)S(1)} collective-permute-done((f32[384,128]{1,0:T(8,128)S(1)}, f32[384,128]{1,0:T(8,128)S(1)}, u32[]{:S(2)}, u32[]{:S(2)}) %collective-permute-start.15) | collective-permute-done | bytes 196640 | tf_op jit(solution)/shard_map/ppermute | solution.py:340
  38.7 0.0 collective-permute-done.14.refs_17_
  38.7 0.0 copy-done.1
  38.7 0.0 copy-done.2
  38.7 0.0 copy-done.3
  38.7 4.9 %shard_map.65.refs_8_ = f32[16,128,128]{2,1,0:T(8,128)S(1)} custom-call(s32[32]{0:T(128)S(1)} %copy-done.2, s32[2,10]{1,0:T(2,128)S(1)} %bitcast.14, s32[2,10]{1,0:T(2,128)S(1)} %collective-permute-done.refs_2_, s32[16]{0:T(128)S(1)} %bitcast.16, bf16[40,128,256]{2,1,0:T(8,128)(2,1)S(1)} %get-tuple-element.7.refs_4_, ...), custom_call_target="tpu_custom_call" | custom-call | tf_op jit(solution)/shard_map/pallas_call | solution.py:288
  43.6 0.0 collective-permute-done.5.refs_6_
  43.6 0.0 collective-permute-done.9.refs_7_
  43.6 2.7 %shard_map.66 = f32[16,128,128]{2,1,0:T(8,128)} custom-call(s32[32]{0:T(128)S(1)} %copy-done.2, s32[2,10]{1,0:T(2,128)S(1)} %bitcast.15, s32[2,10]{1,0:T(2,128)S(1)} %collective-permute-done.refs_2_, s32[16]{0:T(128)S(1)} %bitcast.17, bf16[40,128,256]{2,1,0:T(8,128)(2,1)S(1)} %get-tuple-element.7.refs_4_, f32[40,1,128]{2,1,0:T(1,128)S(1)} %get-tuple-element.8.refs_5_, ...), custom_call_target="tpu_custom_call" | custom-call | tf_op jit(solution)/shard_map/pallas_call | solution.py:288
  (1 shorter events, 0.0 us)
Async XLA Ops:
  0.0 33.2 %collective-permute-start.1 = (f32[20,128,128]{2,1,0:T(8,128)}, f32[20,128,128]{2,1,0:T(8,128)S(1)}, u32[]{:S(2)}, u32[]{:S(2)}) collective-permute-start(f32[20,128,128]{2,1,0:T(8,128)} %bitcast.8), channel_id=1, source_target_pairs={{0,1},{1,0},{2,3},{3,2},{4,5},{5,4},{6,7},{7,6},{8,9},{9,8},{10,11... | collective-permute-start | bytes 3932168 | tf_op jit(solution)/shard_map/ppermute | solution.py:346
  2.3 8.3 %collective-permute-start.6 = (f32[392,128]{1,0:T(8,128)S(1)}, f32[392,128]{1,0:T(8,128)S(1)}, u32[]{:S(2)}, u32[]{:S(2)}) collective-permute-start(f32[392,128]{1,0:T(8,128)S(1)} %select_maximum_fusion.refs_7_), channel_id=1, source_target_pairs={{4,0},{8,4},{12,8},{14,12},{10,14},{6,10},{2,6},{0,2},{5,1},{9,5},... | collective-permute-start | bytes 602120 | tf_op jit(solution)/shard_map/ppermute | solution.py:342
  4.9 9.0 %collective-permute-start.2 = (f32[384,128]{1,0:T(8,128)S(1)}, f32[384,128]{1,0:T(8,128)S(1)}, u32[]{:S(2)}, u32[]{:S(2)}) collective-permute-start(f32[384,128]{1,0:T(8,128)S(1)} %bitcast.10), channel_id=1, source_target_pairs={{0,4},{4,8},{8,12},{12,14},{14,10},{10,6},{6,2},{2,0},{1,5},{5,9},... | collective-permute-start | bytes 589832 | tf_op jit(solution)/shard_map/ppermute | solution.py:339
  5.0 11.7 %collective-permute-start.10 = (f32[392,128]{1,0:T(8,128)S(1)}, f32[392,128]{1,0:T(8,128)S(1)}, u32[]{:S(2)}, u32[]{:S(2)}) collective-permute-start(f32[392,128]{1,0:T(8,128)S(1)} %select_maximum_fusion.refs_7_), channel_id=1, source_target_pairs={{0,4},{4,8},{8,12},{12,14},{14,10},{10,6},{6,2},{2,0},{1,5},{5,9},... | collective-permute-start | bytes 602120 | tf_op jit(solution)/shard_map/ppermute | solution.py:341
  10.6 7.9 %collective-permute-start.7 = (f32[392,128]{1,0:T(8,128)S(1)}, f32[392,128]{1,0:T(8,128)S(1)}, u32[]{:S(2)}, u32[]{:S(2)}) collective-permute-start(f32[392,128]{1,0:T(8,128)S(1)} %collective-permute-done.6.refs_11_), channel_id=1, source_target_pairs={{4,0},{8,4},{12,8},{14,12},{10,14},{6,10},{2,6},{0,2},{5,1},{9,5},... | collective-permute-start | bytes 602120 | tf_op jit(solution)/shard_map/ppermute | solution.py:342
  12.3 10.4 %collective-permute-start.11 = (f32[384,128]{1,0:T(8,128)S(1)}, f32[384,128]{1,0:T(8,128)S(1)}, u32[]{:S(2)}, u32[]{:S(2)}) collective-permute-start(f32[384,128]{1,0:T(8,128)S(1)} %bitcast.11), channel_id=1, source_target_pairs={{4,0},{8,4},{12,8},{14,12},{10,14},{6,10},{2,6},{0,2},{5,1},{9,5},... | collective-permute-start | bytes 589832 | tf_op jit(solution)/shard_map/ppermute | solution.py:340
  13.9 10.5 %collective-permute-start.3 = (f32[384,128]{1,0:T(8,128)S(1)}, f32[384,128]{1,0:T(8,128)S(1)}, u32[]{:S(2)}, u32[]{:S(2)}) collective-permute-start(f32[384,128]{1,0:T(8,128)S(1)} %collective-permute-done.2.refs_8_), channel_id=1, source_target_pairs={{0,4},{4,8},{8,12},{12,14},{14,10},{10,6},{6,2},{2,0},{1,5},{5,9},... | collective-permute-start | bytes 589832 | tf_op jit(solution)/shard_map/ppermute | solution.py:339
  16.7 8.4 %collective-permute-start.12 = (f32[392,128]{1,0:T(8,128)S(1)}, f32[392,128]{1,0:T(8,128)S(1)}, u32[]{:S(2)}, u32[]{:S(2)}) collective-permute-start(f32[392,128]{1,0:T(8,128)S(1)} %collective-permute-done.10.refs_9_), channel_id=1, source_target_pairs={{0,4},{4,8},{8,12},{12,14},{14,10},{10,6},{6,2},{2,0},{1,5},{5,9},... | collective-permute-start | bytes 602120 | tf_op jit(solution)/shard_map/ppermute | solution.py:341
  18.5 8.5 %collective-permute-start.8 = (f32[392,128]{1,0:T(8,128)S(1)}, f32[392,128]{1,0:T(8,128)S(1)}, u32[]{:S(2)}, u32[]{:S(2)}) collective-permute-start(f32[392,128]{1,0:T(8,128)S(1)} %collective-permute-done.7.refs_15_), channel_id=1, source_target_pairs={{4,0},{8,4},{12,8},{14,12},{10,14},{6,10},{2,6},{0,2},{5,1},{9,5},... | collective-permute-start | bytes 602120 | tf_op jit(solution)/shard_map/ppermute | solution.py:342
  22.7 8.5 %collective-permute-start.13 = (f32[384,128]{1,0:T(8,128)S(1)}, f32[384,128]{1,0:T(8,128)S(1)}, u32[]{:S(2)}, u32[]{:S(2)}) collective-permute-start(f32[384,128]{1,0:T(8,128)S(1)} %collective-permute-done.11.refs_10_), channel_id=1, source_target_pairs={{4,0},{8,4},{12,8},{14,12},{10,14},{6,10},{2,6},{0,2},{5,1},{9,5},... | collective-permute-start | bytes 589832 | tf_op jit(solution)/shard_map/ppermute | solution.py:340
  24.4 8.5 %collective-permute-start.4 = (f32[384,128]{1,0:T(8,128)S(1)}, f32[384,128]{1,0:T(8,128)S(1)}, u32[]{:S(2)}, u32[]{:S(2)}) collective-permute-start(f32[384,128]{1,0:T(8,128)S(1)} %collective-permute-done.3.refs_12_), channel_id=1, source_target_pairs={{0,4},{4,8},{8,12},{12,14},{14,10},{10,6},{6,2},{2,0},{1,5},{5,9},... | collective-permute-start | bytes 589832 | tf_op jit(solution)/shard_map/ppermute | solution.py:339
  25.1 13.5 %collective-permute-start.14 = (f32[392,128]{1,0:T(8,128)S(1)}, f32[392,128]{1,0:T(8,128)S(1)}, u32[]{:S(2)}, u32[]{:S(2)}) collective-permute-start(f32[392,128]{1,0:T(8,128)S(1)} %collective-permute-done.12.refs_13_), channel_id=1, source_target_pairs={{0,4},{4,8},{8,12},{12,14},{14,10},{10,6},{6,2},{2,0},{1,5},{5,9},... | collective-permute-start | bytes 602120 | tf_op jit(solution)/shard_map/ppermute | solution.py:341
  27.0 16.7 %collective-permute-start.9 = (f32[392,128]{1,0:T(8,128)S(1)}, f32[392,128]{1,0:T(8,128)S(1)}, u32[]{:S(2)}, u32[]{:S(2)}) collective-permute-start(f32[392,128]{1,0:T(8,128)S(1)} %collective-permute-done.8.refs_19_), channel_id=1, source_target_pairs={{4,0},{8,4},{12,8},{14,12},{10,14},{6,10},{2,6},{0,2},{5,1},{9,5},... | collective-permute-start | bytes 602120 | tf_op jit(solution)/shard_map/ppermute | solution.py:351
  31.2 7.5 %collective-permute-start.15 = (f32[384,128]{1,0:T(8,128)S(1)}, f32[384,128]{1,0:T(8,128)S(1)}, u32[]{:S(2)}, u32[]{:S(2)}) collective-permute-start(f32[384,128]{1,0:T(8,128)S(1)} %collective-permute-done.13.refs_14_), channel_id=1, source_target_pairs={{4,0},{8,4},{12,8},{14,12},{10,14},{6,10},{2,6},{0,2},{5,1},{9,5},... | collective-permute-start | bytes 589832 | tf_op jit(solution)/shard_map/ppermute | solution.py:340
  32.9 10.7 %collective-permute-start.5 = (f32[384,128]{1,0:T(8,128)S(1)}, f32[384,128]{1,0:T(8,128)S(1)}, u32[]{:S(2)}, u32[]{:S(2)}) collective-permute-start(f32[384,128]{1,0:T(8,128)S(1)} %collective-permute-done.4.refs_16_), channel_id=1, source_target_pairs={{0,4},{4,8},{8,12},{12,14},{14,10},{10,6},{6,2},{2,0},{1,5},{5,9},... | collective-permute-start | bytes 589832 | tf_op jit(solution)/shard_map/ppermute | solution.py:350
  33.2 2.5 %collective-permute-start = (s32[2,10]{1,0:T(2,128)}, s32[2,10]{1,0:T(2,128)S(1)}, u32[]{:S(2)}, u32[]{:S(2)}) collective-permute-start(s32[2,10]{1,0:T(2,128)} %bitcast.13), channel_id=1, source_target_pairs={{0,1},{1,0},{2,3},{3,2},{4,5},{5,4},{6,7},{7,6},{8,9},{9,8},{10,11... | collective-permute-start | bytes 248 | tf_op jit(solution)/shard_map/ppermute | solution.py:348
  33.2 1.3 %copy-start = (f32[1,2,10,128,128]{4,3,2,1,0:T(8,128)S(1)}, f32[1,2,10,128,128]{4,3,2,1,0:T(8,128)}, u32[]{:S(2)}) copy-start(f32[1,2,10,128,128]{4,3,2,1,0:T(8,128)} %param.9) | copy-start | bytes 3932164
  34.5 4.1 %copy-start.1 = (s32[1,2,10]{2,1,0:T(2,128)S(1)}, s32[1,2,10]{2,1,0:T(2,128)}, u32[]{:S(2)}) copy-start(s32[1,2,10]{2,1,0:T(2,128)} %param.10) | copy-start | bytes 244
  34.5 4.1 %copy-start.2 = (s32[32]{0:T(128)S(1)}, s32[32]{0:T(128)}, u32[]{:S(2)}) copy-start(s32[32]{0:T(128)} %refs_0_.3) | copy-start | bytes 388
  34.5 4.1 %copy-start.3 = (s32[1,1,16]{2,1,0:T(1,128)S(1)}, s32[1,1,16]{2,1,0:T(1,128)}, u32[]{:S(2)}) copy-start(s32[1,1,16]{2,1,0:T(1,128)} %param.11) | copy-start | bytes 196

commit v2 on v1

--- a/solution.py
+++ b/solution.py
@@ -135,101 +135,209 @@
     return pltpu.with_memory_space_constraint(x, pltpu.VMEM)
 
 
-SMEM_SPEC = pl.BlockSpec(memory_space=pltpu.SMEM)
+def in_hbm(x):
+    return pltpu.with_memory_space_constraint(x, pltpu.HBM)
+
+
 VMEM_SPEC = pl.BlockSpec(memory_space=pltpu.VMEM)
-
-
-def split_kernel(own_ref, twin_ref, parts_ref, norms_ref):
-    count = own_ref.shape[0]
-    for half, ref in enumerate((own_ref, twin_ref)):
-
-        def one(q, _, half=half, ref=ref):
-            block = ref[q]
-            parts_ref[half * count + q] = jnp.concatenate(split_bf16(block), axis=1)
-            norms_ref[half * count + q] = jnp.broadcast_to(norm_of(block), norms_ref.shape[1:])
-
-        lax.fori_loop(0, count, one, None, unroll=4)
-
-
-def split_ks(own, twin):
-    count, block_size, _ = own.shape
+HBM_SPEC = pl.BlockSpec(memory_space=pltpu.HBM)
+GRANT = pltpu.CompilerParams(vmem_limit_bytes=VMEM_GRANT)
+
+
+def small_cost(microseconds):
+    return pl.CostEstimate(flops=0, bytes_accessed=int(3.7e6 * microseconds), transcendentals=0)
+
+
+def start_all(pairs, sems):
+    copies = [pltpu.make_async_copy(src, dst, sems.at[n]) for n, (src, dst) in enumerate(pairs)]
+    for copy in copies:
+        copy.start()
+    return copies
+
+
+def pack_kernel(lead, index_ref, places_ref, blocks_ref, ks_ref, lead_ref, rest_ref, ks_out_ref, index, places, sems):
+    slots = index.shape[3]
+    width = lead_ref.shape[1]
+    lead_rows = blocks_ref.shape[0] // slots * lead
+    rest_rows = blocks_ref.shape[0] - lead_rows
+    ks_rows = ks_ref.shape[0]
+    copies = start_all(
+        [
+            (index_ref, index),
+            (places_ref, places),
+            (blocks_ref.at[pl.ds(0, lead_rows)], lead_ref.at[pl.ds(0, lead_rows)]),
+            (blocks_ref.at[pl.ds(lead_rows, rest_rows)], rest_ref.at[pl.ds(0, rest_rows)]),
+            (ks_ref, ks_out_ref.at[pl.ds(0, ks_rows)]),
+        ],
+        sems,
+    )
+
+    def label_rows(ref, rows, numbers):
+        shape = (ref.shape[0] - rows, width)
+        line = lax.broadcasted_iota(jnp.int32, shape, 0)
+        lane = lax.broadcasted_iota(jnp.int32, shape, 1)
+        labels = jnp.zeros(shape, jnp.int32)
+        for (x, y), number in numbers:
+            labels = jnp.where((line == x) & (lane == y), number, labels)
+        ref[pl.ds(rows, shape[0]), :] = labels.astype(jnp.float32)
+
+    copies[0].wait()
+    copies[1].wait()
+    for ref, rows, first, count in ((lead_ref, lead_rows, 0, lead), (rest_ref, rest_rows, lead, slots - lead)):
+        label_rows(
+            ref,
+            rows,
+            [((n, field), index[0, 0, field, first + n]) for n in range(count) for field in range(2)],
+        )
+    _, stops, present = places.shape
+    label_rows(
+        ks_out_ref, ks_rows, [((x, y), places[0, x, y]) for x in range(stops) for y in range(present)]
+    )
+    for copy in copies[2:]:
+        copy.wait()
+
+
+def pack(blocks, index, ks, places, lead):
+    slots = index.shape[3]
+    rows, width = blocks.shape
+    ks_rows = ks.shape[0]
+    lead_rows = rows // slots * lead
     return pl.pallas_call(
-        split_kernel,
+        functools.partial(pack_kernel, lead),
         out_shape=(
-            pltpu.VMEM((2 * count, block_size, 2 * block_size), jnp.bfloat16),
-            pltpu.VMEM((2 * count, 1, block_size), jnp.float32),
+            pltpu.VMEM((lead_rows + -(-lead // 8) * 8, width), jnp.float32),
+            pltpu.VMEM((rows - lead_rows + -(-(slots - lead) // 8) * 8, width), jnp.float32),
+            pltpu.VMEM((ks_rows + -(-places.shape[1] // 8) * 8, width), jnp.float32),
         ),
-        in_specs=[VMEM_SPEC] * 2,
-        out_specs=(VMEM_SPEC,) * 2,
-        compiler_params=pltpu.CompilerParams(vmem_limit_bytes=VMEM_GRANT),
-    )(in_vmem(own), in_vmem(twin))
-
-
-def product_kernel(config, *refs):
-    row_count, stop_count, half_cols, limit, pieces, first = config
-    perm_ref, own_place_ref, twin_place_ref, target_ref, parts_ref, norms_ref = refs[:6]
-    chunk_refs = refs[6 : 6 + len(pieces)]
-    rest = refs[6 + len(pieces) :]
-    if first:
-        c_ref = rest[0]
-        rest = rest[1:]
-    else:
-        c_in_ref, c_ref = rest[:2]
-        rest = rest[2:]
-    target_at, ks_at, label, list_t, list_q, list_b, held, sems = rest
-    block_size = c_ref.shape[-1]
-    half_stops, present = own_place_ref.shape
-    row, col = lax.axis_index("row"), lax.axis_index("col")
-
-    copies = []
-    for number, (blocks, _, labels) in enumerate(pieces):
-        if labels is None:
-            chunk_ref = chunk_refs[number]
-            rows = pl.ds(blocks * block_size, chunk_ref.shape[0] - blocks * block_size)
-            slot = len(copies)
-            copies.append(pltpu.make_async_copy(chunk_ref.at[rows], label.at[slot], sems.at[slot]))
-            copies[-1].start()
-
-    for i in range(target_at.shape[0]):
-        target_at[i] = -1
-    for i in range(ks_at.shape[0]):
-        ks_at[i] = -1
-    for t in range(target_ref.shape[0]):
-        target_at[target_ref[t]] = t
+        in_specs=[HBM_SPEC] * 4,
+        out_specs=(VMEM_SPEC,) * 3,
+        scratch_shapes=[
+            pltpu.SMEM(index.shape, jnp.int32),
+            pltpu.SMEM(places.shape, jnp.int32),
+            pltpu.SemaphoreType.DMA((5,)),
+        ],
+        compiler_params=GRANT,
+        cost_estimate=small_cost(1),
+    )(*map(in_hbm, (index, places, blocks, ks)))
+
+
+def window_kernel(
+    half_cols, present, perm_ref, target_ref, own_ref, twin_ref, parts_ref, norms_ref, table_ref,
+    perm, targets, own_place, twin_place, table, sems, out_sem,
+):
+    block_size = own_ref.shape[1]
+    count = parts_ref.shape[0] // 2
+    half_stops = count // present
+    ks_rows = count * block_size
+    col = lax.axis_index("col")
+    ks_cells = 2 * half_stops * BR * BR
+    target_cells = BR * half_cols
+    place_rows = pl.ds(ks_rows, own_ref.shape[0] - ks_rows)
+    copies = start_all(
+        [
+            (perm_ref, perm),
+            (target_ref, targets),
+            (own_ref.at[place_rows], own_place),
+            (twin_ref.at[place_rows], twin_place),
+        ],
+        sems,
+    )
+    for i in range(ks_cells + target_cells):
+        table[i] = -1
+    for copy in copies:
+        copy.wait()
+    for i in range(perm.shape[0]):
+        table[ks_cells + target_cells + i] = perm[i]
+    for t in range(targets.shape[2]):
+        table[ks_cells + targets[0, 0, t]] = t
     for local in range(half_stops):
         own_base = (col * half_stops + local) * BR * BR
         twin_base = ((1 - col) * half_stops + local) * BR * BR
         for q in range(present):
-            ks_at[own_base + own_place_ref[local, q]] = local * present + q
-            ks_at[twin_base + twin_place_ref[local, q]] = (half_stops + local) * present + q
+            table[own_base + own_place[local, q].astype(jnp.int32)] = local * present + q
+            table[twin_base + twin_place[local, q].astype(jnp.int32)] = (half_stops + local) * present + q
+    publish = pltpu.make_async_copy(table, table_ref, out_sem)
+    publish.start()
+    for half, ref in enumerate((own_ref, twin_ref)):
+
+        def one(q, _, half=half, ref=ref):
+            block = ref[pl.ds(pl.multiple_of(q * block_size, block_size), block_size), :]
+            parts_ref[half * count + q] = jnp.concatenate(split_bf16(block), axis=1)
+            norms_ref[half * count + q] = jnp.broadcast_to(norm_of(block), norms_ref.shape[1:])
+
+        lax.fori_loop(0, count, one, None, unroll=4)
+    publish.wait()
+
+
+def prepare_window(row_perm, targets, own, twin, half_cols, half_stops, present):
+    rows, block_size = own.shape
+    count = half_stops * present
+    place_rows = rows - count * block_size
+    cells = 2 * half_stops * BR * BR + BR * half_cols + row_perm.shape[0]
+    cells = -(-cells // 128) * 128
+    return pl.pallas_call(
+        functools.partial(window_kernel, half_cols, present),
+        out_shape=(
+            pltpu.VMEM((2 * count, block_size, 2 * block_size), jnp.bfloat16),
+            pltpu.VMEM((2 * count, 1, block_size), jnp.float32),
+            pltpu.VMEM((cells,), jnp.int32),
+        ),
+        in_specs=[HBM_SPEC] * 2 + [VMEM_SPEC] * 2,
+        out_specs=(VMEM_SPEC,) * 3,
+        scratch_shapes=[
+            pltpu.SMEM(row_perm.shape, jnp.int32),
+            pltpu.SMEM(targets.shape, jnp.int32),
+            pltpu.SMEM((place_rows, block_size), jnp.float32),
+            pltpu.SMEM((place_rows, block_size), jnp.float32),
+            pltpu.SMEM((cells,), jnp.int32),
+            pltpu.SemaphoreType.DMA((4,)),
+            pltpu.SemaphoreType.DMA,
+        ],
+        compiler_params=GRANT,
+        cost_estimate=small_cost(2),
+    )(in_hbm(row_perm), in_hbm(targets), in_vmem(own), in_vmem(twin))
+
+
+def product_kernel(config, *refs):
+    row_count, stop_count, half_cols, limit, pieces, first, final = config
+    table_ref, parts_ref, norms_ref = refs[:3]
+    chunk_refs = refs[3 : 3 + len(pieces)]
+    rest = refs[3 + len(pieces) + (not first) + (final == "touched") :]
+    c_ref = rest[0]
+    if final:
+        out_ref = rest[1]
+        rest = rest[1:]
+    table, label, list_t, list_q, list_b, touched, held, sems, out_sems = rest[1:]
+    block_size = c_ref.shape[-1]
+    row = lax.axis_index("row")
+    ks_cells = stop_count * BR * BR
+    perm_at = ks_cells + BR * half_cols
+
+    moves = [(table_ref, table)]
+    for number, blocks in enumerate(pieces):
+        rows = pl.ds(blocks * block_size, label.shape[1])
+        moves.append((chunk_refs[number].at[rows], label.at[number]))
+    copies = start_all(moves, sems)
     if first:
         c_ref[...] = jnp.zeros_like(c_ref)
-    else:
-        c_ref[...] = c_in_ref[...]
     for copy in copies:
         copy.wait()
 
-    slots = {}
-    for number, (_, _, labels) in enumerate(pieces):
-        if labels is None:
-            slots[number] = len(slots)
     found = (jnp.int32(0), jnp.int32(0))
-    for number, (blocks, offset, labels) in enumerate(pieces):
-        chunk_ref = chunk_refs[number]
-        slot = slots[number if labels is None else labels]
-
-        def look(b, found, chunk_ref=chunk_ref, slot=slot, offset=offset):
+    for number, blocks in enumerate(pieces):
+
+        def look(b, found, number=number, chunk_ref=chunk_refs[number]):
             pairs, kept = found
-            position = perm_ref[label[slot, offset + b, 0].astype(jnp.int32)]
-            column = label[slot, offset + b, 1].astype(jnp.int32)
+            position = table[perm_at + label[number, b, 0].astype(jnp.int32)]
+            column = label[number, b, 1].astype(jnp.int32)
             behind = lax.div(position, BR) - row
             stop = jnp.where(behind < 0, behind + row_count, behind)
             in_window = stop < stop_count
             place = jnp.minimum(stop, stop_count - 1) * BR * BR + lax.rem(position, BR)
             before = pairs
             for i in range(BR):
-                target = target_at[i * half_cols + column]
-                ks = ks_at[place + i * BR]
+                target = table[ks_cells + i * half_cols + column]
+                ks = table[place + i * BR]
                 list_t[pairs] = target
                 list_q[pairs] = ks
                 list_b[pairs] = kept
@@ -270,93 +378,132 @@
             c_ref[target] += jnp.where(keep, value, 0.0)
 
     lax.fori_loop(0, lax.div(pairs + UNROLL - 1, UNROLL), multiply, None)
-
-
-def add_products(sizes, tables, parts, norms, accumulated, pieces, chunks, shape):
+    if final == "whole":
+        copy = pltpu.make_async_copy(c_ref, out_ref, out_sems.at[0])
+        copy.start()
+        copy.wait()
+    elif final == "touched":
+        targets = c_ref.shape[0]
+        for t in range(targets):
+            touched[t] = 0
+
+        def touch(p, _):
+            touched[list_t[p]] = 1
+
+        lax.fori_loop(0, pairs, touch, None)
+        for begin in (True, False):
+            for t in range(targets):
+                copy = pltpu.make_async_copy(c_ref.at[t], out_ref.at[t], out_sems.at[t])
+
+                @pl.when(touched[t] == 1)
+                def _(copy=copy, begin=begin):
+                    (copy.start if begin else copy.wait)()
+
+
+def add_products(sizes, window, accumulated, pieces, chunks, shape, final=None, written=None):
     block_size = shape[-1]
     limit = FILTER * block_size * math.sqrt(block_size)
     first = accumulated is None
-    blocks = sum(piece[0] for piece in pieces)
-    labelled = [n for n, piece in enumerate(pieces) if piece[2] is None]
-    label_rows = chunks[labelled[0]].shape[0] - pieces[labelled[0]][0] * block_size
-    operands = [*tables, in_vmem(parts), in_vmem(norms), *map(in_vmem, chunks)]
-    in_specs = [SMEM_SPEC] * len(tables) + [VMEM_SPEC] * (2 + len(chunks))
+    blocks = sum(pieces)
+    label_rows = -(-max(pieces) // 8) * 8
+    parts, norms, table = window
+    operands = [*map(in_vmem, (table, parts, norms, *chunks))]
+    aliases = {}
     if not first:
+        aliases = {len(operands): 0}
         operands.append(in_vmem(accumulated))
-        in_specs.append(VMEM_SPEC)
+    if written is not None:
+        aliases[len(operands)] = 1
+        operands.append(in_hbm(written))
+    in_specs = [VMEM_SPEC] * (len(operands) - (written is not None)) + [HBM_SPEC] * (written is not None)
     longest = blocks * BR + 2 * UNROLL
+    outs = 1 if final is None else 2
+    out_shape = [pltpu.VMEM(shape, jnp.float32), pltpu.HBM(shape, jnp.float32)][:outs]
     return pl.pallas_call(
-        functools.partial(product_kernel, (*sizes, limit, pieces, first)),
-        out_shape=pltpu.VMEM(shape, jnp.float32) if first else jax.ShapeDtypeStruct(shape, jnp.float32),
+        functools.partial(product_kernel, (*sizes, limit, pieces, first, final)),
+        out_shape=out_shape,
         in_specs=in_specs,
-        out_specs=VMEM_SPEC,
+        out_specs=[VMEM_SPEC, HBM_SPEC][:outs],
         scratch_shapes=[
-            pltpu.SMEM((BR * sizes[2],), jnp.int32),
-            pltpu.SMEM((sizes[1] * BR * BR,), jnp.int32),
-            pltpu.SMEM((len(labelled), label_rows, block_size), jnp.float32),
+            pltpu.SMEM(table.shape, jnp.int32),
+            pltpu.SMEM((len(pieces), label_rows, block_size), jnp.float32),
             pltpu.SMEM((longest,), jnp.int32),
             pltpu.SMEM((longest,), jnp.int32),
             pltpu.SMEM((longest,), jnp.int32),
+            pltpu.SMEM((shape[0],), jnp.int32),
             pltpu.VMEM((blocks, block_size, block_size), jnp.float32),
-            pltpu.SemaphoreType.DMA((len(labelled),)),
+            pltpu.SemaphoreType.DMA((1 + len(pieces),)),
+            pltpu.SemaphoreType.DMA((shape[0],)),
         ],
-        compiler_params=pltpu.CompilerParams(vmem_limit_bytes=VMEM_GRANT),
+        input_output_aliases=aliases,
+        compiler_params=GRANT,
+        cost_estimate=small_cost(2),
     )(*operands)
+
+
+def tied(values, token):
+    return lax.optimization_barrier((*values, token))[:-1]
 
 
 def ring_plan(d_blocks, d_index, row_perm, ks_blocks, ks_index, c_index):
     row_count = lax.axis_size("row")
     block_size = d_blocks.shape[-1]
     half_cols = row_perm.shape[0] // lax.axis_size("col")
-    own = d_blocks.reshape(-1, block_size)
     slots = d_blocks.shape[2]
     lead = slots // 2
-    tail = slots - lead
-    label_rows = -(-slots // 8) * 8
-    labels = jnp.pad(
-        d_index[0, 0].astype(jnp.float32), ((0, label_rows - slots), (0, block_size - 2))
-    )
     order = ring_order(row_count)
     forward = [(order[i], order[(i + 1) % row_count]) for i in range(row_count)]
     backward = [(b, a) for a, b in forward]
     twins = [(0, 1), (1, 0)]
-
-    first_part = own[: lead * block_size]
-    second_part = jnp.concatenate([own[lead * block_size :], labels], axis=0)
-    pieces, chunks = [], []
-
-    def arrived(first, second):
-        pieces.append((lead, 0, len(pieces) + 1))
-        pieces.append((tail, lead, None))
-        chunks.extend([first, second])
-
-    arrived(first_part, second_part)
-    a_fwd = a_bwd = first_part
-    b_fwd = b_bwd = second_part
-    half = row_count // 2
-    ks_own = ks_blocks.reshape(-1, block_size, block_size)
-    for step in range(1, half):
-        a_fwd = lax.ppermute(a_fwd, "row", forward)
-        a_bwd = lax.ppermute(a_bwd, "row", backward)
-        b_fwd = lax.ppermute(b_fwd, "row", forward)
-        b_bwd = lax.ppermute(b_bwd, "row", backward)
-        arrived(a_fwd, b_fwd)
-        arrived(a_bwd, b_bwd)
-        if step == 1:
-            ks_twin = lax.ppermute(ks_own, "col", twins)
-            ks_places = ks_index.reshape(ks_index.shape[1:])
-            ks_places_twin = lax.ppermute(ks_places, "col", twins)
-            parts, norms = split_ks(ks_own, ks_twin)
-    a_fwd = lax.ppermute(a_fwd, "row", forward)
-    b_bwd = lax.ppermute(b_bwd, "row", backward)
-
-    tables = [row_perm, ks_places, ks_places_twin, c_index.reshape(-1)]
     stop_count = 2 * ks_blocks.shape[1]
     shape = (c_index.shape[-1], block_size, block_size)
     sizes = (row_count, stop_count, half_cols)
-    partial = add_products(sizes, tables, parts, norms, None, pieces, chunks, shape)
-    last = [(lead, 0, 1), (tail, lead, None)]
-    total = add_products(sizes, tables, parts, norms, partial, last, [a_fwd, b_bwd], shape)
+
+    _, half_stops, present = ks_index.shape
+    a_fwd, b_fwd, ks_own = pack(
+        d_blocks.reshape(-1, block_size),
+        jnp.swapaxes(d_index, 2, 3),
+        ks_blocks.reshape(-1, block_size),
+        ks_index,
+        lead,
+    )
+    a_bwd, b_bwd = a_fwd, b_fwd
+    ks_twin = lax.ppermute(ks_own, "col", twins)
+    window = prepare_window(row_perm, c_index, ks_own, ks_twin, half_cols, half_stops, present)
+    pieces, chunks = [], []
+    accumulated = None
+
+    def arrived(first, second):
+        pieces.extend([lead, slots - lead])
+        chunks.extend([first, second])
+
+    arrived(a_fwd, b_fwd)
+    written = []
+    half = row_count // 2
+    for step in range(1, half + 1):
+        a_fwd = lax.ppermute(a_fwd, "row", forward)
+        b_bwd = lax.ppermute(b_bwd, "row", backward)
+        if step > 1:
+            if step > 2:
+                (accumulated,) = tied((accumulated,), ready)
+            final = {half - 1: "whole", half: "touched"}.get(step)
+            accumulated, *written = add_products(
+                sizes, window, accumulated, pieces, chunks, shape, final, *written
+            )
+            pieces, chunks = [], []
+        if step < half:
+            if step > 1:
+                a_bwd, b_fwd = tied((a_bwd, b_fwd), window[1] if step == 2 else before)
+            before = accumulated
+            a_bwd = lax.ppermute(a_bwd, "row", backward)
+            b_fwd = lax.ppermute(b_fwd, "row", forward)
+            arrived(a_fwd, b_fwd)
+            arrived(a_bwd, b_bwd)
+            ready = a_fwd
+    arrived(a_fwd, b_bwd)
+    _, total = add_products(
+        sizes, window, accumulated, pieces, chunks, shape, "touched", written[0]
+    )
     return total.reshape(c_index.shape + (block_size, block_size))
 
 

time: 46.5 us -> 40 us (0.86)
  waiting for transfers between devices: 16.4 us -> 9.4 us
  Pallas kernels: 8.8 us -> 14.3 us
  local copies, waits for them, and re-layouts: 2.47 us -> 0 us
  starting transfers between devices: 17.9 us -> 16.1 us
  other arithmetic: 0.7 us -> 0 us
    ppermute x4, starting transfers between devices: 1.2 us -> 8.67 us  [ring_plan(): a_fwd = lax.ppermute(a_fwd, 'row', forward)]
    ppermute x4, starting transfers between devices: 7.67 us -> 0.83 us  [ring_plan(): b_bwd = lax.ppermute(b_bwd, 'row', backward)]
    ppermute x4, waiting for transfers between devices: 5.6 us -> 0.09 us  [ring_plan(): b_bwd = lax.ppermute(b_bwd, 'row', backward)]
    ppermute x4, waiting for transfers between devices: 0.01 us -> 4.71 us  [ring_plan(): a_fwd = lax.ppermute(a_fwd, 'row', forward)]
    ppermute x3, starting transfers between devices: 5 us -> 0.48 us  [ring_plan(): a_bwd = lax.ppermute(a_bwd, 'row', backward)]
    ppermute x3, waiting for transfers between devices: 7.94 us -> 4.41 us  [ring_plan(): a_bwd = lax.ppermute(a_bwd, 'row', backward)]
    pallas_call x2 -> x4, Pallas kernels: 7.64 us -> 10.7 us  [add_products(): pl.pallas_call(functools.partial(product_kernel, (*sizes, limit, pieces,...]
    ppermute x3, waiting for transfers between devices: 2.84 us -> 0.19 us  [ring_plan(): b_fwd = lax.ppermute(b_fwd, 'row', forward)]
  transfers between devices with their start and end apart: 16 -> 15, of which waited for: 8 -> 7; matrix products, arithmetic and copies ran while one was open for 4% -> 0% of each run, Pallas kernels for 13% -> 27%
where the time goes in v2:
time: 40 us; the launch traced here: 39.9 us
  starting transfers between devices  16.1 us (40%)
  Pallas kernels  14.3 us (36%)
  waiting for transfers between devices  9.4 us (24%)
    pallas_call x4, Pallas kernels, add_products(): pl.pallas_call(functools.partial(product_kernel, (*sizes, limit, pieces,...  10.7 us
    ppermute x4, starting transfers between devices, ring_plan(): a_fwd = lax.ppermute(a_fwd, 'row', forward)  8.67 us
    ppermute x3, starting transfers between devices, ring_plan(): b_fwd = lax.ppermute(b_fwd, 'row', forward)  5.6 us
    ppermute x4, waiting for transfers between devices, ring_plan(): a_fwd = lax.ppermute(a_fwd, 'row', forward)  4.71 us
    ppermute x3, waiting for transfers between devices, ring_plan(): a_bwd = lax.ppermute(a_bwd, 'row', backward)  4.41 us
    pallas_call x1, Pallas kernels, prepare_window(): pl.pallas_call(functools.partial(window_kernel, half_cols, present), out_...  2.06 us
    pallas_call x1, Pallas kernels, pack(): pl.pallas_call(functools.partial(pack_kernel, lead), out_shape=(pltpu.VME...  1.57 us
    ppermute x4, starting transfers between devices, ring_plan(): b_bwd = lax.ppermute(b_bwd, 'row', backward)  0.83 us
  transfers between devices with their start and end apart: 15, of which 7 were waited for; matrix products, arithmetic and copies ran while one was open for 0% of the time, Pallas kernels for 27%

profile of v2, /device:TPU:0, one launch (start us, length us, event | category | flops | bytes accessed | tf_op | source)
XLA Modules:
  0.0 39.9 jit_solution(16580960129303614482)
XLA Ops:
  0.0 1.6 %shard_map.64 = (f32[392,128]{1,0:T(8,128)S(1)}, f32[392,128]{1,0:T(8,128)S(1)}, f32[2568,128]{1,0:T(8,128)S(1)}) custom-call(s32[1,1,2,6]{3,2,1,0:T(2,128)} %bitcast.6, s32[1,2,10]{2,1,0:T(2,128)} %places_ref.1, f32[768,128]{1,0:T(8,128)} %bitcast.5, f32[2560,128]{1,0:T(8,128)} %bitcast.4), custom_call_target="tpu_custom_call" | custom-call | bytes 3700000 | tf_op jit(solution)/shard_map/pallas_call | solution.py:205
  1.6 0.5 %collective-permute-start = (f32[2568,128]{1,0:T(8,128)S(1)}, f32[2568,128]{1,0:T(8,128)S(1)}, u32[]{:S(2)}, u32[]{:S(2)}) collective-permute-start(f32[2568,128]{1,0:T(8,128)S(1)} %get-tuple-element.22.own_ref), channel_id=1, source_target_pairs={{0,1},{1,0},{2,3},{3,2},{4,5},{5,4},{6,7},{7,6},{8,9},{9,8},{10,11... | collective-permute-start | bytes 3944456 | tf_op jit(solution)/shard_map/ppermute | solution.py:471
  2.1 2.6 %collective-permute-start.1 = (f32[392,128]{1,0:T(8,128)S(1)}, f32[392,128]{1,0:T(8,128)S(1)}, u32[]{:S(2)}, u32[]{:S(2)}) collective-permute-start(f32[392,128]{1,0:T(8,128)S(1)} %get-tuple-element.26.refs_3_), channel_id=1, source_target_pairs={{0,4},{4,8},{8,12},{12,14},{14,10},{10,6},{6,2},{2,0},{1,5},{5,9},... | collective-permute-start | bytes 602120 | tf_op jit(solution)/shard_map/ppermute | solution.py:484
  4.7 0.0 collective-permute-start.5
  4.8 2.0 %collective-permute-start.10 = (f32[392,128]{1,0:T(8,128)S(1)}, f32[392,128]{1,0:T(8,128)S(1)}, u32[]{:S(2)}, u32[]{:S(2)}) collective-permute-start(f32[392,128]{1,0:T(8,128)S(1)} %get-tuple-element.27.refs_4_), channel_id=1, source_target_pairs={{0,4},{4,8},{8,12},{12,14},{14,10},{10,6},{6,2},{2,0},{1,5},{5,9},... | collective-permute-start | bytes 602120 | tf_op jit(solution)/shard_map/ppermute | solution.py:499
  6.8 0.0 collective-permute-start.9
  6.8 3.7 %collective-permute-done.1.refs_5_ = f32[392,128]{1,0:T(8,128)S(1)} collective-permute-done((f32[392,128]{1,0:T(8,128)S(1)}, f32[392,128]{1,0:T(8,128)S(1)}, u32[]{:S(2)}, u32[]{:S(2)}) %collective-permute-start.1) | collective-permute-done | bytes 200736 | tf_op jit(solution)/shard_map/ppermute | solution.py:484
  10.5 2.0 %collective-permute-start.2 = (f32[392,128]{1,0:T(8,128)S(1)}, f32[392,128]{1,0:T(8,128)S(1)}, u32[]{:S(2)}, u32[]{:S(2)}) collective-permute-start(f32[392,128]{1,0:T(8,128)S(1)} %collective-permute-done.1.refs_5_), channel_id=1, source_target_pairs={{0,4},{4,8},{8,12},{12,14},{14,10},{10,6},{6,2},{2,0},{1,5},{5,9},... | collective-permute-start | bytes 602120 | tf_op jit(solution)/shard_map/ppermute | solution.py:484
  12.5 0.0 collective-permute-done.5.refs_8_
  12.6 0.0 collective-permute-start.6
  12.6 0.0 collective-permute-done.twin_ref
  12.6 2.1 %shard_map.65 = (bf16[40,128,256]{2,1,0:T(8,128)(2,1)S(1)}, f32[40,1,128]{2,1,0:T(1,128)S(1)}, s32[256]{0:T(256)S(1)}) custom-call(s32[32]{0:T(128)} %perm_ref.1, s32[1,1,16]{2,1,0:T(1,128)} %target_ref.1, f32[2568,128]{1,0:T(8,128)S(1)} %get-tuple-element.22.own_ref, f32[2568,128]{1,0:T(8,128)S(1)} %collective-permute-done.twin_ref), custom_call_target="tpu_custom_call" | custom-call | bytes 7400000 | tf_op jit(solution)/shard_map/pallas_call | solution.py:278
  14.6 0.2 collective-permute-done.10.refs_6_
  14.8 2.0 %collective-permute-done.9.refs_7_ = f32[392,128]{1,0:T(8,128)S(1)} collective-permute-done((f32[392,128]{1,0:T(8,128)S(1)}, f32[392,128]{1,0:T(8,128)S(1)}, u32[]{:S(2)}, u32[]{:S(2)}) %collective-permute-start.9) | collective-permute-done | bytes 200736 | tf_op jit(solution)/shard_map/ppermute | solution.py:498
  16.9 0.0 collective-permute-start.11
  16.9 2.0 %collective-permute-start.12 = (f32[392,128]{1,0:T(8,128)S(1)}, f32[392,128]{1,0:T(8,128)S(1)}, u32[]{:S(2)}, u32[]{:S(2)}) collective-permute-start(f32[392,128]{1,0:T(8,128)S(1)} %collective-permute-done.10.refs_6_), channel_id=1, source_target_pairs={{0,4},{4,8},{8,12},{12,14},{14,10},{10,6},{6,2},{2,0},{1,5},{5,9},... | collective-permute-start | bytes 602120 | tf_op jit(solution)/shard_map/ppermute | solution.py:499
  18.9 0.2 collective-permute-done.2.refs_3_
  19.1 2.0 %collective-permute-start.3 = (f32[392,128]{1,0:T(8,128)S(1)}, f32[392,128]{1,0:T(8,128)S(1)}, u32[]{:S(2)}, u32[]{:S(2)}) collective-permute-start(f32[392,128]{1,0:T(8,128)S(1)} %collective-permute-done.2.refs_3_), channel_id=1, source_target_pairs={{0,4},{4,8},{8,12},{12,14},{14,10},{10,6},{6,2},{2,0},{1,5},{5,9},... | collective-permute-start | bytes 602120 | tf_op jit(solution)/shard_map/ppermute | solution.py:484
  21.1 0.0 collective-permute-done.6.refs_6_
  21.2 0.0 collective-permute-start.7
  21.2 3.0 %shard_map.66.refs_7_ = f32[16,128,128]{2,1,0:T(8,128)S(1)} custom-call(s32[256]{0:T(256)S(1)} %get-tuple-element.23.refs_0_, bf16[40,128,256]{2,1,0:T(8,128)(2,1)S(1)} %get-tuple-element.24.refs_1_, f32[40,1,128]{2,1,0:T(1,128)S(1)} %get-tuple-element.25.refs_2_, f32[392,128]{1,0:T(8,128)S(1)} %get-tuple-element.26.refs_3_, ...), custom_call_target="tpu_custom_call" | custom-call | bytes 7400000 | tf_op jit(solution)/shard_map/pallas_call | solution.py:422
  24.2 1.3 %collective-permute-done.11.refs_5_ = f32[392,128]{1,0:T(8,128)S(1)} collective-permute-done((f32[392,128]{1,0:T(8,128)S(1)}, f32[392,128]{1,0:T(8,128)S(1)}, u32[]{:S(2)}, u32[]{:S(2)}) %collective-permute-start.11) | collective-permute-done | bytes 200736 | tf_op jit(solution)/shard_map/ppermute | solution.py:498
  25.5 0.0 collective-permute-done.12.refs_4_
  25.5 1.6 %collective-permute-start.13 = (f32[392,128]{1,0:T(8,128)S(1)}, f32[392,128]{1,0:T(8,128)S(1)}, u32[]{:S(2)}, u32[]{:S(2)}) collective-permute-start(f32[392,128]{1,0:T(8,128)S(1)} %collective-permute-done.12.refs_4_), channel_id=1, source_target_pairs={{0,4},{4,8},{8,12},{12,14},{14,10},{10,6},{6,2},{2,0},{1,5},{5,9},... | collective-permute-start | bytes 602120 | tf_op jit(solution)/shard_map/ppermute | solution.py:499
  27.1 0.4 %collective-permute-start.14 = (f32[392,128]{1,0:T(8,128)S(1)}, f32[392,128]{1,0:T(8,128)S(1)}, u32[]{:S(2)}, u32[]{:S(2)}) collective-permute-start(f32[392,128]{1,0:T(8,128)S(1)} %collective-permute-done.11.refs_5_), channel_id=1, source_target_pairs={{4,0},{8,4},{12,8},{14,12},{10,14},{6,10},{2,6},{0,2},{5,1},{9,5},... | collective-permute-start | bytes 602120 | tf_op jit(solution)/shard_map/ppermute | solution.py:498
  27.5 0.8 %collective-permute-done.3.refs_3_ = f32[392,128]{1,0:T(8,128)S(1)} collective-permute-done((f32[392,128]{1,0:T(8,128)S(1)}, f32[392,128]{1,0:T(8,128)S(1)}, u32[]{:S(2)}, u32[]{:S(2)}) %collective-permute-start.3) | collective-permute-done | bytes 200736 | tf_op jit(solution)/shard_map/ppermute | solution.py:484
  28.3 2.0 %collective-permute-start.4 = (f32[392,128]{1,0:T(8,128)S(1)}, f32[392,128]{1,0:T(8,128)S(1)}, u32[]{:S(2)}, u32[]{:S(2)}) collective-permute-start(f32[392,128]{1,0:T(8,128)S(1)} %collective-permute-done.3.refs_3_), channel_id=1, source_target_pairs={{0,4},{4,8},{8,12},{12,14},{14,10},{10,6},{6,2},{2,0},{1,5},{5,9},... | collective-permute-start | bytes 602120 | tf_op jit(solution)/shard_map/ppermute | solution.py:484
  30.3 0.0 collective-permute-done.7.refs_6_
  30.3 0.8 %collective-permute-start.8 = (f32[392,128]{1,0:T(8,128)S(1)}, f32[392,128]{1,0:T(8,128)S(1)}, u32[]{:S(2)}, u32[]{:S(2)}) collective-permute-start(f32[392,128]{1,0:T(8,128)S(1)} %collective-permute-done.7.refs_6_), channel_id=1, source_target_pairs={{4,0},{8,4},{12,8},{14,12},{10,14},{6,10},{2,6},{0,2},{5,1},{9,5},... | collective-permute-start | bytes 602120 | tf_op jit(solution)/shard_map/ppermute | solution.py:485
  31.1 2.8 %shard_map.67 = (f32[16,128,128]{2,1,0:T(8,128)S(1)}, f32[16,128,128]{2,1,0:T(8,128)}) custom-call(s32[256]{0:T(256)S(1)} %get-tuple-element.23.refs_0_, bf16[40,128,256]{2,1,0:T(8,128)(2,1)S(1)} %get-tuple-element.24.refs_1_, f32[40,1,128]{2,1,0:T(1,128)S(1)} %get-tuple-element.25.refs_2_, ...), custom_call_target="tpu_custom_call", output_to_operand_aliasing={{0}: (7, {})} | custom-call | bytes 7400000 | tf_op jit(solution)/shard_map/pallas_call | solution.py:422
  33.9 0.0 collective-permute-done.13.refs_4_
  33.9 1.1 %collective-permute-done.14.refs_5_ = f32[392,128]{1,0:T(8,128)S(1)} collective-permute-done((f32[392,128]{1,0:T(8,128)S(1)}, f32[392,128]{1,0:T(8,128)S(1)}, u32[]{:S(2)}, u32[]{:S(2)}) %collective-permute-start.14) | collective-permute-done | bytes 200736 | tf_op jit(solution)/shard_map/ppermute | solution.py:498
  35.0 2.8 %shard_map.68 = (f32[16,128,128]{2,1,0:T(8,128)S(1)}, f32[16,128,128]{2,1,0:T(8,128)}) custom-call(s32[256]{0:T(256)S(1)} %get-tuple-element.23.refs_0_, bf16[40,128,256]{2,1,0:T(8,128)(2,1)S(1)} %get-tuple-element.24.refs_1_, f32[40,1,128]{2,1,0:T(1,128)S(1)} %get-tuple-element.25.refs_2_, ...), custom_call_target="tpu_custom_call", output_to_operand_aliasing={{0}: (7, {}), {1}: (8, {})} | custom-call | bytes 7400000 | tf_op jit(solution)/shard_map/pallas_call | solution.py:422
  37.8 0.0 collective-permute-done.4.refs_3_
  37.8 0.0 collective-permute-done.8.refs_4_
  37.8 2.1 %shard_map.69 = (f32[16,128,128]{2,1,0:T(8,128)S(1)}, f32[16,128,128]{2,1,0:T(8,128)}) custom-call(s32[256]{0:T(256)S(1)} %get-tuple-element.23.refs_0_, bf16[40,128,256]{2,1,0:T(8,128)(2,1)S(1)} %get-tuple-element.24.refs_1_, f32[40,1,128]{2,1,0:T(1,128)S(1)} %get-tuple-element.25.refs_2_, ...), custom_call_target="tpu_custom_call", output_to_operand_aliasing={{0}: (5, {}), {1}: (6, {})} | custom-call | bytes 7400000 | tf_op jit(solution)/shard_map/pallas_call | solution.py:422
Async XLA Ops:
  1.6 11.0 %collective-permute-start = (f32[2568,128]{1,0:T(8,128)S(1)}, f32[2568,128]{1,0:T(8,128)S(1)}, u32[]{:S(2)}, u32[]{:S(2)}) collective-permute-start(f32[2568,128]{1,0:T(8,128)S(1)} %get-tuple-element.22.own_ref), channel_id=1, source_target_pairs={{0,1},{1,0},{2,3},{3,2},{4,5},{5,4},{6,7},{7,6},{8,9},{9,8},{10,11... | collective-permute-start | bytes 3944456 | tf_op jit(solution)/shard_map/ppermute | solution.py:471
  2.1 8.4 %collective-permute-start.1 = (f32[392,128]{1,0:T(8,128)S(1)}, f32[392,128]{1,0:T(8,128)S(1)}, u32[]{:S(2)}, u32[]{:S(2)}) collective-permute-start(f32[392,128]{1,0:T(8,128)S(1)} %get-tuple-element.26.refs_3_), channel_id=1, source_target_pairs={{0,4},{4,8},{8,12},{12,14},{14,10},{10,6},{6,2},{2,0},{1,5},{5,9},... | collective-permute-start | bytes 602120 | tf_op jit(solution)/shard_map/ppermute | solution.py:484
  4.7 7.8 %collective-permute-start.5 = (f32[392,128]{1,0:T(8,128)S(1)}, f32[392,128]{1,0:T(8,128)S(1)}, u32[]{:S(2)}, u32[]{:S(2)}) collective-permute-start(f32[392,128]{1,0:T(8,128)S(1)} %get-tuple-element.27.refs_4_), channel_id=1, source_target_pairs={{4,0},{8,4},{12,8},{14,12},{10,14},{6,10},{2,6},{0,2},{5,1},{9,5},... | collective-permute-start | bytes 602120 | tf_op jit(solution)/shard_map/ppermute | solution.py:485
  4.8 10.1 %collective-permute-start.10 = (f32[392,128]{1,0:T(8,128)S(1)}, f32[392,128]{1,0:T(8,128)S(1)}, u32[]{:S(2)}, u32[]{:S(2)}) collective-permute-start(f32[392,128]{1,0:T(8,128)S(1)} %get-tuple-element.27.refs_4_), channel_id=1, source_target_pairs={{0,4},{4,8},{8,12},{12,14},{14,10},{10,6},{6,2},{2,0},{1,5},{5,9},... | collective-permute-start | bytes 602120 | tf_op jit(solution)/shard_map/ppermute | solution.py:499
  6.8 10.1 %collective-permute-start.9 = (f32[392,128]{1,0:T(8,128)S(1)}, f32[392,128]{1,0:T(8,128)S(1)}, u32[]{:S(2)}, u32[]{:S(2)}) collective-permute-start(f32[392,128]{1,0:T(8,128)S(1)} %get-tuple-element.26.refs_3_), channel_id=1, source_target_pairs={{4,0},{8,4},{12,8},{14,12},{10,14},{6,10},{2,6},{0,2},{5,1},{9,5},... | collective-permute-start | bytes 602120 | tf_op jit(solution)/shard_map/ppermute | solution.py:498
  10.5 8.6 %collective-permute-start.2 = (f32[392,128]{1,0:T(8,128)S(1)}, f32[392,128]{1,0:T(8,128)S(1)}, u32[]{:S(2)}, u32[]{:S(2)}) collective-permute-start(f32[392,128]{1,0:T(8,128)S(1)} %collective-permute-done.1.refs_5_), channel_id=1, source_target_pairs={{0,4},{4,8},{8,12},{12,14},{14,10},{10,6},{6,2},{2,0},{1,5},{5,9},... | collective-permute-start | bytes 602120 | tf_op jit(solution)/shard_map/ppermute | solution.py:484
  12.6 8.6 %collective-permute-start.6 = (f32[392,128]{1,0:T(8,128)S(1)}, f32[392,128]{1,0:T(8,128)S(1)}, u32[]{:S(2)}, u32[]{:S(2)}) collective-permute-start(f32[392,128]{1,0:T(8,128)S(1)} %collective-permute-done.5.refs_8_), channel_id=1, source_target_pairs={{4,0},{8,4},{12,8},{14,12},{10,14},{6,10},{2,6},{0,2},{5,1},{9,5},... | collective-permute-start | bytes 602120 | tf_op jit(solution)/shard_map/ppermute | solution.py:485
  16.9 8.6 %collective-permute-start.11 = (f32[392,128]{1,0:T(8,128)S(1)}, f32[392,128]{1,0:T(8,128)S(1)}, u32[]{:S(2)}, u32[]{:S(2)}) collective-permute-start(f32[392,128]{1,0:T(8,128)S(1)} %collective-permute-done.9.refs_7_), channel_id=1, source_target_pairs={{4,0},{8,4},{12,8},{14,12},{10,14},{6,10},{2,6},{0,2},{5,1},{9,5},... | collective-permute-start | bytes 602120 | tf_op jit(solution)/shard_map/ppermute | solution.py:498
  16.9 8.6 %collective-permute-start.12 = (f32[392,128]{1,0:T(8,128)S(1)}, f32[392,128]{1,0:T(8,128)S(1)}, u32[]{:S(2)}, u32[]{:S(2)}) collective-permute-start(f32[392,128]{1,0:T(8,128)S(1)} %collective-permute-done.10.refs_6_), channel_id=1, source_target_pairs={{0,4},{4,8},{8,12},{12,14},{14,10},{10,6},{6,2},{2,0},{1,5},{5,9},... | collective-permute-start | bytes 602120 | tf_op jit(solution)/shard_map/ppermute | solution.py:499
  19.1 9.1 %collective-permute-start.3 = (f32[392,128]{1,0:T(8,128)S(1)}, f32[392,128]{1,0:T(8,128)S(1)}, u32[]{:S(2)}, u32[]{:S(2)}) collective-permute-start(f32[392,128]{1,0:T(8,128)S(1)} %collective-permute-done.2.refs_3_), channel_id=1, source_target_pairs={{0,4},{4,8},{8,12},{12,14},{14,10},{10,6},{6,2},{2,0},{1,5},{5,9},... | collective-permute-start | bytes 602120 | tf_op jit(solution)/shard_map/ppermute | solution.py:484
  21.2 9.1 %collective-permute-start.7 = (f32[392,128]{1,0:T(8,128)S(1)}, f32[392,128]{1,0:T(8,128)S(1)}, u32[]{:S(2)}, u32[]{:S(2)}) collective-permute-start(f32[392,128]{1,0:T(8,128)S(1)} %collective-permute-done.6.refs_6_), channel_id=1, source_target_pairs={{4,0},{8,4},{12,8},{14,12},{10,14},{6,10},{2,6},{0,2},{5,1},{9,5},... | collective-permute-start | bytes 602120 | tf_op jit(solution)/shard_map/ppermute | solution.py:485
  25.5 8.4 %collective-permute-start.13 = (f32[392,128]{1,0:T(8,128)S(1)}, f32[392,128]{1,0:T(8,128)S(1)}, u32[]{:S(2)}, u32[]{:S(2)}) collective-permute-start(f32[392,128]{1,0:T(8,128)S(1)} %collective-permute-done.12.refs_4_), channel_id=1, source_target_pairs={{0,4},{4,8},{8,12},{12,14},{14,10},{10,6},{6,2},{2,0},{1,5},{5,9},... | collective-permute-start | bytes 602120 | tf_op jit(solution)/shard_map/ppermute | solution.py:499
  27.1 7.9 %collective-permute-start.14 = (f32[392,128]{1,0:T(8,128)S(1)}, f32[392,128]{1,0:T(8,128)S(1)}, u32[]{:S(2)}, u32[]{:S(2)}) collective-permute-start(f32[392,128]{1,0:T(8,128)S(1)} %collective-permute-done.11.refs_5_), channel_id=1, source_target_pairs={{4,0},{8,4},{12,8},{14,12},{10,14},{6,10},{2,6},{0,2},{5,1},{9,5},... | collective-permute-start | bytes 602120 | tf_op jit(solution)/shard_map/ppermute | solution.py:498
  28.3 9.5 %collective-permute-start.4 = (f32[392,128]{1,0:T(8,128)S(1)}, f32[392,128]{1,0:T(8,128)S(1)}, u32[]{:S(2)}, u32[]{:S(2)}) collective-permute-start(f32[392,128]{1,0:T(8,128)S(1)} %collective-permute-done.3.refs_3_), channel_id=1, source_target_pairs={{0,4},{4,8},{8,12},{12,14},{14,10},{10,6},{6,2},{2,0},{1,5},{5,9},... | collective-permute-start | bytes 602120 | tf_op jit(solution)/shard_map/ppermute | solution.py:484
  30.3 7.5 %collective-permute-start.8 = (f32[392,128]{1,0:T(8,128)S(1)}, f32[392,128]{1,0:T(8,128)S(1)}, u32[]{:S(2)}, u32[]{:S(2)}) collective-permute-start(f32[392,128]{1,0:T(8,128)S(1)} %collective-permute-done.7.refs_6_), channel_id=1, source_target_pairs={{4,0},{8,4},{12,8},{14,12},{10,14},{6,10},{2,6},{0,2},{5,1},{9,5},... | collective-permute-start | bytes 602120 | tf_op jit(solution)/shard_map/ppermute | solution.py:485

commit v3 on v2

--- a/solution.py
+++ b/solution.py
@@ -155,151 +155,143 @@
     return copies
 
 
-def pack_kernel(lead, index_ref, places_ref, blocks_ref, ks_ref, lead_ref, rest_ref, ks_out_ref, index, places, sems):
+def write_labels(ref, rows, numbers):
+    shape = (ref.shape[0] - rows, ref.shape[1])
+    line = lax.broadcasted_iota(jnp.int32, shape, 0)
+    lane = lax.broadcasted_iota(jnp.int32, shape, 1)
+    labels = jnp.zeros(shape, jnp.int32)
+    for (x, y), number in numbers:
+        labels = jnp.where((line == x) & (lane == y), number, labels)
+    ref[pl.ds(rows, shape[0]), :] = labels.astype(jnp.float32)
+
+
+def pack_kernel(lead, index_ref, blocks_ref, lead_ref, rest_ref, index, sems):
     slots = index.shape[3]
-    width = lead_ref.shape[1]
     lead_rows = blocks_ref.shape[0] // slots * lead
     rest_rows = blocks_ref.shape[0] - lead_rows
-    ks_rows = ks_ref.shape[0]
     copies = start_all(
         [
             (index_ref, index),
-            (places_ref, places),
             (blocks_ref.at[pl.ds(0, lead_rows)], lead_ref.at[pl.ds(0, lead_rows)]),
             (blocks_ref.at[pl.ds(lead_rows, rest_rows)], rest_ref.at[pl.ds(0, rest_rows)]),
-            (ks_ref, ks_out_ref.at[pl.ds(0, ks_rows)]),
         ],
         sems,
     )
-
-    def label_rows(ref, rows, numbers):
-        shape = (ref.shape[0] - rows, width)
-        line = lax.broadcasted_iota(jnp.int32, shape, 0)
-        lane = lax.broadcasted_iota(jnp.int32, shape, 1)
-        labels = jnp.zeros(shape, jnp.int32)
-        for (x, y), number in numbers:
-            labels = jnp.where((line == x) & (lane == y), number, labels)
-        ref[pl.ds(rows, shape[0]), :] = labels.astype(jnp.float32)
-
     copies[0].wait()
-    copies[1].wait()
     for ref, rows, first, count in ((lead_ref, lead_rows, 0, lead), (rest_ref, rest_rows, lead, slots - lead)):
-        label_rows(
+        write_labels(
             ref,
             rows,
             [((n, field), index[0, 0, field, first + n]) for n in range(count) for field in range(2)],
         )
-    _, stops, present = places.shape
-    label_rows(
-        ks_out_ref, ks_rows, [((x, y), places[0, x, y]) for x in range(stops) for y in range(present)]
-    )
-    for copy in copies[2:]:
+    for copy in copies[1:]:
         copy.wait()
 
 
-def pack(blocks, index, ks, places, lead):
+def pack(blocks, index, lead):
     slots = index.shape[3]
     rows, width = blocks.shape
-    ks_rows = ks.shape[0]
     lead_rows = rows // slots * lead
     return pl.pallas_call(
         functools.partial(pack_kernel, lead),
         out_shape=(
             pltpu.VMEM((lead_rows + -(-lead // 8) * 8, width), jnp.float32),
             pltpu.VMEM((rows - lead_rows + -(-(slots - lead) // 8) * 8, width), jnp.float32),
-            pltpu.VMEM((ks_rows + -(-places.shape[1] // 8) * 8, width), jnp.float32),
         ),
-        in_specs=[HBM_SPEC] * 4,
-        out_specs=(VMEM_SPEC,) * 3,
-        scratch_shapes=[
-            pltpu.SMEM(index.shape, jnp.int32),
-            pltpu.SMEM(places.shape, jnp.int32),
-            pltpu.SemaphoreType.DMA((5,)),
-        ],
+        in_specs=[HBM_SPEC] * 2,
+        out_specs=(VMEM_SPEC,) * 2,
+        scratch_shapes=[pltpu.SMEM(index.shape, jnp.int32), pltpu.SemaphoreType.DMA((3,))],
         compiler_params=GRANT,
         cost_estimate=small_cost(1),
-    )(*map(in_hbm, (index, places, blocks, ks)))
-
-
-def window_kernel(
-    half_cols, present, perm_ref, target_ref, own_ref, twin_ref, parts_ref, norms_ref, table_ref,
-    perm, targets, own_place, twin_place, table, sems, out_sem,
-):
-    block_size = own_ref.shape[1]
-    count = parts_ref.shape[0] // 2
-    half_stops = count // present
-    ks_rows = count * block_size
+    )(in_hbm(index), in_hbm(blocks))
+
+
+def lines_of(entries, lanes):
+    return -(-entries * BR // lanes)
+
+
+def window_kernel(half_cols, *refs):
+    hbm_refs, twin_ref = refs[:5], refs[5]
+    parts_ref, norms_ref, table_ref = refs[6:9]
+    perm, own_place, twin_place, targets, own = refs[9:14]
+    stop_at, table, sems, out_sem = refs[14:]
+    lanes = table.shape[1]
+    column_line = lines_of(perm.shape[0], lanes)
+    row, row_count = lax.axis_index("row"), lax.axis_size("row")
+    count = own.shape[0]
+    _, half_stops, present = own_place.shape
     col = lax.axis_index("col")
-    ks_cells = 2 * half_stops * BR * BR
-    target_cells = BR * half_cols
-    place_rows = pl.ds(ks_rows, own_ref.shape[0] - ks_rows)
-    copies = start_all(
-        [
-            (perm_ref, perm),
-            (target_ref, targets),
-            (own_ref.at[place_rows], own_place),
-            (twin_ref.at[place_rows], twin_place),
-        ],
-        sems,
-    )
-    for i in range(ks_cells + target_cells):
-        table[i] = -1
-    for copy in copies:
+    copies = start_all(list(zip(hbm_refs, refs[9:14])), sems)
+
+    def split_half(half, ref):
+        def one(q, _):
+            block = ref[q]
+            parts_ref[half * count + q] = jnp.concatenate(split_bf16(block), axis=1)
+            norms_ref[half * count + q] = jnp.broadcast_to(norm_of(block), norms_ref.shape[1:])
+
+        lax.fori_loop(0, count, one, None, unroll=4)
+
+    split_half(1, twin_ref)
+    for i in range(stop_at.shape[0]):
+        stop_at[i] = -1
+    for cell in range(half_cols * BR):
+        table[column_line + cell // lanes, cell % lanes] = -1.0
+    for copy in copies[:4]:
         copy.wait()
-    for i in range(perm.shape[0]):
-        table[ks_cells + target_cells + i] = perm[i]
-    for t in range(targets.shape[2]):
-        table[ks_cells + targets[0, 0, t]] = t
     for local in range(half_stops):
         own_base = (col * half_stops + local) * BR * BR
         twin_base = ((1 - col) * half_stops + local) * BR * BR
         for q in range(present):
-            table[own_base + own_place[local, q].astype(jnp.int32)] = local * present + q
-            table[twin_base + twin_place[local, q].astype(jnp.int32)] = (half_stops + local) * present + q
+            stop_at[own_base + own_place[0, local, q]] = local * present + q
+            stop_at[twin_base + twin_place[0, local, q]] = (half_stops + local) * present + q
+    for t in range(targets.shape[2]):
+        place = targets[0, 0, t]
+        cell = lax.rem(place, half_cols) * BR + lax.div(place, half_cols)
+        table[column_line + lax.div(cell, lanes), lax.rem(cell, lanes)] = jnp.float32(t)
+    for block_row in range(perm.shape[0]):
+        behind = lax.div(perm[block_row], BR) - row
+        stop = jnp.where(behind < 0, behind + row_count, behind)
+        place = jnp.minimum(stop, 2 * half_stops - 1) * BR * BR + lax.rem(perm[block_row], BR)
+        for i in range(BR):
+            cell = block_row * BR + i
+            slot = jnp.where(stop < 2 * half_stops, stop_at[place + i * BR], -1)
+            table[cell // lanes, cell % lanes] = slot.astype(jnp.float32)
     publish = pltpu.make_async_copy(table, table_ref, out_sem)
     publish.start()
-    for half, ref in enumerate((own_ref, twin_ref)):
-
-        def one(q, _, half=half, ref=ref):
-            block = ref[pl.ds(pl.multiple_of(q * block_size, block_size), block_size), :]
-            parts_ref[half * count + q] = jnp.concatenate(split_bf16(block), axis=1)
-            norms_ref[half * count + q] = jnp.broadcast_to(norm_of(block), norms_ref.shape[1:])
-
-        lax.fori_loop(0, count, one, None, unroll=4)
+    copies[4].wait()
+    split_half(0, own)
     publish.wait()
 
 
-def prepare_window(row_perm, targets, own, twin, half_cols, half_stops, present):
-    rows, block_size = own.shape
-    count = half_stops * present
-    place_rows = rows - count * block_size
-    cells = 2 * half_stops * BR * BR + BR * half_cols + row_perm.shape[0]
-    cells = -(-cells // 128) * 128
+def prepare_window(row_perm, own_places, twin_places, targets, own, twin, half_cols):
+    count, block_size, _ = own.shape
+    lines = lines_of(row_perm.shape[0], block_size) + lines_of(half_cols, block_size)
+    lines = -(-lines // 8) * 8
+    held = [row_perm, own_places, twin_places, targets]
     return pl.pallas_call(
-        functools.partial(window_kernel, half_cols, present),
+        functools.partial(window_kernel, half_cols),
         out_shape=(
             pltpu.VMEM((2 * count, block_size, 2 * block_size), jnp.bfloat16),
             pltpu.VMEM((2 * count, 1, block_size), jnp.float32),
-            pltpu.VMEM((cells,), jnp.int32),
+            pltpu.VMEM((lines, block_size), jnp.float32),
         ),
-        in_specs=[HBM_SPEC] * 2 + [VMEM_SPEC] * 2,
+        in_specs=[HBM_SPEC] * 5 + [VMEM_SPEC],
         out_specs=(VMEM_SPEC,) * 3,
         scratch_shapes=[
-            pltpu.SMEM(row_perm.shape, jnp.int32),
-            pltpu.SMEM(targets.shape, jnp.int32),
-            pltpu.SMEM((place_rows, block_size), jnp.float32),
-            pltpu.SMEM((place_rows, block_size), jnp.float32),
-            pltpu.SMEM((cells,), jnp.int32),
-            pltpu.SemaphoreType.DMA((4,)),
+            *(pltpu.SMEM(x.shape, jnp.int32) for x in held),
+            pltpu.VMEM(own.shape, jnp.float32),
+            pltpu.SMEM((2 * own_places.shape[1] * BR * BR,), jnp.int32),
+            pltpu.SMEM((lines, block_size), jnp.float32),
+            pltpu.SemaphoreType.DMA((5,)),
             pltpu.SemaphoreType.DMA,
         ],
         compiler_params=GRANT,
         cost_estimate=small_cost(2),
-    )(in_hbm(row_perm), in_hbm(targets), in_vmem(own), in_vmem(twin))
+    )(*map(in_hbm, held), in_hbm(own), in_vmem(twin))
 
 
 def product_kernel(config, *refs):
-    row_count, stop_count, half_cols, limit, pieces, first, final = config
+    block_rows, half_cols, limit, pieces, first, final = config
     table_ref, parts_ref, norms_ref = refs[:3]
     chunk_refs = refs[3 : 3 + len(pieces)]
     rest = refs[3 + len(pieces) + (not first) + (final == "touched") :]
@@ -307,61 +299,67 @@
     if final:
         out_ref = rest[1]
         rest = rest[1:]
-    table, label, list_t, list_q, list_b, touched, held, sems, out_sems = rest[1:]
+    listed, touched, held, out_sems = rest[1:]
     block_size = c_ref.shape[-1]
-    row = lax.axis_index("row")
-    ks_cells = stop_count * BR * BR
-    perm_at = ks_cells + BR * half_cols
-
-    moves = [(table_ref, table)]
-    for number, blocks in enumerate(pieces):
-        rows = pl.ds(blocks * block_size, label.shape[1])
-        moves.append((chunk_refs[number].at[rows], label.at[number]))
-    copies = start_all(moves, sems)
+    slot_bits = (parts_ref.shape[0] - 1).bit_length()
+    code_bits = slot_bits + c_ref.shape[0].bit_length()
+    slot_mask, none = (1 << slot_bits) - 1, (1 << code_bits) - 1
+    per_word = 2 if 2 * code_bits < 32 else 1
+
+    def target_of(entry):
+        return (entry & none) >> slot_bits
+
     if first:
         c_ref[...] = jnp.zeros_like(c_ref)
-    for copy in copies:
-        copy.wait()
-
-    found = (jnp.int32(0), jnp.int32(0))
-    for number, blocks in enumerate(pieces):
-
-        def look(b, found, number=number, chunk_ref=chunk_refs[number]):
-            pairs, kept = found
-            position = table[perm_at + label[number, b, 0].astype(jnp.int32)]
-            column = label[number, b, 1].astype(jnp.int32)
-            behind = lax.div(position, BR) - row
-            stop = jnp.where(behind < 0, behind + row_count, behind)
-            in_window = stop < stop_count
-            place = jnp.minimum(stop, stop_count - 1) * BR * BR + lax.rem(position, BR)
+
+    lane = lax.broadcasted_iota(jnp.int32, (1, block_size), 1).astype(jnp.float32)
+    slot_lines = lines_of(block_rows, block_size)
+    target_lines = lines_of(half_cols, block_size)
+
+    def look_up(cells, first_line, lines):
+        found = 0.0
+        for n in range(lines):
+            line = table_ref[pl.ds(first_line + n, 1), :]
+            hit = cells - float(n * block_size) == lane
+            found += jnp.sum(jnp.where(hit, line, 0.0), axis=1, keepdims=True)
+        return found
+
+    pairs, kept = jnp.int32(0), jnp.int32(0)
+    words = []
+    for chunk_ref, blocks in zip(chunk_refs, pieces):
+        labels = chunk_ref[pl.ds(blocks * block_size, chunk_ref.shape[0] - blocks * block_size), :]
+        for i in range(BR):
+            slot = look_up(labels[:, 0:1] * float(BR) + float(i), 0, slot_lines)
+            target = look_up(labels[:, 1:2] * float(BR) + float(i), slot_lines, target_lines)
+            present = (slot >= 0.0) & (target >= 0.0)
+            code = jnp.where(present, target * float(1 << slot_bits) + slot, float(none)).astype(jnp.int32)
+            if i % per_word:
+                words[-1] = words[-1] + (code << (code_bits * (i % per_word)))
+            else:
+                words.append(code)
+    read = [
+        [words[number * (BR // per_word) + w][b, 0] for w in range(BR // per_word)]
+        for number, blocks in enumerate(pieces)
+        for b in range(blocks)
+    ]
+    for number, (chunk_ref, blocks) in enumerate(zip(chunk_refs, pieces)):
+        for b in range(blocks):
             before = pairs
-            for i in range(BR):
-                target = table[ks_cells + i * half_cols + column]
-                ks = table[place + i * BR]
-                list_t[pairs] = target
-                list_q[pairs] = ks
-                list_b[pairs] = kept
-                hit = (target >= 0) & (ks >= 0) & in_window
-                pairs = pairs + hit.astype(jnp.int32)
-            some = pairs > before
-
-            @pl.when(some)
-            def _():
-                held[kept] = chunk_ref[pl.ds(pl.multiple_of(b * block_size, block_size), block_size), :]
-
-            return pairs, kept + some.astype(jnp.int32)
-
-        found = lax.fori_loop(0, blocks, look, found)
-    pairs, _ = found
+            for word in read.pop(0):
+                for n in range(per_word):
+                    code = (word >> (code_bits * n)) & none
+                    listed[pairs] = code + (kept << code_bits)
+                    pairs = pairs + (code != none).astype(jnp.int32)
+            held[kept] = chunk_ref[pl.ds(b * block_size, block_size), :]
+            kept = kept + (pairs > before).astype(jnp.int32)
     for u in range(UNROLL):
-        list_t[pairs + u] = 0
-        list_q[pairs + u] = 0
-        list_b[pairs + u] = 0
+        listed[pairs + u] = 0
 
     def multiply(step, _):
         for u in range(UNROLL):
             at = step * UNROLL + u
-            target, ks, slot = list_t[at], list_q[at], list_b[at]
+            entry = listed[at]
+            ks, target, slot = entry & slot_mask, target_of(entry), entry >> code_bits
             density = held[slot]
             bound = jnp.where(at < pairs, limit, jnp.inf)
             keep = norms_ref[ks] * norm_of(density) >= bound
@@ -388,7 +386,7 @@
             touched[t] = 0
 
         def touch(p, _):
-            touched[list_t[p]] = 1
+            touched[target_of(listed[p])] = 1
 
         lax.fori_loop(0, pairs, touch, None)
         for begin in (True, False):
@@ -400,12 +398,13 @@
                     (copy.start if begin else copy.wait)()
 
 
-def add_products(sizes, window, accumulated, pieces, chunks, shape, final=None, written=None):
+def add_products(sizes, window, accumulated, group, shape, final=None, written=None):
     block_size = shape[-1]
     limit = FILTER * block_size * math.sqrt(block_size)
     first = accumulated is None
+    pieces = [count for count, _ in group]
+    chunks = [chunk for _, chunk in group]
     blocks = sum(pieces)
-    label_rows = -(-max(pieces) // 8) * 8
     parts, norms, table = window
     operands = [*map(in_vmem, (table, parts, norms, *chunks))]
     aliases = {}
@@ -425,14 +424,9 @@
         in_specs=in_specs,
         out_specs=[VMEM_SPEC, HBM_SPEC][:outs],
         scratch_shapes=[
-            pltpu.SMEM(table.shape, jnp.int32),
-            pltpu.SMEM((len(pieces), label_rows, block_size), jnp.float32),
-            pltpu.SMEM((longest,), jnp.int32),
-            pltpu.SMEM((longest,), jnp.int32),
             pltpu.SMEM((longest,), jnp.int32),
             pltpu.SMEM((shape[0],), jnp.int32),
             pltpu.VMEM((blocks, block_size, block_size), jnp.float32),
-            pltpu.SemaphoreType.DMA((1 + len(pieces),)),
             pltpu.SemaphoreType.DMA((shape[0],)),
         ],
         input_output_aliases=aliases,
@@ -455,55 +449,41 @@
     forward = [(order[i], order[(i + 1) % row_count]) for i in range(row_count)]
     backward = [(b, a) for a, b in forward]
     twins = [(0, 1), (1, 0)]
-    stop_count = 2 * ks_blocks.shape[1]
     shape = (c_index.shape[-1], block_size, block_size)
-    sizes = (row_count, stop_count, half_cols)
-
-    _, half_stops, present = ks_index.shape
-    a_fwd, b_fwd, ks_own = pack(
-        d_blocks.reshape(-1, block_size),
-        jnp.swapaxes(d_index, 2, 3),
-        ks_blocks.reshape(-1, block_size),
-        ks_index,
-        lead,
-    )
+    sizes = (row_perm.shape[0], half_cols)
+
+    a_fwd, b_fwd = pack(d_blocks.reshape(-1, block_size), jnp.swapaxes(d_index, 2, 3), lead)
     a_bwd, b_bwd = a_fwd, b_fwd
+    ks_own = ks_blocks.reshape(-1, block_size, block_size)
     ks_twin = lax.ppermute(ks_own, "col", twins)
-    window = prepare_window(row_perm, c_index, ks_own, ks_twin, half_cols, half_stops, present)
-    pieces, chunks = [], []
-    accumulated = None
-
-    def arrived(first, second):
-        pieces.extend([lead, slots - lead])
-        chunks.extend([first, second])
-
-    arrived(a_fwd, b_fwd)
-    written = []
+    places_twin = lax.ppermute(ks_index, "col", twins)
+    window = prepare_window(row_perm, ks_index, places_twin, c_index, ks_own, ks_twin, half_cols)
+    accumulated, written = None, []
+    group = [(lead, a_fwd), (slots - lead, b_bwd)]
     half = row_count // 2
     for step in range(1, half + 1):
         a_fwd = lax.ppermute(a_fwd, "row", forward)
         b_bwd = lax.ppermute(b_bwd, "row", backward)
         if step > 1:
-            if step > 2:
-                (accumulated,) = tied((accumulated,), ready)
             final = {half - 1: "whole", half: "touched"}.get(step)
-            accumulated, *written = add_products(
-                sizes, window, accumulated, pieces, chunks, shape, final, *written
-            )
-            pieces, chunks = [], []
+            if step == half - 1:
+                (accumulated,) = tied((accumulated,), a_fwd)
+                group += [(lead, a_fwd), (slots - lead, b_bwd)]
+            accumulated, *written = add_products(sizes, window, accumulated, group, shape, final, *written)
+            group = []
         if step < half:
             if step > 1:
-                a_bwd, b_fwd = tied((a_bwd, b_fwd), window[1] if step == 2 else before)
+                token = window[1] if step == 2 else before
+                (a_bwd,) = tied((a_bwd,), token)
+                (b_fwd,) = tied((b_fwd,), token)
             before = accumulated
             a_bwd = lax.ppermute(a_bwd, "row", backward)
             b_fwd = lax.ppermute(b_fwd, "row", forward)
-            arrived(a_fwd, b_fwd)
-            arrived(a_bwd, b_bwd)
-            ready = a_fwd
-    arrived(a_fwd, b_bwd)
-    _, total = add_products(
-        sizes, window, accumulated, pieces, chunks, shape, "touched", written[0]
-    )
+            if step < half - 1:
+                group += [(lead, a_fwd), (slots - lead, b_bwd)]
+            group += [(lead, a_bwd), (slots - lead, b_fwd)]
+    group = [(lead, a_fwd), (slots - lead, b_bwd)]
+    _, total = add_products(sizes, window, accumulated, group, shape, "touched", *written)
     return total.reshape(c_index.shape + (block_size, block_size))
 
 

time: 40 us -> 38.8 us (0.970)
  Pallas kernels: 14.3 us -> 12.4 us
  waiting for transfers between devices: 9.4 us -> 11 us
  starting transfers between devices: 16.1 us -> 15.2 us
    ppermute x0 -> x1, waiting for transfers between devices: none -> 1.35 us  [ring_plan(): places_twin = lax.ppermute(ks_index, 'col', twins)]
    pallas_call x4, Pallas kernels: 10.7 us -> 9.42 us  [add_products(): pl.pallas_call(functools.partial(product_kernel, (*sizes, limit, pieces,...]
    ppermute x3, waiting for transfers between devices: 4.41 us -> 3.27 us  [ring_plan(): a_bwd = lax.ppermute(a_bwd, 'row', backward)]
    ppermute x4, waiting for transfers between devices: 0.09 us -> 0.91 us  [ring_plan(): b_bwd = lax.ppermute(b_bwd, 'row', backward)]
    ppermute x4, starting transfers between devices: 0.83 us -> 0.02 us  [ring_plan(): b_bwd = lax.ppermute(b_bwd, 'row', backward)]
    pallas_call x1, Pallas kernels: 1.57 us -> 1.05 us  [pack(): pl.pallas_call(functools.partial(pack_kernel, lead), out_shape=(pltpu.VME...]
  transfers between devices with their start and end apart: 15 -> 16, of which waited for: 7 -> 9; matrix products, arithmetic and copies ran while one was open for 0% -> 0% of each run, Pallas kernels for 27% -> 28%
where the time goes in v3:
time: 38.8 us; the launch traced here: 38.6 us
  starting transfers between devices  15.2 us (39%)
  Pallas kernels  12.4 us (32%)
  waiting for transfers between devices  11 us (28%)
    pallas_call x4, Pallas kernels, add_products(): pl.pallas_call(functools.partial(product_kernel, (*sizes, limit, pieces,...  9.42 us
    ppermute x4, starting transfers between devices, ring_plan(): a_fwd = lax.ppermute(a_fwd, 'row', forward)  8.63 us
    ppermute x3, starting transfers between devices, ring_plan(): b_fwd = lax.ppermute(b_fwd, 'row', forward)  5.59 us
    ppermute x4, waiting for transfers between devices, ring_plan(): a_fwd = lax.ppermute(a_fwd, 'row', forward)  4.89 us
    ppermute x3, waiting for transfers between devices, ring_plan(): a_bwd = lax.ppermute(a_bwd, 'row', backward)  3.27 us
    pallas_call x1, Pallas kernels, prepare_window(): pl.pallas_call(functools.partial(window_kernel, half_cols), out_shape=(pl...  1.97 us
    ppermute x1, waiting for transfers between devices, ring_plan(): places_twin = lax.ppermute(ks_index, 'col', twins)  1.35 us
    pallas_call x1, Pallas kernels, pack(): pl.pallas_call(functools.partial(pack_kernel, lead), out_shape=(pltpu.VME...  1.05 us
  transfers between devices with their start and end apart: 16, of which 9 were waited for; matrix products, arithmetic and copies ran while one was open for 0% of the time, Pallas kernels for 28%

profile of v3, /device:TPU:0, one launch (start us, length us, event | category | flops | bytes accessed | tf_op | source)
XLA Modules:
  0.0 38.6 jit_solution(13538585994144234771)
XLA Ops:
  0.0 0.5 %collective-permute-start.1 = (f32[20,128,128]{2,1,0:T(8,128)}, f32[20,128,128]{2,1,0:T(8,128)S(1)}, u32[]{:S(2)}, u32[]{:S(2)}) collective-permute-start(f32[20,128,128]{2,1,0:T(8,128)} %bitcast.4), channel_id=1, source_target_pairs={{0,1},{1,0},{2,3},{3,2},{4,5},{5,4},{6,7},{7,6},{8,9},{9,8},{10,11... | collective-permute-start | bytes 3932168 | tf_op jit(solution)/shard_map/ppermute | solution.py:458
  0.5 1.0 %shard_map.65 = (f32[392,128]{1,0:T(8,128)S(1)}, f32[392,128]{1,0:T(8,128)S(1)}) custom-call(s32[1,1,2,6]{3,2,1,0:T(2,128)} %bitcast.7, f32[768,128]{1,0:T(8,128)} %bitcast.6), custom_call_target="tpu_custom_call" | custom-call | bytes 3700000 | tf_op jit(solution)/shard_map/pallas_call | solution.py:195
  1.5 2.6 %collective-permute-start.2 = (f32[392,128]{1,0:T(8,128)S(1)}, f32[392,128]{1,0:T(8,128)S(1)}, u32[]{:S(2)}, u32[]{:S(2)}) collective-permute-start(f32[392,128]{1,0:T(8,128)S(1)} %get-tuple-element.23.refs_3_), channel_id=1, source_target_pairs={{0,4},{4,8},{8,12},{12,14},{14,10},{10,6},{6,2},{2,0},{1,5},{5,9},... | collective-permute-start | bytes 602120 | tf_op jit(solution)/shard_map/ppermute | solution.py:465
  4.1 0.0 collective-permute-start.6
  4.1 2.0 %collective-permute-start.12 = (f32[392,128]{1,0:T(8,128)S(1)}, f32[392,128]{1,0:T(8,128)S(1)}, u32[]{:S(2)}, u32[]{:S(2)}) collective-permute-start(f32[392,128]{1,0:T(8,128)S(1)} %get-tuple-element.24.refs_4_), channel_id=1, source_target_pairs={{0,4},{4,8},{8,12},{12,14},{14,10},{10,6},{6,2},{2,0},{1,5},{5,9},... | collective-permute-start | bytes 602120 | tf_op jit(solution)/shard_map/ppermute | solution.py:481
  6.2 0.0 collective-permute-start
  6.2 1.3 %collective-permute-done.refs_2_ = s32[1,2,10]{2,1,0:T(2,128)S(1)} collective-permute-done((s32[1,2,10]{2,1,0:T(2,128)}, s32[1,2,10]{2,1,0:T(2,128)S(1)}, u32[]{:S(2)}, u32[]{:S(2)}) %collective-permute-start) | collective-permute-done | bytes 112 | tf_op jit(solution)/shard_map/ppermute | solution.py:459
  7.5 0.0 copy-start
  7.5 0.0 collective-permute-start.10
  7.5 2.4 %collective-permute-done.2.refs_5_ = f32[392,128]{1,0:T(8,128)S(1)} collective-permute-done((f32[392,128]{1,0:T(8,128)S(1)}, f32[392,128]{1,0:T(8,128)S(1)}, u32[]{:S(2)}, u32[]{:S(2)}) %collective-permute-start.2) | collective-permute-done | bytes 200736 | tf_op jit(solution)/shard_map/ppermute | solution.py:465
  9.9 2.0 %collective-permute-start.3 = (f32[392,128]{1,0:T(8,128)S(1)}, f32[392,128]{1,0:T(8,128)S(1)}, u32[]{:S(2)}, u32[]{:S(2)}) collective-permute-start(f32[392,128]{1,0:T(8,128)S(1)} %collective-permute-done.2.refs_5_), channel_id=1, source_target_pairs={{0,4},{4,8},{8,12},{12,14},{14,10},{10,6},{6,2},{2,0},{1,5},{5,9},... | collective-permute-start | bytes 602120 | tf_op jit(solution)/shard_map/ppermute | solution.py:465
  11.9 0.0 collective-permute-done.6.refs_6_
  12.0 0.0 collective-permute-start.7
  12.0 0.0 collective-permute-done.1.refs_5_
  12.0 0.0 copy-done
  12.0 2.0 %shard_map.64 = (bf16[40,128,256]{2,1,0:T(8,128)(2,1)S(1)}, f32[40,1,128]{2,1,0:T(1,128)S(1)}, f32[8,128]{1,0:T(8,128)S(1)}) custom-call(s32[32]{0:T(128)} %refs_0_.1, s32[1,2,10]{2,1,0:T(2,128)} %refs_1_.1, s32[1,2,10]{2,1,0:T(2,128)} %copy-done, s32[1,1,16]{2,1,0:T(1,128)} %refs_3_.1, f32[20,128,128]{2,1,0:T(8,128)} %bitcast.5, ...), custom_call_target="tpu_custom_call" | custom-call | bytes 7400000 | tf_op jit(solution)/shard_map/pallas_call | solution.py:271
  14.0 0.3 collective-permute-done.12.refs_8_
  14.2 2.0 %collective-permute-start.14 = (f32[392,128]{1,0:T(8,128)S(1)}, f32[392,128]{1,0:T(8,128)S(1)}, u32[]{:S(2)}, u32[]{:S(2)}) collective-permute-start(f32[392,128]{1,0:T(8,128)S(1)} %collective-permute-done.12.refs_8_), channel_id=1, source_target_pairs={{0,4},{4,8},{8,12},{12,14},{14,10},{10,6},{6,2},{2,0},{1,5},{5,9},... | collective-permute-start | bytes 602120 | tf_op jit(solution)/shard_map/ppermute | solution.py:481
  16.2 0.0 collective-permute-done.10.refs_7_
  16.3 0.0 collective-permute-start.11
  16.3 2.3 %collective-permute-done.3.refs_3_ = f32[392,128]{1,0:T(8,128)S(1)} collective-permute-done((f32[392,128]{1,0:T(8,128)S(1)}, f32[392,128]{1,0:T(8,128)S(1)}, u32[]{:S(2)}, u32[]{:S(2)}) %collective-permute-start.3) | collective-permute-done | bytes 200736 | tf_op jit(solution)/shard_map/ppermute | solution.py:465
  18.5 2.0 %collective-permute-start.4 = (f32[392,128]{1,0:T(8,128)S(1)}, f32[392,128]{1,0:T(8,128)S(1)}, u32[]{:S(2)}, u32[]{:S(2)}) collective-permute-start(f32[392,128]{1,0:T(8,128)S(1)} %collective-permute-done.3.refs_3_), channel_id=1, source_target_pairs={{0,4},{4,8},{8,12},{12,14},{14,10},{10,6},{6,2},{2,0},{1,5},{5,9},... | collective-permute-start | bytes 602120 | tf_op jit(solution)/shard_map/ppermute | solution.py:465
  20.5 0.0 collective-permute-done.7.refs_4_
  20.6 0.0 collective-permute-start.8
  20.6 2.6 %shard_map.66.refs_9_ = f32[16,128,128]{2,1,0:T(8,128)S(1)} custom-call(f32[8,128]{1,0:T(8,128)S(1)} %get-tuple-element.20.refs_0_, bf16[40,128,256]{2,1,0:T(8,128)(2,1)S(1)} %get-tuple-element.21.refs_1_, f32[40,1,128]{2,1,0:T(1,128)S(1)} %get-tuple-element.22.refs_2_, f32[392,128]{1,0:T(8,128)S(1)} %get-tuple-element.23.refs_3_, ...), custom_call_target="tpu_custom_call" | custom-call | bytes 7400000 | tf_op jit(solution)/shard_map/pallas_call | solution.py:421
  23.2 0.0 collective-permute-done.14.refs_6_
  23.2 1.7 %collective-permute-done.11.refs_5_ = f32[392,128]{1,0:T(8,128)S(1)} collective-permute-done((f32[392,128]{1,0:T(8,128)S(1)}, f32[392,128]{1,0:T(8,128)S(1)}, u32[]{:S(2)}, u32[]{:S(2)}) %collective-permute-start.11) | collective-permute-done | bytes 200736 | tf_op jit(solution)/shard_map/ppermute | solution.py:480
  24.9 1.6 %collective-permute-start.15 = (f32[392,128]{1,0:T(8,128)S(1)}, f32[392,128]{1,0:T(8,128)S(1)}, u32[]{:S(2)}, u32[]{:S(2)}) collective-permute-start(f32[392,128]{1,0:T(8,128)S(1)} %collective-permute-done.14.refs_6_), channel_id=1, source_target_pairs={{0,4},{4,8},{8,12},{12,14},{14,10},{10,6},{6,2},{2,0},{1,5},{5,9},... | collective-permute-start | bytes 602120 | tf_op jit(solution)/shard_map/ppermute | solution.py:481
  26.4 0.4 %collective-permute-start.13 = (f32[392,128]{1,0:T(8,128)S(1)}, f32[392,128]{1,0:T(8,128)S(1)}, u32[]{:S(2)}, u32[]{:S(2)}) collective-permute-start(f32[392,128]{1,0:T(8,128)S(1)} %collective-permute-done.11.refs_5_), channel_id=1, source_target_pairs={{4,0},{8,4},{12,8},{14,12},{10,14},{6,10},{2,6},{0,2},{5,1},{9,5},... | collective-permute-start | bytes 602120 | tf_op jit(solution)/shard_map/ppermute | solution.py:480
  26.9 0.2 collective-permute-done.4.refs_7_
  27.1 2.0 %collective-permute-start.5 = (f32[392,128]{1,0:T(8,128)S(1)}, f32[392,128]{1,0:T(8,128)S(1)}, u32[]{:S(2)}, u32[]{:S(2)}) collective-permute-start(f32[392,128]{1,0:T(8,128)S(1)} %collective-permute-done.4.refs_7_), channel_id=1, source_target_pairs={{0,4},{4,8},{8,12},{12,14},{14,10},{10,6},{6,2},{2,0},{1,5},{5,9},... | collective-permute-start | bytes 602120 | tf_op jit(solution)/shard_map/ppermute | solution.py:465
  29.1 0.0 collective-permute-done.8.refs_8_
  29.2 0.0 collective-permute-start.9
  29.2 3.4 %shard_map.67 = (f32[16,128,128]{2,1,0:T(8,128)S(1)}, f32[16,128,128]{2,1,0:T(8,128)}) custom-call(f32[8,128]{1,0:T(8,128)S(1)} %get-tuple-element.20.refs_0_, bf16[40,128,256]{2,1,0:T(8,128)(2,1)S(1)} %get-tuple-element.21.refs_1_, f32[40,1,128]{2,1,0:T(1,128)S(1)} %get-tuple-element.22.refs_2_, ...), custom_call_target="tpu_custom_call", output_to_operand_aliasing={{0}: (9, {})} | custom-call | bytes 7400000 | tf_op jit(solution)/shard_map/pallas_call | solution.py:421
  32.5 0.3 collective-permute-done.15.refs_4_
  32.8 1.6 %collective-permute-done.13.refs_3_ = f32[392,128]{1,0:T(8,128)S(1)} collective-permute-done((f32[392,128]{1,0:T(8,128)S(1)}, f32[392,128]{1,0:T(8,128)S(1)}, u32[]{:S(2)}, u32[]{:S(2)}) %collective-permute-start.13) | collective-permute-done | bytes 200736 | tf_op jit(solution)/shard_map/ppermute | solution.py:480
  34.4 1.9 %shard_map.68 = (f32[16,128,128]{2,1,0:T(8,128)S(1)}, f32[16,128,128]{2,1,0:T(8,128)}) custom-call(f32[8,128]{1,0:T(8,128)S(1)} %get-tuple-element.20.refs_0_, bf16[40,128,256]{2,1,0:T(8,128)(2,1)S(1)} %get-tuple-element.21.refs_1_, f32[40,1,128]{2,1,0:T(1,128)S(1)} %get-tuple-element.22.refs_2_, ...), custom_call_target="tpu_custom_call", output_to_operand_aliasing={{0}: (5, {}), {1}: (6, {})} | custom-call | bytes 7400000 | tf_op jit(solution)/shard_map/pallas_call | solution.py:421
  36.3 0.0 collective-permute-done.5.refs_3_
  36.3 0.8 %collective-permute-done.9.refs_4_ = f32[392,128]{1,0:T(8,128)S(1)} collective-permute-done((f32[392,128]{1,0:T(8,128)S(1)}, f32[392,128]{1,0:T(8,128)S(1)}, u32[]{:S(2)}, u32[]{:S(2)}) %collective-permute-start.9) | collective-permute-done | bytes 200736 | tf_op jit(solution)/shard_map/ppermute | solution.py:466
  37.1 1.6 %shard_map.69 = (f32[16,128,128]{2,1,0:T(8,128)S(1)}, f32[16,128,128]{2,1,0:T(8,128)}) custom-call(f32[8,128]{1,0:T(8,128)S(1)} %get-tuple-element.20.refs_0_, bf16[40,128,256]{2,1,0:T(8,128)(2,1)S(1)} %get-tuple-element.21.refs_1_, f32[40,1,128]{2,1,0:T(1,128)S(1)} %get-tuple-element.22.refs_2_, ...), custom_call_target="tpu_custom_call", output_to_operand_aliasing={{0}: (5, {}), {1}: (6, {})} | custom-call | bytes 7400000 | tf_op jit(solution)/shard_map/pallas_call | solution.py:421
Async XLA Ops:
  0.0 12.0 %collective-permute-start.1 = (f32[20,128,128]{2,1,0:T(8,128)}, f32[20,128,128]{2,1,0:T(8,128)S(1)}, u32[]{:S(2)}, u32[]{:S(2)}) collective-permute-start(f32[20,128,128]{2,1,0:T(8,128)} %bitcast.4), channel_id=1, source_target_pairs={{0,1},{1,0},{2,3},{3,2},{4,5},{5,4},{6,7},{7,6},{8,9},{9,8},{10,11... | collective-permute-start | bytes 3932168 | tf_op jit(solution)/shard_map/ppermute | solution.py:458
  1.5 8.4 %collective-permute-start.2 = (f32[392,128]{1,0:T(8,128)S(1)}, f32[392,128]{1,0:T(8,128)S(1)}, u32[]{:S(2)}, u32[]{:S(2)}) collective-permute-start(f32[392,128]{1,0:T(8,128)S(1)} %get-tuple-element.23.refs_3_), channel_id=1, source_target_pairs={{0,4},{4,8},{8,12},{12,14},{14,10},{10,6},{6,2},{2,0},{1,5},{5,9},... | collective-permute-start | bytes 602120 | tf_op jit(solution)/shard_map/ppermute | solution.py:465
  4.1 7.8 %collective-permute-start.6 = (f32[392,128]{1,0:T(8,128)S(1)}, f32[392,128]{1,0:T(8,128)S(1)}, u32[]{:S(2)}, u32[]{:S(2)}) collective-permute-start(f32[392,128]{1,0:T(8,128)S(1)} %get-tuple-element.24.refs_4_), channel_id=1, source_target_pairs={{4,0},{8,4},{12,8},{14,12},{10,14},{6,10},{2,6},{0,2},{5,1},{9,5},... | collective-permute-start | bytes 602120 | tf_op jit(solution)/shard_map/ppermute | solution.py:466
  4.1 10.1 %collective-permute-start.12 = (f32[392,128]{1,0:T(8,128)S(1)}, f32[392,128]{1,0:T(8,128)S(1)}, u32[]{:S(2)}, u32[]{:S(2)}) collective-permute-start(f32[392,128]{1,0:T(8,128)S(1)} %get-tuple-element.24.refs_4_), channel_id=1, source_target_pairs={{0,4},{4,8},{8,12},{12,14},{14,10},{10,6},{6,2},{2,0},{1,5},{5,9},... | collective-permute-start | bytes 602120 | tf_op jit(solution)/shard_map/ppermute | solution.py:481
  6.2 1.4 %collective-permute-start = (s32[1,2,10]{2,1,0:T(2,128)}, s32[1,2,10]{2,1,0:T(2,128)S(1)}, u32[]{:S(2)}, u32[]{:S(2)}) collective-permute-start(s32[1,2,10]{2,1,0:T(2,128)} %refs_1_.1), channel_id=1, source_target_pairs={{0,1},{1,0},{2,3},{3,2},{4,5},{5,4},{6,7},{7,6},{8,9},{9,8},{10,11... | collective-permute-start | bytes 248 | tf_op jit(solution)/shard_map/ppermute | solution.py:459
  7.5 4.5 %copy-start = (s32[1,2,10]{2,1,0:T(2,128)}, s32[1,2,10]{2,1,0:T(2,128)S(1)}, u32[]{:S(2)}) copy-start(s32[1,2,10]{2,1,0:T(2,128)S(1)} %collective-permute-done.refs_2_) | copy-start | bytes 244
  7.5 8.7 %collective-permute-start.10 = (f32[392,128]{1,0:T(8,128)S(1)}, f32[392,128]{1,0:T(8,128)S(1)}, u32[]{:S(2)}, u32[]{:S(2)}) collective-permute-start(f32[392,128]{1,0:T(8,128)S(1)} %get-tuple-element.23.refs_3_), channel_id=1, source_target_pairs={{4,0},{8,4},{12,8},{14,12},{10,14},{6,10},{2,6},{0,2},{5,1},{9,5},... | collective-permute-start | bytes 602120 | tf_op jit(solution)/shard_map/ppermute | solution.py:480
  9.9 8.6 %collective-permute-start.3 = (f32[392,128]{1,0:T(8,128)S(1)}, f32[392,128]{1,0:T(8,128)S(1)}, u32[]{:S(2)}, u32[]{:S(2)}) collective-permute-start(f32[392,128]{1,0:T(8,128)S(1)} %collective-permute-done.2.refs_5_), channel_id=1, source_target_pairs={{0,4},{4,8},{8,12},{12,14},{14,10},{10,6},{6,2},{2,0},{1,5},{5,9},... | collective-permute-start | bytes 602120 | tf_op jit(solution)/shard_map/ppermute | solution.py:465
  12.0 8.6 %collective-permute-start.7 = (f32[392,128]{1,0:T(8,128)S(1)}, f32[392,128]{1,0:T(8,128)S(1)}, u32[]{:S(2)}, u32[]{:S(2)}) collective-permute-start(f32[392,128]{1,0:T(8,128)S(1)} %collective-permute-done.6.refs_6_), channel_id=1, source_target_pairs={{4,0},{8,4},{12,8},{14,12},{10,14},{6,10},{2,6},{0,2},{5,1},{9,5},... | collective-permute-start | bytes 602120 | tf_op jit(solution)/shard_map/ppermute | solution.py:466
  14.2 9.0 %collective-permute-start.14 = (f32[392,128]{1,0:T(8,128)S(1)}, f32[392,128]{1,0:T(8,128)S(1)}, u32[]{:S(2)}, u32[]{:S(2)}) collective-permute-start(f32[392,128]{1,0:T(8,128)S(1)} %collective-permute-done.12.refs_8_), channel_id=1, source_target_pairs={{0,4},{4,8},{8,12},{12,14},{14,10},{10,6},{6,2},{2,0},{1,5},{5,9},... | collective-permute-start | bytes 602120 | tf_op jit(solution)/shard_map/ppermute | solution.py:481
  16.3 8.6 %collective-permute-start.11 = (f32[392,128]{1,0:T(8,128)S(1)}, f32[392,128]{1,0:T(8,128)S(1)}, u32[]{:S(2)}, u32[]{:S(2)}) collective-permute-start(f32[392,128]{1,0:T(8,128)S(1)} %collective-permute-done.10.refs_7_), channel_id=1, source_target_pairs={{4,0},{8,4},{12,8},{14,12},{10,14},{6,10},{2,6},{0,2},{5,1},{9,5},... | collective-permute-start | bytes 602120 | tf_op jit(solution)/shard_map/ppermute | solution.py:480
  18.5 8.6 %collective-permute-start.4 = (f32[392,128]{1,0:T(8,128)S(1)}, f32[392,128]{1,0:T(8,128)S(1)}, u32[]{:S(2)}, u32[]{:S(2)}) collective-permute-start(f32[392,128]{1,0:T(8,128)S(1)} %collective-permute-done.3.refs_3_), channel_id=1, source_target_pairs={{0,4},{4,8},{8,12},{12,14},{14,10},{10,6},{6,2},{2,0},{1,5},{5,9},... | collective-permute-start | bytes 602120 | tf_op jit(solution)/shard_map/ppermute | solution.py:465
  20.6 8.6 %collective-permute-start.8 = (f32[392,128]{1,0:T(8,128)S(1)}, f32[392,128]{1,0:T(8,128)S(1)}, u32[]{:S(2)}, u32[]{:S(2)}) collective-permute-start(f32[392,128]{1,0:T(8,128)S(1)} %collective-permute-done.7.refs_4_), channel_id=1, source_target_pairs={{4,0},{8,4},{12,8},{14,12},{10,14},{6,10},{2,6},{0,2},{5,1},{9,5},... | collective-permute-start | bytes 602120 | tf_op jit(solution)/shard_map/ppermute | solution.py:466
  24.9 7.9 %collective-permute-start.15 = (f32[392,128]{1,0:T(8,128)S(1)}, f32[392,128]{1,0:T(8,128)S(1)}, u32[]{:S(2)}, u32[]{:S(2)}) collective-permute-start(f32[392,128]{1,0:T(8,128)S(1)} %collective-permute-done.14.refs_6_), channel_id=1, source_target_pairs={{0,4},{4,8},{8,12},{12,14},{14,10},{10,6},{6,2},{2,0},{1,5},{5,9},... | collective-permute-start | bytes 602120 | tf_op jit(solution)/shard_map/ppermute | solution.py:481
  26.4 7.9 %collective-permute-start.13 = (f32[392,128]{1,0:T(8,128)S(1)}, f32[392,128]{1,0:T(8,128)S(1)}, u32[]{:S(2)}, u32[]{:S(2)}) collective-permute-start(f32[392,128]{1,0:T(8,128)S(1)} %collective-permute-done.11.refs_5_), channel_id=1, source_target_pairs={{4,0},{8,4},{12,8},{14,12},{10,14},{6,10},{2,6},{0,2},{5,1},{9,5},... | collective-permute-start | bytes 602120 | tf_op jit(solution)/shard_map/ppermute | solution.py:480
  27.1 9.1 %collective-permute-start.5 = (f32[392,128]{1,0:T(8,128)S(1)}, f32[392,128]{1,0:T(8,128)S(1)}, u32[]{:S(2)}, u32[]{:S(2)}) collective-permute-start(f32[392,128]{1,0:T(8,128)S(1)} %collective-permute-done.4.refs_7_), channel_id=1, source_target_pairs={{0,4},{4,8},{8,12},{12,14},{14,10},{10,6},{6,2},{2,0},{1,5},{5,9},... | collective-permute-start | bytes 602120 | tf_op jit(solution)/shard_map/ppermute | solution.py:465
  29.2 7.9 %collective-permute-start.9 = (f32[392,128]{1,0:T(8,128)S(1)}, f32[392,128]{1,0:T(8,128)S(1)}, u32[]{:S(2)}, u32[]{:S(2)}) collective-permute-start(f32[392,128]{1,0:T(8,128)S(1)} %collective-permute-done.8.refs_8_), channel_id=1, source_target_pairs={{4,0},{8,4},{12,8},{14,12},{10,14},{6,10},{2,6},{0,2},{5,1},{9,5},... | collective-permute-start | bytes 602120 | tf_op jit(solution)/shard_map/ppermute | solution.py:466

commit v4 on v3

--- a/solution.py
+++ b/solution.py
@@ -13,7 +13,7 @@
 
 
 FILTER = 0.055
-UNROLL = 4
+UNROLL = 6
 VMEM_GRANT = 8 * 1024 * 1024
 
 
@@ -155,35 +155,29 @@
     return copies
 
 
-def write_labels(ref, rows, numbers):
-    shape = (ref.shape[0] - rows, ref.shape[1])
-    line = lax.broadcasted_iota(jnp.int32, shape, 0)
-    lane = lax.broadcasted_iota(jnp.int32, shape, 1)
-    labels = jnp.zeros(shape, jnp.int32)
-    for (x, y), number in numbers:
-        labels = jnp.where((line == x) & (lane == y), number, labels)
-    ref[pl.ds(rows, shape[0]), :] = labels.astype(jnp.float32)
+def matrix_of(ref, rows):
+    return ref.at[pl.ds(0, rows)].reshape(rows, ref.shape[2])
 
 
 def pack_kernel(lead, index_ref, blocks_ref, lead_ref, rest_ref, index, sems):
     slots = index.shape[3]
-    lead_rows = blocks_ref.shape[0] // slots * lead
-    rest_rows = blocks_ref.shape[0] - lead_rows
+    lead_rows, rest_rows = lead_ref.shape[0] - 1, rest_ref.shape[0] - 1
     copies = start_all(
         [
             (index_ref, index),
-            (blocks_ref.at[pl.ds(0, lead_rows)], lead_ref.at[pl.ds(0, lead_rows)]),
-            (blocks_ref.at[pl.ds(lead_rows, rest_rows)], rest_ref.at[pl.ds(0, rest_rows)]),
+            (blocks_ref.at[pl.ds(0, lead_rows)], matrix_of(lead_ref, lead_rows)),
+            (blocks_ref.at[pl.ds(lead_rows, rest_rows)], matrix_of(rest_ref, rest_rows)),
         ],
         sems,
     )
+    lane = lax.broadcasted_iota(jnp.int32, lead_ref.shape[1:], 1)
     copies[0].wait()
     for ref, rows, first, count in ((lead_ref, lead_rows, 0, lead), (rest_ref, rest_rows, lead, slots - lead)):
-        write_labels(
-            ref,
-            rows,
-            [((n, field), index[0, 0, field, first + n]) for n in range(count) for field in range(2)],
-        )
+        labels = jnp.zeros(ref.shape[1:], jnp.int32)
+        for n in range(count):
+            for field in range(2):
+                labels = jnp.where(lane == 2 * n + field, index[0, 0, field, first + n], labels)
+        ref[rows] = labels.astype(jnp.float32)
     for copy in copies[1:]:
         copy.wait()
 
@@ -195,8 +189,8 @@
     return pl.pallas_call(
         functools.partial(pack_kernel, lead),
         out_shape=(
-            pltpu.VMEM((lead_rows + -(-lead // 8) * 8, width), jnp.float32),
-            pltpu.VMEM((rows - lead_rows + -(-(slots - lead) // 8) * 8, width), jnp.float32),
+            pltpu.VMEM((lead_rows + 1, 1, width), jnp.float32),
+            pltpu.VMEM((rows - lead_rows + 1, 1, width), jnp.float32),
         ),
         in_specs=[HBM_SPEC] * 2,
         out_specs=(VMEM_SPEC,) * 2,
@@ -206,15 +200,21 @@
     )(in_hbm(index), in_hbm(blocks))
 
 
+def field_bits(count):
+    return count.bit_length()
+
+
 def lines_of(entries, lanes):
-    return -(-entries * BR // lanes)
+    return -(-entries // lanes)
 
 
 def window_kernel(half_cols, *refs):
     hbm_refs, twin_ref = refs[:5], refs[5]
     parts_ref, norms_ref, table_ref = refs[6:9]
     perm, own_place, twin_place, targets, own = refs[9:14]
-    stop_at, table, sems, out_sem = refs[14:]
+    stop_at, target_at, table, sems, out_sem = refs[14:]
+    slot_bits, target_bits = field_bits(parts_ref.shape[0]), field_bits(targets.shape[2])
+    no_slot, no_target = (1 << slot_bits) - 1, (1 << target_bits) - 1
     lanes = table.shape[1]
     column_line = lines_of(perm.shape[0], lanes)
     row, row_count = lax.axis_index("row"), lax.axis_size("row")
@@ -233,9 +233,9 @@
 
     split_half(1, twin_ref)
     for i in range(stop_at.shape[0]):
-        stop_at[i] = -1
-    for cell in range(half_cols * BR):
-        table[column_line + cell // lanes, cell % lanes] = -1.0
+        stop_at[i] = no_slot
+    for i in range(target_at.shape[0]):
+        target_at[i] = no_target
     for copy in copies[:4]:
         copy.wait()
     for local in range(half_stops):
@@ -245,17 +245,21 @@
             stop_at[own_base + own_place[0, local, q]] = local * present + q
             stop_at[twin_base + twin_place[0, local, q]] = (half_stops + local) * present + q
     for t in range(targets.shape[2]):
-        place = targets[0, 0, t]
-        cell = lax.rem(place, half_cols) * BR + lax.div(place, half_cols)
-        table[column_line + lax.div(cell, lanes), lax.rem(cell, lanes)] = jnp.float32(t)
+        target_at[targets[0, 0, t]] = t
+    for j in range(half_cols):
+        packed = target_at[j]
+        for i in range(1, BR):
+            packed = packed | (target_at[i * half_cols + j] << (target_bits * i))
+        table[column_line + j // lanes, j % lanes] = packed.astype(jnp.float32)
     for block_row in range(perm.shape[0]):
         behind = lax.div(perm[block_row], BR) - row
         stop = jnp.where(behind < 0, behind + row_count, behind)
         place = jnp.minimum(stop, 2 * half_stops - 1) * BR * BR + lax.rem(perm[block_row], BR)
-        for i in range(BR):
-            cell = block_row * BR + i
-            slot = jnp.where(stop < 2 * half_stops, stop_at[place + i * BR], -1)
-            table[cell // lanes, cell % lanes] = slot.astype(jnp.float32)
+        packed = stop_at[place]
+        for i in range(1, BR):
+            packed = packed | (stop_at[place + i * BR] << (slot_bits * i))
+        packed = jnp.where(stop < 2 * half_stops, packed, (1 << (slot_bits * BR)) - 1)
+        table[block_row // lanes, block_row % lanes] = packed.astype(jnp.float32)
     publish = pltpu.make_async_copy(table, table_ref, out_sem)
     publish.start()
     copies[4].wait()
@@ -281,6 +285,7 @@
             *(pltpu.SMEM(x.shape, jnp.int32) for x in held),
             pltpu.VMEM(own.shape, jnp.float32),
             pltpu.SMEM((2 * own_places.shape[1] * BR * BR,), jnp.int32),
+            pltpu.SMEM((BR * half_cols,), jnp.int32),
             pltpu.SMEM((lines, block_size), jnp.float32),
             pltpu.SemaphoreType.DMA((5,)),
             pltpu.SemaphoreType.DMA,
@@ -301,57 +306,51 @@
         rest = rest[1:]
     listed, touched, held, out_sems = rest[1:]
     block_size = c_ref.shape[-1]
-    slot_bits = (parts_ref.shape[0] - 1).bit_length()
-    code_bits = slot_bits + c_ref.shape[0].bit_length()
-    slot_mask, none = (1 << slot_bits) - 1, (1 << code_bits) - 1
-    per_word = 2 if 2 * code_bits < 32 else 1
+    slot_bits, target_bits = field_bits(parts_ref.shape[0]), field_bits(c_ref.shape[0])
+    no_slot, no_target = (1 << slot_bits) - 1, (1 << target_bits) - 1
+    code_bits = slot_bits + target_bits
 
     def target_of(entry):
-        return (entry & none) >> slot_bits
+        return (entry >> slot_bits) & no_target
 
     if first:
         c_ref[...] = jnp.zeros_like(c_ref)
 
     lane = lax.broadcasted_iota(jnp.int32, (1, block_size), 1).astype(jnp.float32)
+    label_rows = -(-max(pieces) // 8) * 8
+    line = lax.broadcasted_iota(jnp.int32, (label_rows, 1), 0).astype(jnp.float32)
     slot_lines = lines_of(block_rows, block_size)
     target_lines = lines_of(half_cols, block_size)
 
     def look_up(cells, first_line, lines):
         found = 0.0
         for n in range(lines):
-            line = table_ref[pl.ds(first_line + n, 1), :]
+            entries = table_ref[pl.ds(first_line + n, 1), :]
             hit = cells - float(n * block_size) == lane
-            found += jnp.sum(jnp.where(hit, line, 0.0), axis=1, keepdims=True)
+            found += jnp.sum(jnp.where(hit, entries, 0.0), axis=1, keepdims=True)
         return found
 
+    read = []
+    for chunk_ref, blocks in zip(chunk_refs, pieces):
+        labels = jnp.broadcast_to(chunk_ref[blocks * block_size], (label_rows, block_size))
+        block_row, column = (
+            jnp.sum(jnp.where(lane == 2.0 * line + float(field), labels, 0.0), axis=1, keepdims=True)
+            for field in range(2)
+        )
+        slot = look_up(block_row, 0, slot_lines).astype(jnp.int32)
+        target = look_up(column, slot_lines, target_lines).astype(jnp.int32)
+        blocks_ref = matrix_of(chunk_ref, blocks * block_size)
+        read += [(blocks_ref, b, slot[b, 0], target[b, 0]) for b in range(blocks)]
     pairs, kept = jnp.int32(0), jnp.int32(0)
-    words = []
-    for chunk_ref, blocks in zip(chunk_refs, pieces):
-        labels = chunk_ref[pl.ds(blocks * block_size, chunk_ref.shape[0] - blocks * block_size), :]
+    for blocks_ref, b, slots, targets in read:
+        before = pairs
         for i in range(BR):
-            slot = look_up(labels[:, 0:1] * float(BR) + float(i), 0, slot_lines)
-            target = look_up(labels[:, 1:2] * float(BR) + float(i), slot_lines, target_lines)
-            present = (slot >= 0.0) & (target >= 0.0)
-            code = jnp.where(present, target * float(1 << slot_bits) + slot, float(none)).astype(jnp.int32)
-            if i % per_word:
-                words[-1] = words[-1] + (code << (code_bits * (i % per_word)))
-            else:
-                words.append(code)
-    read = [
-        [words[number * (BR // per_word) + w][b, 0] for w in range(BR // per_word)]
-        for number, blocks in enumerate(pieces)
-        for b in range(blocks)
-    ]
-    for number, (chunk_ref, blocks) in enumerate(zip(chunk_refs, pieces)):
-        for b in range(blocks):
-            before = pairs
-            for word in read.pop(0):
-                for n in range(per_word):
-                    code = (word >> (code_bits * n)) & none
-                    listed[pairs] = code + (kept << code_bits)
-                    pairs = pairs + (code != none).astype(jnp.int32)
-            held[kept] = chunk_ref[pl.ds(b * block_size, block_size), :]
-            kept = kept + (pairs > before).astype(jnp.int32)
+            ks = (slots >> (slot_bits * i)) & no_slot
+            target = (targets >> (target_bits * i)) & no_target
+            listed[pairs] = ks | (target << slot_bits) | (kept << code_bits)
+            pairs = pairs + ((ks != no_slot) & (target != no_target)).astype(jnp.int32)
+        held[kept] = blocks_ref[pl.ds(b * block_size, block_size), :]
+        kept = kept + (pairs > before).astype(jnp.int32)
     for u in range(UNROLL):
         listed[pairs + u] = 0
 
@@ -359,7 +358,7 @@
         for u in range(UNROLL):
             at = step * UNROLL + u
             entry = listed[at]
-            ks, target, slot = entry & slot_mask, target_of(entry), entry >> code_bits
+            ks, target, slot = entry & no_slot, target_of(entry), entry >> code_bits
             density = held[slot]
             bound = jnp.where(at < pairs, limit, jnp.inf)
             keep = norms_ref[ks] * norm_of(density) >= bound
@@ -385,17 +384,19 @@
         for t in range(targets):
             touched[t] = 0
 
-        def touch(p, _):
-            touched[target_of(listed[p])] = 1
-
-        lax.fori_loop(0, pairs, touch, None)
-        for begin in (True, False):
-            for t in range(targets):
-                copy = pltpu.make_async_copy(c_ref.at[t], out_ref.at[t], out_sems.at[t])
-
-                @pl.when(touched[t] == 1)
-                def _(copy=copy, begin=begin):
-                    (copy.start if begin else copy.wait)()
+        def each_target(act, before, after):
+            def one(p, _):
+                target = target_of(listed[p])
+
+                @pl.when(touched[target] == before)
+                def _():
+                    act(pltpu.make_async_copy(c_ref.at[target], out_ref.at[target], out_sems.at[target]))
+                    touched[target] = after
+
+            lax.fori_loop(0, pairs, one, None)
+
+        each_target(lambda copy: copy.start(), 0, 1)
+        each_target(lambda copy: copy.wait(), 1, 2)
 
 
 def add_products(sizes, window, accumulated, group, shape, final=None, written=None):
@@ -482,16 +483,18 @@
             if step < half - 1:
                 group += [(lead, a_fwd), (slots - lead, b_bwd)]
             group += [(lead, a_bwd), (slots - lead, b_fwd)]
-    group = [(lead, a_fwd), (slots - lead, b_bwd)]
-    _, total = add_products(sizes, window, accumulated, group, shape, "touched", *written)
-    return total.reshape(c_index.shape + (block_size, block_size))
+    for group in ([(lead, a_fwd)], [(slots - lead, b_bwd)]):
+        accumulated, *written = add_products(sizes, window, accumulated, group, shape, "touched", *written)
+    return written[0].reshape(c_index.shape + (block_size, block_size))
 
 
 def on_device(d_blocks, d_index, row_perm, ks_blocks, ks_index, c_index):
     rows, slots = lax.axis_size("row"), d_blocks.shape[2]
     gathered = rows * slots
     routed = rows * CAPX + 3 * (3 * rows // 2)
-    plan = ring_plan if gathered <= routed else panel_plan
+    window_slots = lax.axis_size("col") * ks_index.shape[1] * ks_index.shape[2]
+    packable = BR * max(field_bits(window_slots), field_bits(c_index.shape[2])) <= 24
+    plan = ring_plan if gathered <= routed and packable else panel_plan
     return plan(d_blocks, d_index, row_perm, ks_blocks, ks_index, c_index)
 
 

time: 38.8 us -> 38.4 us (0.990)
  Pallas kernels: 12.4 us -> 9.64 us
  waiting for transfers between devices: 11 us -> 13 us
    pallas_call x4 -> x5, Pallas kernels: 9.42 us -> 6.62 us  [add_products(): pl.pallas_call(functools.partial(product_kernel, (*sizes, limit, pieces,...]
    ppermute x3, waiting for transfers between devices: 0.54 us -> 2.54 us  [ring_plan(): b_fwd = lax.ppermute(b_fwd, 'row', forward)]
  transfers between devices with their start and end apart: 16 -> 16, of which waited for: 9 -> 10; matrix products, arithmetic and copies ran while one was open for 0% -> 0% of each run, Pallas kernels for 28% -> 22%
where the time goes in v4:
time: 38.4 us; the launch traced here: 37.9 us
  starting transfers between devices  15.1 us (39%)
  waiting for transfers between devices  13 us (34%)
  Pallas kernels  9.64 us (25%)
    ppermute x4, starting transfers between devices, ring_plan(): a_fwd = lax.ppermute(a_fwd, 'row', forward)  8.62 us
    pallas_call x5, Pallas kernels, add_products(): pl.pallas_call(functools.partial(product_kernel, (*sizes, limit, pieces,...  6.62 us
    ppermute x3, starting transfers between devices, ring_plan(): b_fwd = lax.ppermute(b_fwd, 'row', forward)  5.59 us
    ppermute x4, waiting for transfers between devices, ring_plan(): a_fwd = lax.ppermute(a_fwd, 'row', forward)  4.66 us
    ppermute x3, waiting for transfers between devices, ring_plan(): a_bwd = lax.ppermute(a_bwd, 'row', backward)  3.65 us
    ppermute x3, waiting for transfers between devices, ring_plan(): b_fwd = lax.ppermute(b_fwd, 'row', forward)  2.54 us
    pallas_call x1, Pallas kernels, prepare_window(): pl.pallas_call(functools.partial(window_kernel, half_cols), out_shape=(pl...  1.97 us
    ppermute x1, waiting for transfers between devices, ring_plan(): places_twin = lax.ppermute(ks_index, 'col', twins)  1.35 us
  transfers between devices with their start and end apart: 16, of which 10 were waited for; matrix products, arithmetic and copies ran while one was open for 0% of the time, Pallas kernels for 22%

profile of v4, /device:TPU:0, one launch (start us, length us, event | category | flops | bytes accessed | tf_op | source)
XLA Modules:
  0.0 37.9 jit_solution(14327371454808536636)
XLA Ops:
  0.0 0.5 %collective-permute-start.1 = (f32[20,128,128]{2,1,0:T(8,128)}, f32[20,128,128]{2,1,0:T(8,128)S(1)}, u32[]{:S(2)}, u32[]{:S(2)}) collective-permute-start(f32[20,128,128]{2,1,0:T(8,128)} %bitcast.4), channel_id=1, source_target_pairs={{0,1},{1,0},{2,3},{3,2},{4,5},{5,4},{6,7},{7,6},{8,9},{9,8},{10,11... | collective-permute-start | bytes 3932168 | tf_op jit(solution)/shard_map/ppermute | solution.py:459
  0.5 1.0 %shard_map.65 = (f32[385,1,128]{2,1,0:T(1,128)S(1)}, f32[385,1,128]{2,1,0:T(1,128)S(1)}) custom-call(s32[1,1,2,6]{3,2,1,0:T(2,128)} %bitcast.7, f32[768,128]{1,0:T(8,128)} %bitcast.6), custom_call_target="tpu_custom_call" | custom-call | bytes 3700000 | tf_op jit(solution)/shard_map/pallas_call | solution.py:189
  1.5 2.6 %collective-permute-start.6 = (f32[385,1,128]{2,1,0:T(1,128)S(1)}, f32[385,1,128]{2,1,0:T(1,128)S(1)}, u32[]{:S(2)}, u32[]{:S(2)}) collective-permute-start(f32[385,1,128]{2,1,0:T(1,128)S(1)} %get-tuple-element.26.refs_3_), channel_id=1, source_target_pairs={{0,4},{4,8},{8,12},{12,14},{14,10},{10,6},{6,2},{2,0},{1,5},{5,9},... | collective-permute-start | bytes 591368 | tf_op jit(solution)/shard_map/ppermute | solution.py:466
  4.1 0.0 collective-permute-start.2
  4.1 2.0 %collective-permute-start.12 = (f32[385,1,128]{2,1,0:T(1,128)S(1)}, f32[385,1,128]{2,1,0:T(1,128)S(1)}, u32[]{:S(2)}, u32[]{:S(2)}) collective-permute-start(f32[385,1,128]{2,1,0:T(1,128)S(1)} %get-tuple-element.25.refs_4_), channel_id=1, source_target_pairs={{0,4},{4,8},{8,12},{12,14},{14,10},{10,6},{6,2},{2,0},{1,5},{5,9},... | collective-permute-start | bytes 591368 | tf_op jit(solution)/shard_map/ppermute | solution.py:482
  6.2 0.0 collective-permute-start
  6.2 1.3 %collective-permute-done.refs_2_ = s32[1,2,10]{2,1,0:T(2,128)S(1)} collective-permute-done((s32[1,2,10]{2,1,0:T(2,128)}, s32[1,2,10]{2,1,0:T(2,128)S(1)}, u32[]{:S(2)}, u32[]{:S(2)}) %collective-permute-start) | collective-permute-done | bytes 112 | tf_op jit(solution)/shard_map/ppermute | solution.py:460
  7.5 0.0 copy-start
  7.5 0.0 collective-permute-start.10
  7.5 2.3 %collective-permute-done.6.refs_5_ = f32[385,1,128]{2,1,0:T(1,128)S(1)} collective-permute-done((f32[385,1,128]{2,1,0:T(1,128)S(1)}, f32[385,1,128]{2,1,0:T(1,128)S(1)}, u32[]{:S(2)}, u32[]{:S(2)}) %collective-permute-start.6) | collective-permute-done | bytes 197152 | tf_op jit(solution)/shard_map/ppermute | solution.py:466
  9.8 2.0 %collective-permute-start.7 = (f32[385,1,128]{2,1,0:T(1,128)S(1)}, f32[385,1,128]{2,1,0:T(1,128)S(1)}, u32[]{:S(2)}, u32[]{:S(2)}) collective-permute-start(f32[385,1,128]{2,1,0:T(1,128)S(1)} %collective-permute-done.6.refs_5_), channel_id=1, source_target_pairs={{0,4},{4,8},{8,12},{12,14},{14,10},{10,6},{6,2},{2,0},{1,5},{5,9},... | collective-permute-start | bytes 591368 | tf_op jit(solution)/shard_map/ppermute | solution.py:466
  11.8 0.0 collective-permute-done.2.refs_6_
  11.9 0.0 collective-permute-start.3
  11.9 0.0 collective-permute-done.1.refs_5_
  11.9 0.0 copy-done
  11.9 2.0 %shard_map.64 = (bf16[40,128,256]{2,1,0:T(8,128)(2,1)S(1)}, f32[40,1,128]{2,1,0:T(1,128)S(1)}, f32[8,128]{1,0:T(8,128)S(1)}) custom-call(s32[32]{0:T(128)} %refs_0_.1, s32[1,2,10]{2,1,0:T(2,128)} %refs_1_.1, s32[1,2,10]{2,1,0:T(2,128)} %copy-done, s32[1,1,16]{2,1,0:T(1,128)} %refs_3_.1, f32[20,128,128]{2,1,0:T(8,128)} %bitcast.5, ...), custom_call_target="tpu_custom_call" | custom-call | bytes 7400000 | tf_op jit(solution)/shard_map/pallas_call | solution.py:275
  13.9 0.2 collective-permute-done.12.refs_8_
  14.1 2.0 %collective-permute-start.14 = (f32[385,1,128]{2,1,0:T(1,128)S(1)}, f32[385,1,128]{2,1,0:T(1,128)S(1)}, u32[]{:S(2)}, u32[]{:S(2)}) collective-permute-start(f32[385,1,128]{2,1,0:T(1,128)S(1)} %collective-permute-done.12.refs_8_), channel_id=1, source_target_pairs={{0,4},{4,8},{8,12},{12,14},{14,10},{10,6},{6,2},{2,0},{1,5},{5,9},... | collective-permute-start | bytes 591368 | tf_op jit(solution)/shard_map/ppermute | solution.py:482
  16.1 0.0 collective-permute-done.10.refs_7_
  16.1 0.0 collective-permute-start.11
  16.1 2.2 %collective-permute-done.7.refs_3_ = f32[385,1,128]{2,1,0:T(1,128)S(1)} collective-permute-done((f32[385,1,128]{2,1,0:T(1,128)S(1)}, f32[385,1,128]{2,1,0:T(1,128)S(1)}, u32[]{:S(2)}, u32[]{:S(2)}) %collective-permute-start.7) | collective-permute-done | bytes 197152 | tf_op jit(solution)/shard_map/ppermute | solution.py:466
  18.3 2.0 %collective-permute-start.8 = (f32[385,1,128]{2,1,0:T(1,128)S(1)}, f32[385,1,128]{2,1,0:T(1,128)S(1)}, u32[]{:S(2)}, u32[]{:S(2)}) collective-permute-start(f32[385,1,128]{2,1,0:T(1,128)S(1)} %collective-permute-done.7.refs_3_), channel_id=1, source_target_pairs={{0,4},{4,8},{8,12},{12,14},{14,10},{10,6},{6,2},{2,0},{1,5},{5,9},... | collective-permute-start | bytes 591368 | tf_op jit(solution)/shard_map/ppermute | solution.py:466
  20.3 0.0 collective-permute-done.3.refs_4_
  20.3 0.0 collective-permute-start.4
  20.3 1.2 %shard_map.66.refs_9_ = f32[16,128,128]{2,1,0:T(8,128)S(1)} custom-call(f32[8,128]{1,0:T(8,128)S(1)} %get-tuple-element.22.refs_0_, bf16[40,128,256]{2,1,0:T(8,128)(2,1)S(1)} %get-tuple-element.23.refs_1_, f32[40,1,128]{2,1,0:T(1,128)S(1)} %get-tuple-element.24.refs_2_, f32[385,1,128]{2,1,0:T(1,128)S(1)} %get-tuple-element.26.refs_3_, ...), custom_call_target="tpu_custom_call" | custom-call | bytes 7400000 | tf_op jit(solution)/shard_map/pallas_call | solution.py:422
  21.6 0.9 %collective-permute-done.14.refs_6_ = f32[385,1,128]{2,1,0:T(1,128)S(1)} collective-permute-done((f32[385,1,128]{2,1,0:T(1,128)S(1)}, f32[385,1,128]{2,1,0:T(1,128)S(1)}, u32[]{:S(2)}, u32[]{:S(2)}) %collective-permute-start.14) | collective-permute-done | bytes 197152 | tf_op jit(solution)/shard_map/ppermute | solution.py:482
  22.5 2.0 %collective-permute-done.11.refs_5_ = f32[385,1,128]{2,1,0:T(1,128)S(1)} collective-permute-done((f32[385,1,128]{2,1,0:T(1,128)S(1)}, f32[385,1,128]{2,1,0:T(1,128)S(1)}, u32[]{:S(2)}, u32[]{:S(2)}) %collective-permute-start.11) | collective-permute-done | bytes 197152 | tf_op jit(solution)/shard_map/ppermute | solution.py:481
  24.6 1.6 %collective-permute-start.15 = (f32[385,1,128]{2,1,0:T(1,128)S(1)}, f32[385,1,128]{2,1,0:T(1,128)S(1)}, u32[]{:S(2)}, u32[]{:S(2)}) collective-permute-start(f32[385,1,128]{2,1,0:T(1,128)S(1)} %collective-permute-done.14.refs_6_), channel_id=1, source_target_pairs={{0,4},{4,8},{8,12},{12,14},{14,10},{10,6},{6,2},{2,0},{1,5},{5,9},... | collective-permute-start | bytes 591368 | tf_op jit(solution)/shard_map/ppermute | solution.py:482
  26.1 0.4 %collective-permute-start.13 = (f32[385,1,128]{2,1,0:T(1,128)S(1)}, f32[385,1,128]{2,1,0:T(1,128)S(1)}, u32[]{:S(2)}, u32[]{:S(2)}) collective-permute-start(f32[385,1,128]{2,1,0:T(1,128)S(1)} %collective-permute-done.11.refs_5_), channel_id=1, source_target_pairs={{4,0},{8,4},{12,8},{14,12},{10,14},{6,10},{2,6},{0,2},{5,1},{9,5},... | collective-permute-start | bytes 591368 | tf_op jit(solution)/shard_map/ppermute | solution.py:481
  26.6 0.2 collective-permute-done.8.refs_7_
  26.7 2.0 %collective-permute-start.9 = (f32[385,1,128]{2,1,0:T(1,128)S(1)}, f32[385,1,128]{2,1,0:T(1,128)S(1)}, u32[]{:S(2)}, u32[]{:S(2)}) collective-permute-start(f32[385,1,128]{2,1,0:T(1,128)S(1)} %collective-permute-done.8.refs_7_), channel_id=1, source_target_pairs={{0,4},{4,8},{8,12},{12,14},{14,10},{10,6},{6,2},{2,0},{1,5},{5,9},... | collective-permute-start | bytes 591368 | tf_op jit(solution)/shard_map/ppermute | solution.py:466
  28.7 0.0 collective-permute-done.4.refs_8_
  28.8 0.0 collective-permute-start.5
  28.8 2.2 %shard_map.67 = (f32[16,128,128]{2,1,0:T(8,128)S(1)}, f32[16,128,128]{2,1,0:T(8,128)}) custom-call(f32[8,128]{1,0:T(8,128)S(1)} %get-tuple-element.22.refs_0_, bf16[40,128,256]{2,1,0:T(8,128)(2,1)S(1)} %get-tuple-element.23.refs_1_, f32[40,1,128]{2,1,0:T(1,128)S(1)} %get-tuple-element.24.refs_2_, ...), custom_call_target="tpu_custom_call", output_to_operand_aliasing={{0}: (9, {})} | custom-call | bytes 7400000 | tf_op jit(solution)/shard_map/pallas_call | solution.py:422
  31.0 1.4 %collective-permute-done.15.refs_4_ = f32[385,1,128]{2,1,0:T(1,128)S(1)} collective-permute-done((f32[385,1,128]{2,1,0:T(1,128)S(1)}, f32[385,1,128]{2,1,0:T(1,128)S(1)}, u32[]{:S(2)}, u32[]{:S(2)}) %collective-permute-start.15) | collective-permute-done | bytes 197152 | tf_op jit(solution)/shard_map/ppermute | solution.py:482
  32.4 1.6 %collective-permute-done.13.refs_3_ = f32[385,1,128]{2,1,0:T(1,128)S(1)} collective-permute-done((f32[385,1,128]{2,1,0:T(1,128)S(1)}, f32[385,1,128]{2,1,0:T(1,128)S(1)}, u32[]{:S(2)}, u32[]{:S(2)}) %collective-permute-start.13) | collective-permute-done | bytes 197152 | tf_op jit(solution)/shard_map/ppermute | solution.py:481
  34.0 1.4 %shard_map.68 = (f32[16,128,128]{2,1,0:T(8,128)S(1)}, f32[16,128,128]{2,1,0:T(8,128)}) custom-call(f32[8,128]{1,0:T(8,128)S(1)} %get-tuple-element.22.refs_0_, bf16[40,128,256]{2,1,0:T(8,128)(2,1)S(1)} %get-tuple-element.23.refs_1_, f32[40,1,128]{2,1,0:T(1,128)S(1)} %get-tuple-element.24.refs_2_, ...), custom_call_target="tpu_custom_call", output_to_operand_aliasing={{0}: (5, {}), {1}: (6, {})} | custom-call | bytes 7400000 | tf_op jit(solution)/shard_map/pallas_call | solution.py:422
  35.4 0.0 collective-permute-done.9.refs_3_
  35.4 0.4 %shard_map.69 = (f32[16,128,128]{2,1,0:T(8,128)S(1)}, f32[16,128,128]{2,1,0:T(8,128)}) custom-call(f32[8,128]{1,0:T(8,128)S(1)} %get-tuple-element.22.refs_0_, bf16[40,128,256]{2,1,0:T(8,128)(2,1)S(1)} %get-tuple-element.23.refs_1_, f32[40,1,128]{2,1,0:T(1,128)S(1)} %get-tuple-element.24.refs_2_, ...), custom_call_target="tpu_custom_call", output_to_operand_aliasing={{0}: (4, {}), {1}: (5, {})} | custom-call | bytes 7400000 | tf_op jit(solution)/shard_map/pallas_call | solution.py:422
  35.8 0.7 %collective-permute-done.5.refs_3_ = f32[385,1,128]{2,1,0:T(1,128)S(1)} collective-permute-done((f32[385,1,128]{2,1,0:T(1,128)S(1)}, f32[385,1,128]{2,1,0:T(1,128)S(1)}, u32[]{:S(2)}, u32[]{:S(2)}) %collective-permute-start.5) | collective-permute-done | bytes 197152 | tf_op jit(solution)/shard_map/ppermute | solution.py:467
  36.5 1.3 %shard_map.70 = (f32[16,128,128]{2,1,0:T(8,128)S(1)}, f32[16,128,128]{2,1,0:T(8,128)}) custom-call(f32[8,128]{1,0:T(8,128)S(1)} %get-tuple-element.22.refs_0_, bf16[40,128,256]{2,1,0:T(8,128)(2,1)S(1)} %get-tuple-element.23.refs_1_, f32[40,1,128]{2,1,0:T(1,128)S(1)} %get-tuple-element.24.refs_2_, ...), custom_call_target="tpu_custom_call", output_to_operand_aliasing={{0}: (4, {}), {1}: (5, {})} | custom-call | bytes 7400000 | tf_op jit(solution)/shard_map/pallas_call | solution.py:422
Async XLA Ops:
  0.0 11.9 %collective-permute-start.1 = (f32[20,128,128]{2,1,0:T(8,128)}, f32[20,128,128]{2,1,0:T(8,128)S(1)}, u32[]{:S(2)}, u32[]{:S(2)}) collective-permute-start(f32[20,128,128]{2,1,0:T(8,128)} %bitcast.4), channel_id=1, source_target_pairs={{0,1},{1,0},{2,3},{3,2},{4,5},{5,4},{6,7},{7,6},{8,9},{9,8},{10,11... | collective-permute-start | bytes 3932168 | tf_op jit(solution)/shard_map/ppermute | solution.py:459
  1.5 8.3 %collective-permute-start.6 = (f32[385,1,128]{2,1,0:T(1,128)S(1)}, f32[385,1,128]{2,1,0:T(1,128)S(1)}, u32[]{:S(2)}, u32[]{:S(2)}) collective-permute-start(f32[385,1,128]{2,1,0:T(1,128)S(1)} %get-tuple-element.26.refs_3_), channel_id=1, source_target_pairs={{0,4},{4,8},{8,12},{12,14},{14,10},{10,6},{6,2},{2,0},{1,5},{5,9},... | collective-permute-start | bytes 591368 | tf_op jit(solution)/shard_map/ppermute | solution.py:466
  4.1 7.7 %collective-permute-start.2 = (f32[385,1,128]{2,1,0:T(1,128)S(1)}, f32[385,1,128]{2,1,0:T(1,128)S(1)}, u32[]{:S(2)}, u32[]{:S(2)}) collective-permute-start(f32[385,1,128]{2,1,0:T(1,128)S(1)} %get-tuple-element.25.refs_4_), channel_id=1, source_target_pairs={{4,0},{8,4},{12,8},{14,12},{10,14},{6,10},{2,6},{0,2},{5,1},{9,5},... | collective-permute-start | bytes 591368 | tf_op jit(solution)/shard_map/ppermute | solution.py:467
  4.1 9.9 %collective-permute-start.12 = (f32[385,1,128]{2,1,0:T(1,128)S(1)}, f32[385,1,128]{2,1,0:T(1,128)S(1)}, u32[]{:S(2)}, u32[]{:S(2)}) collective-permute-start(f32[385,1,128]{2,1,0:T(1,128)S(1)} %get-tuple-element.25.refs_4_), channel_id=1, source_target_pairs={{0,4},{4,8},{8,12},{12,14},{14,10},{10,6},{6,2},{2,0},{1,5},{5,9},... | collective-permute-start | bytes 591368 | tf_op jit(solution)/shard_map/ppermute | solution.py:482
  6.2 1.4 %collective-permute-start = (s32[1,2,10]{2,1,0:T(2,128)}, s32[1,2,10]{2,1,0:T(2,128)S(1)}, u32[]{:S(2)}, u32[]{:S(2)}) collective-permute-start(s32[1,2,10]{2,1,0:T(2,128)} %refs_1_.1), channel_id=1, source_target_pairs={{0,1},{1,0},{2,3},{3,2},{4,5},{5,4},{6,7},{7,6},{8,9},{9,8},{10,11... | collective-permute-start | bytes 248 | tf_op jit(solution)/shard_map/ppermute | solution.py:460
  7.5 4.4 %copy-start = (s32[1,2,10]{2,1,0:T(2,128)}, s32[1,2,10]{2,1,0:T(2,128)S(1)}, u32[]{:S(2)}) copy-start(s32[1,2,10]{2,1,0:T(2,128)S(1)} %collective-permute-done.refs_2_) | copy-start | bytes 244
  7.5 8.6 %collective-permute-start.10 = (f32[385,1,128]{2,1,0:T(1,128)S(1)}, f32[385,1,128]{2,1,0:T(1,128)S(1)}, u32[]{:S(2)}, u32[]{:S(2)}) collective-permute-start(f32[385,1,128]{2,1,0:T(1,128)S(1)} %get-tuple-element.26.refs_3_), channel_id=1, source_target_pairs={{4,0},{8,4},{12,8},{14,12},{10,14},{6,10},{2,6},{0,2},{5,1},{9,5},... | collective-permute-start | bytes 591368 | tf_op jit(solution)/shard_map/ppermute | solution.py:481
  9.8 8.4 %collective-permute-start.7 = (f32[385,1,128]{2,1,0:T(1,128)S(1)}, f32[385,1,128]{2,1,0:T(1,128)S(1)}, u32[]{:S(2)}, u32[]{:S(2)}) collective-permute-start(f32[385,1,128]{2,1,0:T(1,128)S(1)} %collective-permute-done.6.refs_5_), channel_id=1, source_target_pairs={{0,4},{4,8},{8,12},{12,14},{14,10},{10,6},{6,2},{2,0},{1,5},{5,9},... | collective-permute-start | bytes 591368 | tf_op jit(solution)/shard_map/ppermute | solution.py:466
  11.9 8.4 %collective-permute-start.3 = (f32[385,1,128]{2,1,0:T(1,128)S(1)}, f32[385,1,128]{2,1,0:T(1,128)S(1)}, u32[]{:S(2)}, u32[]{:S(2)}) collective-permute-start(f32[385,1,128]{2,1,0:T(1,128)S(1)} %collective-permute-done.2.refs_6_), channel_id=1, source_target_pairs={{4,0},{8,4},{12,8},{14,12},{10,14},{6,10},{2,6},{0,2},{5,1},{9,5},... | collective-permute-start | bytes 591368 | tf_op jit(solution)/shard_map/ppermute | solution.py:467
  14.1 8.4 %collective-permute-start.14 = (f32[385,1,128]{2,1,0:T(1,128)S(1)}, f32[385,1,128]{2,1,0:T(1,128)S(1)}, u32[]{:S(2)}, u32[]{:S(2)}) collective-permute-start(f32[385,1,128]{2,1,0:T(1,128)S(1)} %collective-permute-done.12.refs_8_), channel_id=1, source_target_pairs={{0,4},{4,8},{8,12},{12,14},{14,10},{10,6},{6,2},{2,0},{1,5},{5,9},... | collective-permute-start | bytes 591368 | tf_op jit(solution)/shard_map/ppermute | solution.py:482
  16.1 8.4 %collective-permute-start.11 = (f32[385,1,128]{2,1,0:T(1,128)S(1)}, f32[385,1,128]{2,1,0:T(1,128)S(1)}, u32[]{:S(2)}, u32[]{:S(2)}) collective-permute-start(f32[385,1,128]{2,1,0:T(1,128)S(1)} %collective-permute-done.10.refs_7_), channel_id=1, source_target_pairs={{4,0},{8,4},{12,8},{14,12},{10,14},{6,10},{2,6},{0,2},{5,1},{9,5},... | collective-permute-start | bytes 591368 | tf_op jit(solution)/shard_map/ppermute | solution.py:481
  18.3 8.4 %collective-permute-start.8 = (f32[385,1,128]{2,1,0:T(1,128)S(1)}, f32[385,1,128]{2,1,0:T(1,128)S(1)}, u32[]{:S(2)}, u32[]{:S(2)}) collective-permute-start(f32[385,1,128]{2,1,0:T(1,128)S(1)} %collective-permute-done.7.refs_3_), channel_id=1, source_target_pairs={{0,4},{4,8},{8,12},{12,14},{14,10},{10,6},{6,2},{2,0},{1,5},{5,9},... | collective-permute-start | bytes 591368 | tf_op jit(solution)/shard_map/ppermute | solution.py:466
  20.3 8.4 %collective-permute-start.4 = (f32[385,1,128]{2,1,0:T(1,128)S(1)}, f32[385,1,128]{2,1,0:T(1,128)S(1)}, u32[]{:S(2)}, u32[]{:S(2)}) collective-permute-start(f32[385,1,128]{2,1,0:T(1,128)S(1)} %collective-permute-done.3.refs_4_), channel_id=1, source_target_pairs={{4,0},{8,4},{12,8},{14,12},{10,14},{6,10},{2,6},{0,2},{5,1},{9,5},... | collective-permute-start | bytes 591368 | tf_op jit(solution)/shard_map/ppermute | solution.py:467
  24.6 7.9 %collective-permute-start.15 = (f32[385,1,128]{2,1,0:T(1,128)S(1)}, f32[385,1,128]{2,1,0:T(1,128)S(1)}, u32[]{:S(2)}, u32[]{:S(2)}) collective-permute-start(f32[385,1,128]{2,1,0:T(1,128)S(1)} %collective-permute-done.14.refs_6_), channel_id=1, source_target_pairs={{0,4},{4,8},{8,12},{12,14},{14,10},{10,6},{6,2},{2,0},{1,5},{5,9},... | collective-permute-start | bytes 591368 | tf_op jit(solution)/shard_map/ppermute | solution.py:482
  26.1 7.9 %collective-permute-start.13 = (f32[385,1,128]{2,1,0:T(1,128)S(1)}, f32[385,1,128]{2,1,0:T(1,128)S(1)}, u32[]{:S(2)}, u32[]{:S(2)}) collective-permute-start(f32[385,1,128]{2,1,0:T(1,128)S(1)} %collective-permute-done.11.refs_5_), channel_id=1, source_target_pairs={{4,0},{8,4},{12,8},{14,12},{10,14},{6,10},{2,6},{0,2},{5,1},{9,5},... | collective-permute-start | bytes 591368 | tf_op jit(solution)/shard_map/ppermute | solution.py:481
  26.7 8.7 %collective-permute-start.9 = (f32[385,1,128]{2,1,0:T(1,128)S(1)}, f32[385,1,128]{2,1,0:T(1,128)S(1)}, u32[]{:S(2)}, u32[]{:S(2)}) collective-permute-start(f32[385,1,128]{2,1,0:T(1,128)S(1)} %collective-permute-done.8.refs_7_), channel_id=1, source_target_pairs={{0,4},{4,8},{8,12},{12,14},{14,10},{10,6},{6,2},{2,0},{1,5},{5,9},... | collective-permute-start | bytes 591368 | tf_op jit(solution)/shard_map/ppermute | solution.py:466
  28.8 7.7 %collective-permute-start.5 = (f32[385,1,128]{2,1,0:T(1,128)S(1)}, f32[385,1,128]{2,1,0:T(1,128)S(1)}, u32[]{:S(2)}, u32[]{:S(2)}) collective-permute-start(f32[385,1,128]{2,1,0:T(1,128)S(1)} %collective-permute-done.4.refs_8_), channel_id=1, source_target_pairs={{4,0},{8,4},{12,8},{14,12},{10,14},{6,10},{2,6},{0,2},{5,1},{9,5},... | collective-permute-start | bytes 591368 | tf_op jit(solution)/shard_map/ppermute | solution.py:467

commit v5 on v4

--- a/solution.py
+++ b/solution.py
@@ -144,10 +144,6 @@
 GRANT = pltpu.CompilerParams(vmem_limit_bytes=VMEM_GRANT)
 
 
-def small_cost(microseconds):
-    return pl.CostEstimate(flops=0, bytes_accessed=int(3.7e6 * microseconds), transcendentals=0)
-
-
 def start_all(pairs, sems):
     copies = [pltpu.make_async_copy(src, dst, sems.at[n]) for n, (src, dst) in enumerate(pairs)]
     for copy in copies:
@@ -196,7 +192,6 @@
         out_specs=(VMEM_SPEC,) * 2,
         scratch_shapes=[pltpu.SMEM(index.shape, jnp.int32), pltpu.SemaphoreType.DMA((3,))],
         compiler_params=GRANT,
-        cost_estimate=small_cost(1),
     )(in_hbm(index), in_hbm(blocks))
 
 
@@ -291,7 +286,6 @@
             pltpu.SemaphoreType.DMA,
         ],
         compiler_params=GRANT,
-        cost_estimate=small_cost(2),
     )(*map(in_hbm, held), in_hbm(own), in_vmem(twin))
 
 
@@ -432,7 +426,6 @@
         ],
         input_output_aliases=aliases,
         compiler_params=GRANT,
-        cost_estimate=small_cost(2),
     )(*operands)
 
 

time: 38.4 us -> 37.7 us (0.982); the launches traced: 37.9 us -> 37.9 us
    ppermute x4, waiting for transfers between devices: 4.66 us -> 5.21 us  [ring_plan(): a_fwd = lax.ppermute(a_fwd, 'row', forward)]
    ppermute x4, waiting for transfers between devices: 0.8 us -> 0.28 us  [ring_plan(): b_bwd = lax.ppermute(b_bwd, 'row', backward)]
  transfers between devices with their start and end apart: 16 -> 16, of which waited for: 10 -> 11; matrix products, arithmetic and copies ran while one was open for 0% -> 0% of each run, Pallas kernels for 22% -> 22%
where the time goes in v5:
time: 37.7 us; the launch traced here: 37.9 us
  starting transfers between devices  15.2 us (40%)
  waiting for transfers between devices  13 us (34%)
  Pallas kernels  9.6 us (25%)
    ppermute x4, starting transfers between devices, ring_plan(): a_fwd = lax.ppermute(a_fwd, 'row', forward)  8.62 us
    pallas_call x5, Pallas kernels, add_products(): pl.pallas_call(functools.partial(product_kernel, (*sizes, limit, pieces,...  6.57 us
    ppermute x3, starting transfers between devices, ring_plan(): b_fwd = lax.ppermute(b_fwd, 'row', forward)  5.59 us
    ppermute x4, waiting for transfers between devices, ring_plan(): a_fwd = lax.ppermute(a_fwd, 'row', forward)  5.21 us
    ppermute x3, waiting for transfers between devices, ring_plan(): a_bwd = lax.ppermute(a_bwd, 'row', backward)  3.65 us
    ppermute x3, waiting for transfers between devices, ring_plan(): b_fwd = lax.ppermute(b_fwd, 'row', forward)  2.54 us
    pallas_call x1, Pallas kernels, prepare_window(): pl.pallas_call(functools.partial(window_kernel, half_cols), out_shape=(pl...  1.97 us
    ppermute x1, waiting for transfers between devices, ring_plan(): places_twin = lax.ppermute(ks_index, 'col', twins)  1.35 us
  transfers between devices with their start and end apart: 16, of which 11 were waited for; matrix products, arithmetic and copies ran while one was open for 0% of the time, Pallas kernels for 22%

profile of v5, /device:TPU:0, one launch (start us, length us, event | category | flops | bytes accessed | tf_op | source)
XLA Modules:
  0.0 37.9 jit_solution(14327371454808536636)
XLA Ops:
  0.0 0.5 %collective-permute-start.1 = (f32[20,128,128]{2,1,0:T(8,128)}, f32[20,128,128]{2,1,0:T(8,128)S(1)}, u32[]{:S(2)}, u32[]{:S(2)}) collective-permute-start(f32[20,128,128]{2,1,0:T(8,128)} %bitcast.4), channel_id=1, source_target_pairs={{0,1},{1,0},{2,3},{3,2},{4,5},{5,4},{6,7},{7,6},{8,9},{9,8},{10,11... | collective-permute-start | bytes 3932168 | tf_op jit(solution)/shard_map/ppermute | solution.py:452
  0.5 1.0 %shard_map.65 = (f32[385,1,128]{2,1,0:T(1,128)S(1)}, f32[385,1,128]{2,1,0:T(1,128)S(1)}) custom-call(s32[1,1,2,6]{3,2,1,0:T(2,128)} %bitcast.7, f32[768,128]{1,0:T(8,128)} %bitcast.6), custom_call_target="tpu_custom_call" | custom-call | tf_op jit(solution)/shard_map/pallas_call | solution.py:185
  1.5 2.6 %collective-permute-start.6 = (f32[385,1,128]{2,1,0:T(1,128)S(1)}, f32[385,1,128]{2,1,0:T(1,128)S(1)}, u32[]{:S(2)}, u32[]{:S(2)}) collective-permute-start(f32[385,1,128]{2,1,0:T(1,128)S(1)} %get-tuple-element.26.refs_3_), channel_id=1, source_target_pairs={{0,4},{4,8},{8,12},{12,14},{14,10},{10,6},{6,2},{2,0},{1,5},{5,9},... | collective-permute-start | bytes 591368 | tf_op jit(solution)/shard_map/ppermute | solution.py:459
  4.1 0.0 collective-permute-start.2
  4.1 2.0 %collective-permute-start.12 = (f32[385,1,128]{2,1,0:T(1,128)S(1)}, f32[385,1,128]{2,1,0:T(1,128)S(1)}, u32[]{:S(2)}, u32[]{:S(2)}) collective-permute-start(f32[385,1,128]{2,1,0:T(1,128)S(1)} %get-tuple-element.25.refs_4_), channel_id=1, source_target_pairs={{0,4},{4,8},{8,12},{12,14},{14,10},{10,6},{6,2},{2,0},{1,5},{5,9},... | collective-permute-start | bytes 591368 | tf_op jit(solution)/shard_map/ppermute | solution.py:475
  6.2 0.0 collective-permute-start
  6.2 1.3 %collective-permute-done.refs_2_ = s32[1,2,10]{2,1,0:T(2,128)S(1)} collective-permute-done((s32[1,2,10]{2,1,0:T(2,128)}, s32[1,2,10]{2,1,0:T(2,128)S(1)}, u32[]{:S(2)}, u32[]{:S(2)}) %collective-permute-start) | collective-permute-done | bytes 112 | tf_op jit(solution)/shard_map/ppermute | solution.py:453
  7.5 0.0 copy-start
  7.5 0.0 collective-permute-start.10
  7.5 2.3 %collective-permute-done.6.refs_5_ = f32[385,1,128]{2,1,0:T(1,128)S(1)} collective-permute-done((f32[385,1,128]{2,1,0:T(1,128)S(1)}, f32[385,1,128]{2,1,0:T(1,128)S(1)}, u32[]{:S(2)}, u32[]{:S(2)}) %collective-permute-start.6) | collective-permute-done | bytes 197152 | tf_op jit(solution)/shard_map/ppermute | solution.py:459
  9.8 2.0 %collective-permute-start.7 = (f32[385,1,128]{2,1,0:T(1,128)S(1)}, f32[385,1,128]{2,1,0:T(1,128)S(1)}, u32[]{:S(2)}, u32[]{:S(2)}) collective-permute-start(f32[385,1,128]{2,1,0:T(1,128)S(1)} %collective-permute-done.6.refs_5_), channel_id=1, source_target_pairs={{0,4},{4,8},{8,12},{12,14},{14,10},{10,6},{6,2},{2,0},{1,5},{5,9},... | collective-permute-start | bytes 591368 | tf_op jit(solution)/shard_map/ppermute | solution.py:459
  11.8 0.0 collective-permute-done.2.refs_6_
  11.9 0.0 collective-permute-start.3
  11.9 0.0 collective-permute-done.1.refs_5_
  11.9 0.0 copy-done
  11.9 2.0 %shard_map.64 = (bf16[40,128,256]{2,1,0:T(8,128)(2,1)S(1)}, f32[40,1,128]{2,1,0:T(1,128)S(1)}, f32[8,128]{1,0:T(8,128)S(1)}) custom-call(s32[32]{0:T(128)} %refs_0_.1, s32[1,2,10]{2,1,0:T(2,128)} %refs_1_.1, s32[1,2,10]{2,1,0:T(2,128)} %copy-done, s32[1,1,16]{2,1,0:T(1,128)} %refs_3_.1, f32[20,128,128]{2,1,0:T(8,128)} %bitcast.5, ...), custom_call_target="tpu_custom_call" | custom-call | tf_op jit(solution)/shard_map/pallas_call | solution.py:270
  13.9 0.2 collective-permute-done.12.refs_8_
  14.1 2.0 %collective-permute-start.14 = (f32[385,1,128]{2,1,0:T(1,128)S(1)}, f32[385,1,128]{2,1,0:T(1,128)S(1)}, u32[]{:S(2)}, u32[]{:S(2)}) collective-permute-start(f32[385,1,128]{2,1,0:T(1,128)S(1)} %collective-permute-done.12.refs_8_), channel_id=1, source_target_pairs={{0,4},{4,8},{8,12},{12,14},{14,10},{10,6},{6,2},{2,0},{1,5},{5,9},... | collective-permute-start | bytes 591368 | tf_op jit(solution)/shard_map/ppermute | solution.py:475
  16.1 0.0 collective-permute-done.10.refs_7_
  16.1 0.0 collective-permute-start.11
  16.1 2.2 %collective-permute-done.7.refs_3_ = f32[385,1,128]{2,1,0:T(1,128)S(1)} collective-permute-done((f32[385,1,128]{2,1,0:T(1,128)S(1)}, f32[385,1,128]{2,1,0:T(1,128)S(1)}, u32[]{:S(2)}, u32[]{:S(2)}) %collective-permute-start.7) | collective-permute-done | bytes 197152 | tf_op jit(solution)/shard_map/ppermute | solution.py:459
  18.3 2.0 %collective-permute-start.8 = (f32[385,1,128]{2,1,0:T(1,128)S(1)}, f32[385,1,128]{2,1,0:T(1,128)S(1)}, u32[]{:S(2)}, u32[]{:S(2)}) collective-permute-start(f32[385,1,128]{2,1,0:T(1,128)S(1)} %collective-permute-done.7.refs_3_), channel_id=1, source_target_pairs={{0,4},{4,8},{8,12},{12,14},{14,10},{10,6},{6,2},{2,0},{1,5},{5,9},... | collective-permute-start | bytes 591368 | tf_op jit(solution)/shard_map/ppermute | solution.py:459
  20.3 0.0 collective-permute-done.3.refs_4_
  20.3 0.0 collective-permute-start.4
  20.3 1.2 %shard_map.66.refs_9_ = f32[16,128,128]{2,1,0:T(8,128)S(1)} custom-call(f32[8,128]{1,0:T(8,128)S(1)} %get-tuple-element.22.refs_0_, bf16[40,128,256]{2,1,0:T(8,128)(2,1)S(1)} %get-tuple-element.23.refs_1_, f32[40,1,128]{2,1,0:T(1,128)S(1)} %get-tuple-element.24.refs_2_, f32[385,1,128]{2,1,0:T(1,128)S(1)} %get-tuple-element.26.refs_3_, ...), custom_call_target="tpu_custom_call" | custom-call | tf_op jit(solution)/shard_map/pallas_call | solution.py:416
  21.6 0.9 %collective-permute-done.14.refs_6_ = f32[385,1,128]{2,1,0:T(1,128)S(1)} collective-permute-done((f32[385,1,128]{2,1,0:T(1,128)S(1)}, f32[385,1,128]{2,1,0:T(1,128)S(1)}, u32[]{:S(2)}, u32[]{:S(2)}) %collective-permute-start.14) | collective-permute-done | bytes 197152 | tf_op jit(solution)/shard_map/ppermute | solution.py:475
  22.5 2.0 %collective-permute-done.11.refs_5_ = f32[385,1,128]{2,1,0:T(1,128)S(1)} collective-permute-done((f32[385,1,128]{2,1,0:T(1,128)S(1)}, f32[385,1,128]{2,1,0:T(1,128)S(1)}, u32[]{:S(2)}, u32[]{:S(2)}) %collective-permute-start.11) | collective-permute-done | bytes 197152 | tf_op jit(solution)/shard_map/ppermute | solution.py:474
  24.6 1.6 %collective-permute-start.15 = (f32[385,1,128]{2,1,0:T(1,128)S(1)}, f32[385,1,128]{2,1,0:T(1,128)S(1)}, u32[]{:S(2)}, u32[]{:S(2)}) collective-permute-start(f32[385,1,128]{2,1,0:T(1,128)S(1)} %collective-permute-done.14.refs_6_), channel_id=1, source_target_pairs={{0,4},{4,8},{8,12},{12,14},{14,10},{10,6},{6,2},{2,0},{1,5},{5,9},... | collective-permute-start | bytes 591368 | tf_op jit(solution)/shard_map/ppermute | solution.py:475
  26.1 0.4 %collective-permute-start.13 = (f32[385,1,128]{2,1,0:T(1,128)S(1)}, f32[385,1,128]{2,1,0:T(1,128)S(1)}, u32[]{:S(2)}, u32[]{:S(2)}) collective-permute-start(f32[385,1,128]{2,1,0:T(1,128)S(1)} %collective-permute-done.11.refs_5_), channel_id=1, source_target_pairs={{4,0},{8,4},{12,8},{14,12},{10,14},{6,10},{2,6},{0,2},{5,1},{9,5},... | collective-permute-start | bytes 591368 | tf_op jit(solution)/shard_map/ppermute | solution.py:474
  26.6 0.2 collective-permute-done.8.refs_7_
  26.7 2.0 %collective-permute-start.9 = (f32[385,1,128]{2,1,0:T(1,128)S(1)}, f32[385,1,128]{2,1,0:T(1,128)S(1)}, u32[]{:S(2)}, u32[]{:S(2)}) collective-permute-start(f32[385,1,128]{2,1,0:T(1,128)S(1)} %collective-permute-done.8.refs_7_), channel_id=1, source_target_pairs={{0,4},{4,8},{8,12},{12,14},{14,10},{10,6},{6,2},{2,0},{1,5},{5,9},... | collective-permute-start | bytes 591368 | tf_op jit(solution)/shard_map/ppermute | solution.py:459
  28.7 0.0 collective-permute-done.4.refs_8_
  28.8 0.0 collective-permute-start.5
  28.8 2.2 %shard_map.67 = (f32[16,128,128]{2,1,0:T(8,128)S(1)}, f32[16,128,128]{2,1,0:T(8,128)}) custom-call(f32[8,128]{1,0:T(8,128)S(1)} %get-tuple-element.22.refs_0_, bf16[40,128,256]{2,1,0:T(8,128)(2,1)S(1)} %get-tuple-element.23.refs_1_, f32[40,1,128]{2,1,0:T(1,128)S(1)} %get-tuple-element.24.refs_2_, ...), custom_call_target="tpu_custom_call", output_to_operand_aliasing={{0}: (9, {})} | custom-call | tf_op jit(solution)/shard_map/pallas_call | solution.py:416
  31.0 1.4 %collective-permute-done.15.refs_4_ = f32[385,1,128]{2,1,0:T(1,128)S(1)} collective-permute-done((f32[385,1,128]{2,1,0:T(1,128)S(1)}, f32[385,1,128]{2,1,0:T(1,128)S(1)}, u32[]{:S(2)}, u32[]{:S(2)}) %collective-permute-start.15) | collective-permute-done | bytes 197152 | tf_op jit(solution)/shard_map/ppermute | solution.py:475
  32.4 1.6 %collective-permute-done.13.refs_3_ = f32[385,1,128]{2,1,0:T(1,128)S(1)} collective-permute-done((f32[385,1,128]{2,1,0:T(1,128)S(1)}, f32[385,1,128]{2,1,0:T(1,128)S(1)}, u32[]{:S(2)}, u32[]{:S(2)}) %collective-permute-start.13) | collective-permute-done | bytes 197152 | tf_op jit(solution)/shard_map/ppermute | solution.py:474
  34.0 0.5 %shard_map.68 = (f32[16,128,128]{2,1,0:T(8,128)S(1)}, f32[16,128,128]{2,1,0:T(8,128)}) custom-call(f32[8,128]{1,0:T(8,128)S(1)} %get-tuple-element.22.refs_0_, bf16[40,128,256]{2,1,0:T(8,128)(2,1)S(1)} %get-tuple-element.23.refs_1_, f32[40,1,128]{2,1,0:T(1,128)S(1)} %get-tuple-element.24.refs_2_, ...), custom_call_target="tpu_custom_call", output_to_operand_aliasing={{0}: (5, {}), {1}: (6, {})} | custom-call | tf_op jit(solution)/shard_map/pallas_call | solution.py:416
  34.5 0.6 %collective-permute-done.9.refs_3_ = f32[385,1,128]{2,1,0:T(1,128)S(1)} collective-permute-done((f32[385,1,128]{2,1,0:T(1,128)S(1)}, f32[385,1,128]{2,1,0:T(1,128)S(1)}, u32[]{:S(2)}, u32[]{:S(2)}) %collective-permute-start.9) | collective-permute-done | bytes 197152 | tf_op jit(solution)/shard_map/ppermute | solution.py:459
  35.0 1.3 %shard_map.69 = (f32[16,128,128]{2,1,0:T(8,128)S(1)}, f32[16,128,128]{2,1,0:T(8,128)}) custom-call(f32[8,128]{1,0:T(8,128)S(1)} %get-tuple-element.22.refs_0_, bf16[40,128,256]{2,1,0:T(8,128)(2,1)S(1)} %get-tuple-element.23.refs_1_, f32[40,1,128]{2,1,0:T(1,128)S(1)} %get-tuple-element.24.refs_2_, ...), custom_call_target="tpu_custom_call", output_to_operand_aliasing={{0}: (4, {}), {1}: (5, {})} | custom-call | tf_op jit(solution)/shard_map/pallas_call | solution.py:416
  36.4 0.2 collective-permute-done.5.refs_3_
  36.5 1.3 %shard_map.70 = (f32[16,128,128]{2,1,0:T(8,128)S(1)}, f32[16,128,128]{2,1,0:T(8,128)}) custom-call(f32[8,128]{1,0:T(8,128)S(1)} %get-tuple-element.22.refs_0_, bf16[40,128,256]{2,1,0:T(8,128)(2,1)S(1)} %get-tuple-element.23.refs_1_, f32[40,1,128]{2,1,0:T(1,128)S(1)} %get-tuple-element.24.refs_2_, ...), custom_call_target="tpu_custom_call", output_to_operand_aliasing={{0}: (4, {}), {1}: (5, {})} | custom-call | tf_op jit(solution)/shard_map/pallas_call | solution.py:416
Async XLA Ops:
  0.0 11.9 %collective-permute-start.1 = (f32[20,128,128]{2,1,0:T(8,128)}, f32[20,128,128]{2,1,0:T(8,128)S(1)}, u32[]{:S(2)}, u32[]{:S(2)}) collective-permute-start(f32[20,128,128]{2,1,0:T(8,128)} %bitcast.4), channel_id=1, source_target_pairs={{0,1},{1,0},{2,3},{3,2},{4,5},{5,4},{6,7},{7,6},{8,9},{9,8},{10,11... | collective-permute-start | bytes 3932168 | tf_op jit(solution)/shard_map/ppermute | solution.py:452
  1.5 8.3 %collective-permute-start.6 = (f32[385,1,128]{2,1,0:T(1,128)S(1)}, f32[385,1,128]{2,1,0:T(1,128)S(1)}, u32[]{:S(2)}, u32[]{:S(2)}) collective-permute-start(f32[385,1,128]{2,1,0:T(1,128)S(1)} %get-tuple-element.26.refs_3_), channel_id=1, source_target_pairs={{0,4},{4,8},{8,12},{12,14},{14,10},{10,6},{6,2},{2,0},{1,5},{5,9},... | collective-permute-start | bytes 591368 | tf_op jit(solution)/shard_map/ppermute | solution.py:459
  4.1 7.7 %collective-permute-start.2 = (f32[385,1,128]{2,1,0:T(1,128)S(1)}, f32[385,1,128]{2,1,0:T(1,128)S(1)}, u32[]{:S(2)}, u32[]{:S(2)}) collective-permute-start(f32[385,1,128]{2,1,0:T(1,128)S(1)} %get-tuple-element.25.refs_4_), channel_id=1, source_target_pairs={{4,0},{8,4},{12,8},{14,12},{10,14},{6,10},{2,6},{0,2},{5,1},{9,5},... | collective-permute-start | bytes 591368 | tf_op jit(solution)/shard_map/ppermute | solution.py:460
  4.1 9.9 %collective-permute-start.12 = (f32[385,1,128]{2,1,0:T(1,128)S(1)}, f32[385,1,128]{2,1,0:T(1,128)S(1)}, u32[]{:S(2)}, u32[]{:S(2)}) collective-permute-start(f32[385,1,128]{2,1,0:T(1,128)S(1)} %get-tuple-element.25.refs_4_), channel_id=1, source_target_pairs={{0,4},{4,8},{8,12},{12,14},{14,10},{10,6},{6,2},{2,0},{1,5},{5,9},... | collective-permute-start | bytes 591368 | tf_op jit(solution)/shard_map/ppermute | solution.py:475
  6.2 1.4 %collective-permute-start = (s32[1,2,10]{2,1,0:T(2,128)}, s32[1,2,10]{2,1,0:T(2,128)S(1)}, u32[]{:S(2)}, u32[]{:S(2)}) collective-permute-start(s32[1,2,10]{2,1,0:T(2,128)} %refs_1_.1), channel_id=1, source_target_pairs={{0,1},{1,0},{2,3},{3,2},{4,5},{5,4},{6,7},{7,6},{8,9},{9,8},{10,11... | collective-permute-start | bytes 248 | tf_op jit(solution)/shard_map/ppermute | solution.py:453
  7.5 4.4 %copy-start = (s32[1,2,10]{2,1,0:T(2,128)}, s32[1,2,10]{2,1,0:T(2,128)S(1)}, u32[]{:S(2)}) copy-start(s32[1,2,10]{2,1,0:T(2,128)S(1)} %collective-permute-done.refs_2_) | copy-start | bytes 244
  7.5 8.6 %collective-permute-start.10 = (f32[385,1,128]{2,1,0:T(1,128)S(1)}, f32[385,1,128]{2,1,0:T(1,128)S(1)}, u32[]{:S(2)}, u32[]{:S(2)}) collective-permute-start(f32[385,1,128]{2,1,0:T(1,128)S(1)} %get-tuple-element.26.refs_3_), channel_id=1, source_target_pairs={{4,0},{8,4},{12,8},{14,12},{10,14},{6,10},{2,6},{0,2},{5,1},{9,5},... | collective-permute-start | bytes 591368 | tf_op jit(solution)/shard_map/ppermute | solution.py:474
  9.8 8.4 %collective-permute-start.7 = (f32[385,1,128]{2,1,0:T(1,128)S(1)}, f32[385,1,128]{2,1,0:T(1,128)S(1)}, u32[]{:S(2)}, u32[]{:S(2)}) collective-permute-start(f32[385,1,128]{2,1,0:T(1,128)S(1)} %collective-permute-done.6.refs_5_), channel_id=1, source_target_pairs={{0,4},{4,8},{8,12},{12,14},{14,10},{10,6},{6,2},{2,0},{1,5},{5,9},... | collective-permute-start | bytes 591368 | tf_op jit(solution)/shard_map/ppermute | solution.py:459
  11.9 8.4 %collective-permute-start.3 = (f32[385,1,128]{2,1,0:T(1,128)S(1)}, f32[385,1,128]{2,1,0:T(1,128)S(1)}, u32[]{:S(2)}, u32[]{:S(2)}) collective-permute-start(f32[385,1,128]{2,1,0:T(1,128)S(1)} %collective-permute-done.2.refs_6_), channel_id=1, source_target_pairs={{4,0},{8,4},{12,8},{14,12},{10,14},{6,10},{2,6},{0,2},{5,1},{9,5},... | collective-permute-start | bytes 591368 | tf_op jit(solution)/shard_map/ppermute | solution.py:460
  14.1 8.4 %collective-permute-start.14 = (f32[385,1,128]{2,1,0:T(1,128)S(1)}, f32[385,1,128]{2,1,0:T(1,128)S(1)}, u32[]{:S(2)}, u32[]{:S(2)}) collective-permute-start(f32[385,1,128]{2,1,0:T(1,128)S(1)} %collective-permute-done.12.refs_8_), channel_id=1, source_target_pairs={{0,4},{4,8},{8,12},{12,14},{14,10},{10,6},{6,2},{2,0},{1,5},{5,9},... | collective-permute-start | bytes 591368 | tf_op jit(solution)/shard_map/ppermute | solution.py:475
  16.1 8.4 %collective-permute-start.11 = (f32[385,1,128]{2,1,0:T(1,128)S(1)}, f32[385,1,128]{2,1,0:T(1,128)S(1)}, u32[]{:S(2)}, u32[]{:S(2)}) collective-permute-start(f32[385,1,128]{2,1,0:T(1,128)S(1)} %collective-permute-done.10.refs_7_), channel_id=1, source_target_pairs={{4,0},{8,4},{12,8},{14,12},{10,14},{6,10},{2,6},{0,2},{5,1},{9,5},... | collective-permute-start | bytes 591368 | tf_op jit(solution)/shard_map/ppermute | solution.py:474
  18.3 8.4 %collective-permute-start.8 = (f32[385,1,128]{2,1,0:T(1,128)S(1)}, f32[385,1,128]{2,1,0:T(1,128)S(1)}, u32[]{:S(2)}, u32[]{:S(2)}) collective-permute-start(f32[385,1,128]{2,1,0:T(1,128)S(1)} %collective-permute-done.7.refs_3_), channel_id=1, source_target_pairs={{0,4},{4,8},{8,12},{12,14},{14,10},{10,6},{6,2},{2,0},{1,5},{5,9},... | collective-permute-start | bytes 591368 | tf_op jit(solution)/shard_map/ppermute | solution.py:459
  20.3 8.4 %collective-permute-start.4 = (f32[385,1,128]{2,1,0:T(1,128)S(1)}, f32[385,1,128]{2,1,0:T(1,128)S(1)}, u32[]{:S(2)}, u32[]{:S(2)}) collective-permute-start(f32[385,1,128]{2,1,0:T(1,128)S(1)} %collective-permute-done.3.refs_4_), channel_id=1, source_target_pairs={{4,0},{8,4},{12,8},{14,12},{10,14},{6,10},{2,6},{0,2},{5,1},{9,5},... | collective-permute-start | bytes 591368 | tf_op jit(solution)/shard_map/ppermute | solution.py:460
  24.6 7.9 %collective-permute-start.15 = (f32[385,1,128]{2,1,0:T(1,128)S(1)}, f32[385,1,128]{2,1,0:T(1,128)S(1)}, u32[]{:S(2)}, u32[]{:S(2)}) collective-permute-start(f32[385,1,128]{2,1,0:T(1,128)S(1)} %collective-permute-done.14.refs_6_), channel_id=1, source_target_pairs={{0,4},{4,8},{8,12},{12,14},{14,10},{10,6},{6,2},{2,0},{1,5},{5,9},... | collective-permute-start | bytes 591368 | tf_op jit(solution)/shard_map/ppermute | solution.py:475
  26.1 7.9 %collective-permute-start.13 = (f32[385,1,128]{2,1,0:T(1,128)S(1)}, f32[385,1,128]{2,1,0:T(1,128)S(1)}, u32[]{:S(2)}, u32[]{:S(2)}) collective-permute-start(f32[385,1,128]{2,1,0:T(1,128)S(1)} %collective-permute-done.11.refs_5_), channel_id=1, source_target_pairs={{4,0},{8,4},{12,8},{14,12},{10,14},{6,10},{2,6},{0,2},{5,1},{9,5},... | collective-permute-start | bytes 591368 | tf_op jit(solution)/shard_map/ppermute | solution.py:474
  26.7 8.3 %collective-permute-start.9 = (f32[385,1,128]{2,1,0:T(1,128)S(1)}, f32[385,1,128]{2,1,0:T(1,128)S(1)}, u32[]{:S(2)}, u32[]{:S(2)}) collective-permute-start(f32[385,1,128]{2,1,0:T(1,128)S(1)} %collective-permute-done.8.refs_7_), channel_id=1, source_target_pairs={{0,4},{4,8},{8,12},{12,14},{14,10},{10,6},{6,2},{2,0},{1,5},{5,9},... | collective-permute-start | bytes 591368 | tf_op jit(solution)/shard_map/ppermute | solution.py:459
  28.8 7.7 %collective-permute-start.5 = (f32[385,1,128]{2,1,0:T(1,128)S(1)}, f32[385,1,128]{2,1,0:T(1,128)S(1)}, u32[]{:S(2)}, u32[]{:S(2)}) collective-permute-start(f32[385,1,128]{2,1,0:T(1,128)S(1)} %collective-permute-done.4.refs_8_), channel_id=1, source_target_pairs={{4,0},{8,4},{12,8},{14,12},{10,14},{6,10},{2,6},{0,2},{5,1},{9,5},... | collective-permute-start | bytes 591368 | tf_op jit(solution)/shard_map/ppermute | solution.py:460

commit v6 on v5

--- a/solution.py
+++ b/solution.py
@@ -141,6 +141,7 @@
 
 VMEM_SPEC = pl.BlockSpec(memory_space=pltpu.VMEM)
 HBM_SPEC = pl.BlockSpec(memory_space=pltpu.HBM)
+SMEM_SPEC = pl.BlockSpec(memory_space=pltpu.SMEM)
 GRANT = pltpu.CompilerParams(vmem_limit_bytes=VMEM_GRANT)
 
 
@@ -155,7 +156,7 @@
     return ref.at[pl.ds(0, rows)].reshape(rows, ref.shape[2])
 
 
-def pack_kernel(lead, index_ref, blocks_ref, lead_ref, rest_ref, index, sems):
+def pack_kernel(index_ref, blocks_ref, lead_ref, rest_ref, index, sems):
     slots = index.shape[3]
     lead_rows, rest_rows = lead_ref.shape[0] - 1, rest_ref.shape[0] - 1
     copies = start_all(
@@ -168,12 +169,12 @@
     )
     lane = lax.broadcasted_iota(jnp.int32, lead_ref.shape[1:], 1)
     copies[0].wait()
-    for ref, rows, first, count in ((lead_ref, lead_rows, 0, lead), (rest_ref, rest_rows, lead, slots - lead)):
-        labels = jnp.zeros(ref.shape[1:], jnp.int32)
-        for n in range(count):
-            for field in range(2):
-                labels = jnp.where(lane == 2 * n + field, index[0, 0, field, first + n], labels)
-        ref[rows] = labels.astype(jnp.float32)
+    labels = jnp.zeros(lane.shape, jnp.int32)
+    for n in range(slots):
+        for field in range(2):
+            labels = jnp.where(lane == 2 * n + field, index[0, 0, field, n], labels)
+    lead_ref[lead_rows] = labels.astype(jnp.float32)
+    rest_ref[rest_rows] = labels.astype(jnp.float32)
     for copy in copies[1:]:
         copy.wait()
 
@@ -183,7 +184,7 @@
     rows, width = blocks.shape
     lead_rows = rows // slots * lead
     return pl.pallas_call(
-        functools.partial(pack_kernel, lead),
+        pack_kernel,
         out_shape=(
             pltpu.VMEM((lead_rows + 1, 1, width), jnp.float32),
             pltpu.VMEM((rows - lead_rows + 1, 1, width), jnp.float32),
@@ -290,7 +291,9 @@
 
 
 def product_kernel(config, *refs):
-    block_rows, half_cols, limit, pieces, first, final = config
+    block_rows, half_cols, limit, pieces, first, final, ahead, planned = config
+    if planned:
+        plan_ref, *refs = refs
     table_ref, parts_ref, norms_ref = refs[:3]
     chunk_refs = refs[3 : 3 + len(pieces)]
     rest = refs[3 + len(pieces) + (not first) + (final == "touched") :]
@@ -298,6 +301,9 @@
     if final:
         out_ref = rest[1]
         rest = rest[1:]
+    if ahead:
+        next_ref = rest[1]
+        rest = rest[1:]
     listed, touched, held, out_sems = rest[1:]
     block_size = c_ref.shape[-1]
     slot_bits, target_bits = field_bits(parts_ref.shape[0]), field_bits(c_ref.shape[0])
@@ -311,7 +317,7 @@
         c_ref[...] = jnp.zeros_like(c_ref)
 
     lane = lax.broadcasted_iota(jnp.int32, (1, block_size), 1).astype(jnp.float32)
-    label_rows = -(-max(pieces) // 8) * 8
+    label_rows = -(-max(sum(piece) for piece in (*pieces, ahead or (0, 0))) // 8) * 8
     line = lax.broadcasted_iota(jnp.int32, (label_rows, 1), 0).astype(jnp.float32)
     slot_lines = lines_of(block_rows, block_size)
     target_lines = lines_of(half_cols, block_size)
@@ -324,36 +330,63 @@
             found += jnp.sum(jnp.where(hit, entries, 0.0), axis=1, keepdims=True)
         return found
 
-    read = []
-    for chunk_ref, blocks in zip(chunk_refs, pieces):
-        labels = jnp.broadcast_to(chunk_ref[blocks * block_size], (label_rows, block_size))
-        block_row, column = (
-            jnp.sum(jnp.where(lane == 2.0 * line + float(field), labels, 0.0), axis=1, keepdims=True)
-            for field in range(2)
-        )
-        slot = look_up(block_row, 0, slot_lines).astype(jnp.int32)
-        target = look_up(column, slot_lines, target_lines).astype(jnp.int32)
-        blocks_ref = matrix_of(chunk_ref, blocks * block_size)
-        read += [(blocks_ref, b, slot[b, 0], target[b, 0]) for b in range(blocks)]
-    pairs, kept = jnp.int32(0), jnp.int32(0)
-    for blocks_ref, b, slots, targets in read:
-        before = pairs
+    def enlist(at, pairs, slots, targets, block):
         for i in range(BR):
             ks = (slots >> (slot_bits * i)) & no_slot
             target = (targets >> (target_bits * i)) & no_target
-            listed[pairs] = ks | (target << slot_bits) | (kept << code_bits)
+            at[pairs] = ks | (target << slot_bits) | (block << code_bits)
             pairs = pairs + ((ks != no_slot) & (target != no_target)).astype(jnp.int32)
-        held[kept] = blocks_ref[pl.ds(b * block_size, block_size), :]
-        kept = kept + (pairs > before).astype(jnp.int32)
-    for u in range(UNROLL):
-        listed[pairs + u] = 0
+        return pairs
+
+    def fill(at, pairs):
+        for u in range(UNROLL):
+            at[pairs + u] = 0
+
+    if planned:
+        listed = plan_ref
+        pairs = plan_ref[plan_ref.shape[0] - 1]
+        only_block = matrix_of(chunk_refs[0], pieces[0][0] * block_size)
+
+        def density_at(slot):
+            return only_block[pl.ds(pl.multiple_of(slot * block_size, block_size), block_size), :]
+    else:
+
+        def density_at(slot):
+            return held[slot]
+
+        read = []
+        for chunk_ref, (blocks, offset) in zip(chunk_refs, pieces):
+            labels = jnp.broadcast_to(chunk_ref[blocks * block_size], (label_rows, block_size))
+            block_row, column = (
+                jnp.sum(jnp.where(lane == 2.0 * line + float(field), labels, 0.0), axis=1, keepdims=True)
+                for field in range(2)
+            )
+            slot = look_up(block_row, 0, slot_lines).astype(jnp.int32)
+            target = look_up(column, slot_lines, target_lines).astype(jnp.int32)
+            blocks_ref = matrix_of(chunk_ref, blocks * block_size)
+            read += [(blocks_ref, b, slot[offset + b, 0], target[offset + b, 0]) for b in range(blocks)]
+        if ahead:
+            later = [(b, slot[ahead[1] + b, 0], target[ahead[1] + b, 0]) for b in range(ahead[0])]
+        pairs, kept = jnp.int32(0), jnp.int32(0)
+        for blocks_ref, b, slots, targets in read:
+            before = pairs
+            pairs = enlist(listed, pairs, slots, targets, kept)
+            held[kept] = blocks_ref[pl.ds(b * block_size, block_size), :]
+            kept = kept + (pairs > before).astype(jnp.int32)
+        fill(listed, pairs)
+        if ahead:
+            next_pairs = jnp.int32(0)
+            for b, slots, targets in later:
+                next_pairs = enlist(next_ref, next_pairs, slots, targets, b)
+            fill(next_ref, next_pairs)
+            next_ref[next_ref.shape[0] - 1] = next_pairs
 
     def multiply(step, _):
         for u in range(UNROLL):
             at = step * UNROLL + u
             entry = listed[at]
             ks, target, slot = entry & no_slot, target_of(entry), entry >> code_bits
-            density = held[slot]
+            density = density_at(slot)
             bound = jnp.where(at < pairs, limit, jnp.inf)
             keep = norms_ref[ks] * norm_of(density) >= bound
             high, low = split_bf16(density)
@@ -393,15 +426,17 @@
         each_target(lambda copy: copy.wait(), 1, 2)
 
 
-def add_products(sizes, window, accumulated, group, shape, final=None, written=None):
+def add_products(sizes, window, accumulated, group, shape, final=None, written=None, ahead=None, plan=None):
     block_size = shape[-1]
     limit = FILTER * block_size * math.sqrt(block_size)
     first = accumulated is None
-    pieces = [count for count, _ in group]
-    chunks = [chunk for _, chunk in group]
-    blocks = sum(pieces)
+    pieces = [piece[:2] for piece in group]
+    chunks = [piece[2] for piece in group]
+    blocks = sum(count for count, _ in pieces)
     parts, norms, table = window
     operands = [*map(in_vmem, (table, parts, norms, *chunks))]
+    if plan is not None:
+        operands.insert(0, pltpu.with_memory_space_constraint(plan, pltpu.SMEM))
     aliases = {}
     if not first:
         aliases = {len(operands): 0}
@@ -410,14 +445,22 @@
         aliases[len(operands)] = 1
         operands.append(in_hbm(written))
     in_specs = [VMEM_SPEC] * (len(operands) - (written is not None)) + [HBM_SPEC] * (written is not None)
+    if plan is not None:
+        in_specs[0] = SMEM_SPEC
     longest = blocks * BR + 2 * UNROLL
     outs = 1 if final is None else 2
     out_shape = [pltpu.VMEM(shape, jnp.float32), pltpu.HBM(shape, jnp.float32)][:outs]
+    out_specs = [VMEM_SPEC, HBM_SPEC][:outs]
+    if ahead:
+        out_shape.append(pltpu.SMEM((ahead[0] * BR + 2 * UNROLL,), jnp.int32))
+        out_specs.append(SMEM_SPEC)
     return pl.pallas_call(
-        functools.partial(product_kernel, (*sizes, limit, pieces, first, final)),
+        functools.partial(
+            product_kernel, (*sizes, limit, pieces, first, final, ahead, plan is not None)
+        ),
         out_shape=out_shape,
         in_specs=in_specs,
-        out_specs=[VMEM_SPEC, HBM_SPEC][:outs],
+        out_specs=out_specs,
         scratch_shapes=[
             pltpu.SMEM((longest,), jnp.int32),
             pltpu.SMEM((shape[0],), jnp.int32),
@@ -453,7 +496,7 @@
     places_twin = lax.ppermute(ks_index, "col", twins)
     window = prepare_window(row_perm, ks_index, places_twin, c_index, ks_own, ks_twin, half_cols)
     accumulated, written = None, []
-    group = [(lead, a_fwd), (slots - lead, b_bwd)]
+    group = [(lead, 0, a_fwd), (slots - lead, lead, b_bwd)]
     half = row_count // 2
     for step in range(1, half + 1):
         a_fwd = lax.ppermute(a_fwd, "row", forward)
@@ -462,7 +505,7 @@
             final = {half - 1: "whole", half: "touched"}.get(step)
             if step == half - 1:
                 (accumulated,) = tied((accumulated,), a_fwd)
-                group += [(lead, a_fwd), (slots - lead, b_bwd)]
+                group += [(lead, 0, a_fwd), (slots - lead, lead, b_bwd)]
             accumulated, *written = add_products(sizes, window, accumulated, group, shape, final, *written)
             group = []
         if step < half:
@@ -474,11 +517,16 @@
             a_bwd = lax.ppermute(a_bwd, "row", backward)
             b_fwd = lax.ppermute(b_fwd, "row", forward)
             if step < half - 1:
-                group += [(lead, a_fwd), (slots - lead, b_bwd)]
-            group += [(lead, a_bwd), (slots - lead, b_fwd)]
-    for group in ([(lead, a_fwd)], [(slots - lead, b_bwd)]):
-        accumulated, *written = add_products(sizes, window, accumulated, group, shape, "touched", *written)
-    return written[0].reshape(c_index.shape + (block_size, block_size))
+                group += [(lead, 0, a_fwd), (slots - lead, lead, b_bwd)]
+            group += [(lead, 0, a_bwd), (slots - lead, lead, b_fwd)]
+    late = (slots - lead, lead)
+    accumulated, *written, plan = add_products(
+        sizes, window, accumulated, [(lead, 0, a_fwd)], shape, "touched", *written, ahead=late
+    )
+    _, total = add_products(
+        sizes, window, accumulated, [(*late, b_bwd)], shape, "touched", *written, plan=plan
+    )
+    return total.reshape(c_index.shape + (block_size, block_size))
 
 
 def on_device(d_blocks, d_index, row_perm, ks_blocks, ks_index, c_index):

time: 37.7 us -> 38.1 us (1.011)
    ppermute x3, waiting for transfers between devices: 2.54 us -> 3.11 us  [ring_plan(): b_fwd = lax.ppermute(b_fwd, 'row', forward)]
    ppermute x4, waiting for transfers between devices: 5.21 us -> 4.66 us  [ring_plan(): a_fwd = lax.ppermute(a_fwd, 'row', forward)]
  transfers between devices with their start and end apart: 16 -> 16, of which waited for: 11 -> 9; matrix products, arithmetic and copies ran while one was open for 0% -> 0% of each run, Pallas kernels for 22% -> 23%
where the time goes in v6:
time: 38.1 us; the launch traced here: 37.9 us
  starting transfers between devices  15.2 us (40%)
  waiting for transfers between devices  12.9 us (34%)
  Pallas kernels  9.76 us (26%)
    ppermute x4, starting transfers between devices, ring_plan(): a_fwd = lax.ppermute(a_fwd, 'row', forward)  8.62 us
    pallas_call x5, Pallas kernels, add_products(): pl.pallas_call(functools.partial(product_kernel, (*sizes, limit, pieces,...  6.73 us
    ppermute x3, starting transfers between devices, ring_plan(): b_fwd = lax.ppermute(b_fwd, 'row', forward)  5.59 us
    ppermute x4, waiting for transfers between devices, ring_plan(): a_fwd = lax.ppermute(a_fwd, 'row', forward)  4.66 us
    ppermute x3, waiting for transfers between devices, ring_plan(): a_bwd = lax.ppermute(a_bwd, 'row', backward)  3.65 us
    ppermute x3, waiting for transfers between devices, ring_plan(): b_fwd = lax.ppermute(b_fwd, 'row', forward)  3.11 us
    pallas_call x1, Pallas kernels, prepare_window(): pl.pallas_call(functools.partial(window_kernel, half_cols), out_shape=(pl...  1.97 us
    ppermute x1, waiting for transfers between devices, ring_plan(): places_twin = lax.ppermute(ks_index, 'col', twins)  1.35 us
  transfers between devices with their start and end apart: 16, of which 9 were waited for; matrix products, arithmetic and copies ran while one was open for 0% of the time, Pallas kernels for 23%

profile of v6, /device:TPU:0, one launch (start us, length us, event | category | flops | bytes accessed | tf_op | source)
XLA Modules:
  0.0 37.9 jit_solution(14078624626897551027)
XLA Ops:
  0.0 0.5 %collective-permute-start.1 = (f32[20,128,128]{2,1,0:T(8,128)}, f32[20,128,128]{2,1,0:T(8,128)S(1)}, u32[]{:S(2)}, u32[]{:S(2)}) collective-permute-start(f32[20,128,128]{2,1,0:T(8,128)} %bitcast.4), channel_id=1, source_target_pairs={{0,1},{1,0},{2,3},{3,2},{4,5},{5,4},{6,7},{7,6},{8,9},{9,8},{10,11... | collective-permute-start | bytes 3932168 | tf_op jit(solution)/shard_map/ppermute | solution.py:495
  0.5 1.0 %shard_map.65 = (f32[385,1,128]{2,1,0:T(1,128)S(1)}, f32[385,1,128]{2,1,0:T(1,128)S(1)}) custom-call(s32[1,1,2,6]{3,2,1,0:T(2,128)} %bitcast.7, f32[768,128]{1,0:T(8,128)} %bitcast.6), custom_call_target="tpu_custom_call" | custom-call | tf_op jit(solution)/shard_map/pallas_call | solution.py:186
  1.5 2.6 %collective-permute-start.2 = (f32[385,1,128]{2,1,0:T(1,128)S(1)}, f32[385,1,128]{2,1,0:T(1,128)S(1)}, u32[]{:S(2)}, u32[]{:S(2)}) collective-permute-start(f32[385,1,128]{2,1,0:T(1,128)S(1)} %get-tuple-element.26.refs_3_), channel_id=1, source_target_pairs={{0,4},{4,8},{8,12},{12,14},{14,10},{10,6},{6,2},{2,0},{1,5},{5,9},... | collective-permute-start | bytes 591368 | tf_op jit(solution)/shard_map/ppermute | solution.py:502
  4.1 0.0 collective-permute-start.8
  4.1 2.0 %collective-permute-start.9 = (f32[385,1,128]{2,1,0:T(1,128)S(1)}, f32[385,1,128]{2,1,0:T(1,128)S(1)}, u32[]{:S(2)}, u32[]{:S(2)}) collective-permute-start(f32[385,1,128]{2,1,0:T(1,128)S(1)} %get-tuple-element.28.refs_4_), channel_id=1, source_target_pairs={{0,4},{4,8},{8,12},{12,14},{14,10},{10,6},{6,2},{2,0},{1,5},{5,9},... | collective-permute-start | bytes 591368 | tf_op jit(solution)/shard_map/ppermute | solution.py:518
  6.2 0.0 collective-permute-start
  6.2 1.3 %collective-permute-done.refs_2_ = s32[1,2,10]{2,1,0:T(2,128)S(1)} collective-permute-done((s32[1,2,10]{2,1,0:T(2,128)}, s32[1,2,10]{2,1,0:T(2,128)S(1)}, u32[]{:S(2)}, u32[]{:S(2)}) %collective-permute-start) | collective-permute-done | bytes 112 | tf_op jit(solution)/shard_map/ppermute | solution.py:496
  7.5 0.0 copy-start
  7.5 0.0 collective-permute-start.6
  7.5 2.3 %collective-permute-done.2.refs_5_ = f32[385,1,128]{2,1,0:T(1,128)S(1)} collective-permute-done((f32[385,1,128]{2,1,0:T(1,128)S(1)}, f32[385,1,128]{2,1,0:T(1,128)S(1)}, u32[]{:S(2)}, u32[]{:S(2)}) %collective-permute-start.2) | collective-permute-done | bytes 197152 | tf_op jit(solution)/shard_map/ppermute | solution.py:502
  9.8 2.0 %collective-permute-start.3 = (f32[385,1,128]{2,1,0:T(1,128)S(1)}, f32[385,1,128]{2,1,0:T(1,128)S(1)}, u32[]{:S(2)}, u32[]{:S(2)}) collective-permute-start(f32[385,1,128]{2,1,0:T(1,128)S(1)} %collective-permute-done.2.refs_5_), channel_id=1, source_target_pairs={{0,4},{4,8},{8,12},{12,14},{14,10},{10,6},{6,2},{2,0},{1,5},{5,9},... | collective-permute-start | bytes 591368 | tf_op jit(solution)/shard_map/ppermute | solution.py:502
  11.8 0.0 collective-permute-done.8.refs_6_
  11.9 0.0 collective-permute-start.13
  11.9 0.0 collective-permute-done.1.refs_5_
  11.9 0.0 copy-done
  11.9 2.0 %shard_map.64 = (bf16[40,128,256]{2,1,0:T(8,128)(2,1)S(1)}, f32[40,1,128]{2,1,0:T(1,128)S(1)}, f32[8,128]{1,0:T(8,128)S(1)}) custom-call(s32[32]{0:T(128)} %refs_0_.1, s32[1,2,10]{2,1,0:T(2,128)} %refs_1_.1, s32[1,2,10]{2,1,0:T(2,128)} %copy-done, s32[1,1,16]{2,1,0:T(1,128)} %refs_3_.1, f32[20,128,128]{2,1,0:T(8,128)} %bitcast.5, ...), custom_call_target="tpu_custom_call" | custom-call | tf_op jit(solution)/shard_map/pallas_call | solution.py:271
  13.9 0.2 collective-permute-done.9.refs_8_
  14.1 2.0 %collective-permute-start.11 = (f32[385,1,128]{2,1,0:T(1,128)S(1)}, f32[385,1,128]{2,1,0:T(1,128)S(1)}, u32[]{:S(2)}, u32[]{:S(2)}) collective-permute-start(f32[385,1,128]{2,1,0:T(1,128)S(1)} %collective-permute-done.9.refs_8_), channel_id=1, source_target_pairs={{0,4},{4,8},{8,12},{12,14},{14,10},{10,6},{6,2},{2,0},{1,5},{5,9},... | collective-permute-start | bytes 591368 | tf_op jit(solution)/shard_map/ppermute | solution.py:518
  16.1 0.0 collective-permute-done.6.refs_7_
  16.1 0.0 collective-permute-start.7
  16.1 2.2 %collective-permute-done.3.refs_3_ = f32[385,1,128]{2,1,0:T(1,128)S(1)} collective-permute-done((f32[385,1,128]{2,1,0:T(1,128)S(1)}, f32[385,1,128]{2,1,0:T(1,128)S(1)}, u32[]{:S(2)}, u32[]{:S(2)}) %collective-permute-start.3) | collective-permute-done | bytes 197152 | tf_op jit(solution)/shard_map/ppermute | solution.py:502
  18.3 2.0 %collective-permute-start.4 = (f32[385,1,128]{2,1,0:T(1,128)S(1)}, f32[385,1,128]{2,1,0:T(1,128)S(1)}, u32[]{:S(2)}, u32[]{:S(2)}) collective-permute-start(f32[385,1,128]{2,1,0:T(1,128)S(1)} %collective-permute-done.3.refs_3_), channel_id=1, source_target_pairs={{0,4},{4,8},{8,12},{12,14},{14,10},{10,6},{6,2},{2,0},{1,5},{5,9},... | collective-permute-start | bytes 591368 | tf_op jit(solution)/shard_map/ppermute | solution.py:502
  20.3 0.0 collective-permute-done.13.refs_4_
  20.3 0.0 collective-permute-start.14
  20.3 0.9 %shard_map.66.refs_9_ = f32[16,128,128]{2,1,0:T(8,128)S(1)} custom-call(f32[8,128]{1,0:T(8,128)S(1)} %get-tuple-element.23.refs_0_.refs_1_, bf16[40,128,256]{2,1,0:T(8,128)(2,1)S(1)} %get-tuple-element.24.refs_1_.refs_2_, f32[40,1,128]{2,1,0:T(1,128)S(1)} %get-tuple-element.25.refs_2_.refs_3_, f32[385,1,128]{2,1,0:T(1,128)S(1)} %get-tuple-element.26.refs_3_, ...), custom_call_target="tpu_custom_call" | custom-call | tf_op jit(solution)/shard_map/pallas_call | solution.py:457
  21.3 1.2 %collective-permute-done.11.refs_6_ = f32[385,1,128]{2,1,0:T(1,128)S(1)} collective-permute-done((f32[385,1,128]{2,1,0:T(1,128)S(1)}, f32[385,1,128]{2,1,0:T(1,128)S(1)}, u32[]{:S(2)}, u32[]{:S(2)}) %collective-permute-start.11) | collective-permute-done | bytes 197152 | tf_op jit(solution)/shard_map/ppermute | solution.py:518
  22.5 2.0 %collective-permute-done.7.refs_5_ = f32[385,1,128]{2,1,0:T(1,128)S(1)} collective-permute-done((f32[385,1,128]{2,1,0:T(1,128)S(1)}, f32[385,1,128]{2,1,0:T(1,128)S(1)}, u32[]{:S(2)}, u32[]{:S(2)}) %collective-permute-start.7) | collective-permute-done | bytes 197152 | tf_op jit(solution)/shard_map/ppermute | solution.py:517
  24.6 1.6 %collective-permute-start.12 = (f32[385,1,128]{2,1,0:T(1,128)S(1)}, f32[385,1,128]{2,1,0:T(1,128)S(1)}, u32[]{:S(2)}, u32[]{:S(2)}) collective-permute-start(f32[385,1,128]{2,1,0:T(1,128)S(1)} %collective-permute-done.11.refs_6_), channel_id=1, source_target_pairs={{0,4},{4,8},{8,12},{12,14},{14,10},{10,6},{6,2},{2,0},{1,5},{5,9},... | collective-permute-start | bytes 591368 | tf_op jit(solution)/shard_map/ppermute | solution.py:518
  26.1 0.4 %collective-permute-start.10 = (f32[385,1,128]{2,1,0:T(1,128)S(1)}, f32[385,1,128]{2,1,0:T(1,128)S(1)}, u32[]{:S(2)}, u32[]{:S(2)}) collective-permute-start(f32[385,1,128]{2,1,0:T(1,128)S(1)} %collective-permute-done.7.refs_5_), channel_id=1, source_target_pairs={{4,0},{8,4},{12,8},{14,12},{10,14},{6,10},{2,6},{0,2},{5,1},{9,5},... | collective-permute-start | bytes 591368 | tf_op jit(solution)/shard_map/ppermute | solution.py:517
  26.6 0.2 collective-permute-done.4.refs_7_
  26.7 2.0 %collective-permute-start.5 = (f32[385,1,128]{2,1,0:T(1,128)S(1)}, f32[385,1,128]{2,1,0:T(1,128)S(1)}, u32[]{:S(2)}, u32[]{:S(2)}) collective-permute-start(f32[385,1,128]{2,1,0:T(1,128)S(1)} %collective-permute-done.4.refs_7_), channel_id=1, source_target_pairs={{0,4},{4,8},{8,12},{12,14},{14,10},{10,6},{6,2},{2,0},{1,5},{5,9},... | collective-permute-start | bytes 591368 | tf_op jit(solution)/shard_map/ppermute | solution.py:502
  28.7 0.0 collective-permute-done.14.refs_8_
  28.8 0.0 collective-permute-start.15
  28.8 1.9 %shard_map.67 = (f32[16,128,128]{2,1,0:T(8,128)S(1)}, f32[16,128,128]{2,1,0:T(8,128)}) custom-call(f32[8,128]{1,0:T(8,128)S(1)} %get-tuple-element.23.refs_0_.refs_1_, bf16[40,128,256]{2,1,0:T(8,128)(2,1)S(1)} %get-tuple-element.24.refs_1_.refs_2_, f32[40,1,128]{2,1,0:T(1,128)S(1)} %get-tuple-element.25.refs_2_.refs_3_, ...), custom_call_target="tpu_custom_call", output_to_operand_aliasing={{0}: (9, {})} | custom-call | tf_op jit(solution)/shard_map/pallas_call | solution.py:457
  30.7 1.7 %collective-permute-done.12.refs_4_ = f32[385,1,128]{2,1,0:T(1,128)S(1)} collective-permute-done((f32[385,1,128]{2,1,0:T(1,128)S(1)}, f32[385,1,128]{2,1,0:T(1,128)S(1)}, u32[]{:S(2)}, u32[]{:S(2)}) %collective-permute-start.12) | collective-permute-done | bytes 197152 | tf_op jit(solution)/shard_map/ppermute | solution.py:518
  32.4 1.6 %collective-permute-done.10.refs_3_ = f32[385,1,128]{2,1,0:T(1,128)S(1)} collective-permute-done((f32[385,1,128]{2,1,0:T(1,128)S(1)}, f32[385,1,128]{2,1,0:T(1,128)S(1)}, u32[]{:S(2)}, u32[]{:S(2)}) %collective-permute-start.10) | collective-permute-done | bytes 197152 | tf_op jit(solution)/shard_map/ppermute | solution.py:517
  34.0 1.4 %shard_map.68 = (f32[16,128,128]{2,1,0:T(8,128)S(1)}, f32[16,128,128]{2,1,0:T(8,128)}) custom-call(f32[8,128]{1,0:T(8,128)S(1)} %get-tuple-element.23.refs_0_.refs_1_, bf16[40,128,256]{2,1,0:T(8,128)(2,1)S(1)} %get-tuple-element.24.refs_1_.refs_2_, ...), custom_call_target="tpu_custom_call", output_to_operand_aliasing={{0}: (5, {}), {1}: (6, {})} | custom-call | tf_op jit(solution)/shard_map/pallas_call | solution.py:457
  35.4 0.0 collective-permute-done.5.refs_3_
  35.4 1.4 %shard_map.69 = (f32[16,128,128]{2,1,0:T(8,128)S(1)}, f32[16,128,128]{2,1,0:T(8,128)}, s32[24]{0:T(128)S(4)}) custom-call(f32[8,128]{1,0:T(8,128)S(1)} %get-tuple-element.23.refs_0_.refs_1_, bf16[40,128,256]{2,1,0:T(8,128)(2,1)S(1)} %get-tuple-element.24.refs_1_.refs_2_, ...), custom_call_target="tpu_custom_call", output_to_operand_aliasing={{0}: (4, {}), {1}: (5, {})} | custom-call | tf_op jit(solution)/shard_map/pallas_call | solution.py:457
  36.8 0.0 collective-permute-done.15.refs_4_
  36.8 1.1 %shard_map.70 = (f32[16,128,128]{2,1,0:T(8,128)S(1)}, f32[16,128,128]{2,1,0:T(8,128)}) custom-call(s32[24]{0:T(128)S(4)} %get-tuple-element.37.refs_0_, f32[8,128]{1,0:T(8,128)S(1)} %get-tuple-element.23.refs_0_.refs_1_, bf16[40,128,256]{2,1,0:T(8,128)(2,1)S(1)} %get-tuple-element.24.refs_1_.refs_2_, ...), custom_call_target="tpu_custom_call", output_to_operand_aliasing={{0}: (5, {}), {1}: (6, {})} | custom-call | tf_op jit(solution)/shard_map/pallas_call | solution.py:457
Async XLA Ops:
  0.0 11.9 %collective-permute-start.1 = (f32[20,128,128]{2,1,0:T(8,128)}, f32[20,128,128]{2,1,0:T(8,128)S(1)}, u32[]{:S(2)}, u32[]{:S(2)}) collective-permute-start(f32[20,128,128]{2,1,0:T(8,128)} %bitcast.4), channel_id=1, source_target_pairs={{0,1},{1,0},{2,3},{3,2},{4,5},{5,4},{6,7},{7,6},{8,9},{9,8},{10,11... | collective-permute-start | bytes 3932168 | tf_op jit(solution)/shard_map/ppermute | solution.py:495
  1.5 8.3 %collective-permute-start.2 = (f32[385,1,128]{2,1,0:T(1,128)S(1)}, f32[385,1,128]{2,1,0:T(1,128)S(1)}, u32[]{:S(2)}, u32[]{:S(2)}) collective-permute-start(f32[385,1,128]{2,1,0:T(1,128)S(1)} %get-tuple-element.26.refs_3_), channel_id=1, source_target_pairs={{0,4},{4,8},{8,12},{12,14},{14,10},{10,6},{6,2},{2,0},{1,5},{5,9},... | collective-permute-start | bytes 591368 | tf_op jit(solution)/shard_map/ppermute | solution.py:502
  4.1 7.7 %collective-permute-start.8 = (f32[385,1,128]{2,1,0:T(1,128)S(1)}, f32[385,1,128]{2,1,0:T(1,128)S(1)}, u32[]{:S(2)}, u32[]{:S(2)}) collective-permute-start(f32[385,1,128]{2,1,0:T(1,128)S(1)} %get-tuple-element.28.refs_4_), channel_id=1, source_target_pairs={{4,0},{8,4},{12,8},{14,12},{10,14},{6,10},{2,6},{0,2},{5,1},{9,5},... | collective-permute-start | bytes 591368 | tf_op jit(solution)/shard_map/ppermute | solution.py:503
  4.1 9.9 %collective-permute-start.9 = (f32[385,1,128]{2,1,0:T(1,128)S(1)}, f32[385,1,128]{2,1,0:T(1,128)S(1)}, u32[]{:S(2)}, u32[]{:S(2)}) collective-permute-start(f32[385,1,128]{2,1,0:T(1,128)S(1)} %get-tuple-element.28.refs_4_), channel_id=1, source_target_pairs={{0,4},{4,8},{8,12},{12,14},{14,10},{10,6},{6,2},{2,0},{1,5},{5,9},... | collective-permute-start | bytes 591368 | tf_op jit(solution)/shard_map/ppermute | solution.py:518
  6.2 1.4 %collective-permute-start = (s32[1,2,10]{2,1,0:T(2,128)}, s32[1,2,10]{2,1,0:T(2,128)S(1)}, u32[]{:S(2)}, u32[]{:S(2)}) collective-permute-start(s32[1,2,10]{2,1,0:T(2,128)} %refs_1_.1), channel_id=1, source_target_pairs={{0,1},{1,0},{2,3},{3,2},{4,5},{5,4},{6,7},{7,6},{8,9},{9,8},{10,11... | collective-permute-start | bytes 248 | tf_op jit(solution)/shard_map/ppermute | solution.py:496
  7.5 4.4 %copy-start = (s32[1,2,10]{2,1,0:T(2,128)}, s32[1,2,10]{2,1,0:T(2,128)S(1)}, u32[]{:S(2)}) copy-start(s32[1,2,10]{2,1,0:T(2,128)S(1)} %collective-permute-done.refs_2_) | copy-start | bytes 244
  7.5 8.6 %collective-permute-start.6 = (f32[385,1,128]{2,1,0:T(1,128)S(1)}, f32[385,1,128]{2,1,0:T(1,128)S(1)}, u32[]{:S(2)}, u32[]{:S(2)}) collective-permute-start(f32[385,1,128]{2,1,0:T(1,128)S(1)} %get-tuple-element.26.refs_3_), channel_id=1, source_target_pairs={{4,0},{8,4},{12,8},{14,12},{10,14},{6,10},{2,6},{0,2},{5,1},{9,5},... | collective-permute-start | bytes 591368 | tf_op jit(solution)/shard_map/ppermute | solution.py:517
  9.8 8.4 %collective-permute-start.3 = (f32[385,1,128]{2,1,0:T(1,128)S(1)}, f32[385,1,128]{2,1,0:T(1,128)S(1)}, u32[]{:S(2)}, u32[]{:S(2)}) collective-permute-start(f32[385,1,128]{2,1,0:T(1,128)S(1)} %collective-permute-done.2.refs_5_), channel_id=1, source_target_pairs={{0,4},{4,8},{8,12},{12,14},{14,10},{10,6},{6,2},{2,0},{1,5},{5,9},... | collective-permute-start | bytes 591368 | tf_op jit(solution)/shard_map/ppermute | solution.py:502
  11.9 8.4 %collective-permute-start.13 = (f32[385,1,128]{2,1,0:T(1,128)S(1)}, f32[385,1,128]{2,1,0:T(1,128)S(1)}, u32[]{:S(2)}, u32[]{:S(2)}) collective-permute-start(f32[385,1,128]{2,1,0:T(1,128)S(1)} %collective-permute-done.8.refs_6_), channel_id=1, source_target_pairs={{4,0},{8,4},{12,8},{14,12},{10,14},{6,10},{2,6},{0,2},{5,1},{9,5},... | collective-permute-start | bytes 591368 | tf_op jit(solution)/shard_map/ppermute | solution.py:503
  14.1 8.4 %collective-permute-start.11 = (f32[385,1,128]{2,1,0:T(1,128)S(1)}, f32[385,1,128]{2,1,0:T(1,128)S(1)}, u32[]{:S(2)}, u32[]{:S(2)}) collective-permute-start(f32[385,1,128]{2,1,0:T(1,128)S(1)} %collective-permute-done.9.refs_8_), channel_id=1, source_target_pairs={{0,4},{4,8},{8,12},{12,14},{14,10},{10,6},{6,2},{2,0},{1,5},{5,9},... | collective-permute-start | bytes 591368 | tf_op jit(solution)/shard_map/ppermute | solution.py:518
  16.1 8.4 %collective-permute-start.7 = (f32[385,1,128]{2,1,0:T(1,128)S(1)}, f32[385,1,128]{2,1,0:T(1,128)S(1)}, u32[]{:S(2)}, u32[]{:S(2)}) collective-permute-start(f32[385,1,128]{2,1,0:T(1,128)S(1)} %collective-permute-done.6.refs_7_), channel_id=1, source_target_pairs={{4,0},{8,4},{12,8},{14,12},{10,14},{6,10},{2,6},{0,2},{5,1},{9,5},... | collective-permute-start | bytes 591368 | tf_op jit(solution)/shard_map/ppermute | solution.py:517
  18.3 8.4 %collective-permute-start.4 = (f32[385,1,128]{2,1,0:T(1,128)S(1)}, f32[385,1,128]{2,1,0:T(1,128)S(1)}, u32[]{:S(2)}, u32[]{:S(2)}) collective-permute-start(f32[385,1,128]{2,1,0:T(1,128)S(1)} %collective-permute-done.3.refs_3_), channel_id=1, source_target_pairs={{0,4},{4,8},{8,12},{12,14},{14,10},{10,6},{6,2},{2,0},{1,5},{5,9},... | collective-permute-start | bytes 591368 | tf_op jit(solution)/shard_map/ppermute | solution.py:502
  20.3 8.4 %collective-permute-start.14 = (f32[385,1,128]{2,1,0:T(1,128)S(1)}, f32[385,1,128]{2,1,0:T(1,128)S(1)}, u32[]{:S(2)}, u32[]{:S(2)}) collective-permute-start(f32[385,1,128]{2,1,0:T(1,128)S(1)} %collective-permute-done.13.refs_4_), channel_id=1, source_target_pairs={{4,0},{8,4},{12,8},{14,12},{10,14},{6,10},{2,6},{0,2},{5,1},{9,5},... | collective-permute-start | bytes 591368 | tf_op jit(solution)/shard_map/ppermute | solution.py:503
  24.6 7.9 %collective-permute-start.12 = (f32[385,1,128]{2,1,0:T(1,128)S(1)}, f32[385,1,128]{2,1,0:T(1,128)S(1)}, u32[]{:S(2)}, u32[]{:S(2)}) collective-permute-start(f32[385,1,128]{2,1,0:T(1,128)S(1)} %collective-permute-done.11.refs_6_), channel_id=1, source_target_pairs={{0,4},{4,8},{8,12},{12,14},{14,10},{10,6},{6,2},{2,0},{1,5},{5,9},... | collective-permute-start | bytes 591368 | tf_op jit(solution)/shard_map/ppermute | solution.py:518
  26.1 7.9 %collective-permute-start.10 = (f32[385,1,128]{2,1,0:T(1,128)S(1)}, f32[385,1,128]{2,1,0:T(1,128)S(1)}, u32[]{:S(2)}, u32[]{:S(2)}) collective-permute-start(f32[385,1,128]{2,1,0:T(1,128)S(1)} %collective-permute-done.7.refs_5_), channel_id=1, source_target_pairs={{4,0},{8,4},{12,8},{14,12},{10,14},{6,10},{2,6},{0,2},{5,1},{9,5},... | collective-permute-start | bytes 591368 | tf_op jit(solution)/shard_map/ppermute | solution.py:517
  26.7 8.6 %collective-permute-start.5 = (f32[385,1,128]{2,1,0:T(1,128)S(1)}, f32[385,1,128]{2,1,0:T(1,128)S(1)}, u32[]{:S(2)}, u32[]{:S(2)}) collective-permute-start(f32[385,1,128]{2,1,0:T(1,128)S(1)} %collective-permute-done.4.refs_7_), channel_id=1, source_target_pairs={{0,4},{4,8},{8,12},{12,14},{14,10},{10,6},{6,2},{2,0},{1,5},{5,9},... | collective-permute-start | bytes 591368 | tf_op jit(solution)/shard_map/ppermute | solution.py:502
  28.8 8.0 %collective-permute-start.15 = (f32[385,1,128]{2,1,0:T(1,128)S(1)}, f32[385,1,128]{2,1,0:T(1,128)S(1)}, u32[]{:S(2)}, u32[]{:S(2)}) collective-permute-start(f32[385,1,128]{2,1,0:T(1,128)S(1)} %collective-permute-done.14.refs_8_), channel_id=1, source_target_pairs={{4,0},{8,4},{12,8},{14,12},{10,14},{6,10},{2,6},{0,2},{5,1},{9,5},... | collective-permute-start | bytes 591368 | tf_op jit(solution)/shard_map/ppermute | solution.py:503
